TPU v7x, 32 devices: a whole 2x2x4 slice. The times are simulated.
32 devices in a mesh: src: 8 (over y, x, core), tm: 4 (over z).
Axes of the slice: x: 2, y: 2, z: 4, core: 2. Of those that a mesh axis runs over, the one named last changes fastest.
Arguments:
- observed: float32 [4, 8192], P(None, ('src', 'tm')), may hold values from -8 to 8
- weight_obs: float32 [4, 8192], P(None, ('src', 'tm')), may hold values from 0.25 to 4
- present: int32 [4, 8192], P(None, ('src', 'tm')), may hold values 0 or 1
- source_partials: float32 [5, 4, 8192], P(None, None, ('src', 'tm')), may hold values from -6 to 6
- attitude_partials: float32 [4, 4, 8192], P(None, None, ('src', 'tm')), may hold values from -6 to 6
- phase: float32 [4, 8192], P(None, ('src', 'tm')), may hold values from 0 to 1
- knot_base: int32 [4, 8192], P(None, ('src', 'tm')), may hold values from 0 to 28
- source_id: int32 [4, 8192], P(None, ('src', 'tm')), may hold values from 0 to 127, as said below
- cal_id: int32 [4, 8192], P(None, ('src', 'tm')), may hold values from 0 to 32767
- attitude: float32 [512], P('tm'), may hold values from -4 to 4
- calibration: float32 [32768], replicated, may hold values from -4 to 4
Outputs:
- source_params: float32 [5, 4096], P(None, ('src', 'tm'))
- attitude_out: float32 [512], P('tm')
- calibration_out: float32 [32768], replicated
- residual: float32 [4, 8192], P(None, ('src', 'tm'))
Inputs may be any that keep to these rules, and one draw needn't show every extreme that they name: `source_id`: within each device's block of 256 columns the ids name that device's 128 sources, each of them at least once.
All inputs are finite; a program needn't handle non-finite values. No bound on the sum of `present` on one device may be relied on, other than what follows from the above.
Results may differ from a plain program's by a relative error of at most 0.0003.
Values sent between devices are 32-bit elements; how exact they have to be, the bound alone decides.
No kernel may reach another device: no remote copies, remote signals or barrier semaphores. Data moves between devices by JAX's collectives and lax.ppermute only.
A program may use at most 64 MiB of HBM per device.

v0:
```python
import jax
import jax.numpy as jnp
from jax import lax
from jax.sharding import PartitionSpec as P

KNOTS_DEV = 32
SRC_DEV = 128
CAL = 32768
ITERS = 2


PAIRS = [(row_id, col_id) for row_id in range(5) for col_id in range(row_id + 1)]


def spline_terms(phase, attitude_partials):
    other = 1.0 - phase
    square = phase * phase
    cube = square * phase
    basis = [
        other * other * other / 6.0,
        (3.0 * cube - 6.0 * square + 4.0) / 6.0,
        (-3.0 * cube + 3.0 * square + 3.0 * phase + 1.0) / 6.0,
        cube / 6.0,
    ]
    return jnp.stack(
        [
            basis[knot_step] * attitude_partials[channel]
            for knot_step in range(4)
            for channel in range(4)
        ]
    )


def attitude_model(local, terms, knot_base):
    coefficients = lax.all_gather(local, "tm", axis=0, tiled=True)
    blocks, slots = knot_base.shape
    table = coefficients.reshape(blocks, -1, 4)
    knots_count = table.shape[1]
    grid = lax.broadcasted_iota(jnp.int32, (1, knots_count, 1), 1)
    running = jnp.zeros(knot_base.shape, jnp.float32)
    for knot_step in range(4):
        hit = (grid == (knot_base + knot_step)[:, None, :]).astype(jnp.float32)
        picked = jnp.einsum(
            "bkc,bks->bcs",
            table,
            hit,
            precision=lax.Precision.HIGHEST,
            preferred_element_type=jnp.float32,
        )
        for channel in range(4):
            running = running + terms[4 * knot_step + channel] * picked[:, channel, :]
    return running


def small_solve(matrix, right_side):
    extent = len(right_side)
    factor = {}
    for member in range(extent):
        for column in range(member + 1):
            running = matrix[member][column]
            for offset in range(column):
                running = running - factor[member, offset] * factor[column, offset]
            if member == column:
                factor[member, member] = jnp.sqrt(running)
            else:
                factor[member, column] = running / factor[column, column]
    forward = []
    for member in range(extent):
        running = right_side[member]
        for offset in range(member):
            running = running - factor[member, offset] * forward[offset]
        forward.append(running / factor[member, member])
    result = [None] * extent
    for member in reversed(range(extent)):
        running = forward[member]
        for offset in range(member + 1, extent):
            running = running - factor[offset, member] * result[offset]
        result[member] = running / factor[member, member]
    return jnp.stack(result)


def source_solve(ids, count, weighted, source_partials, target):
    products = [
        weighted * source_partials[row_id] * source_partials[col_id] for row_id, col_id in PAIRS
    ]
    products = products + [weighted * source_partials[row_id] * target for row_id in range(5)]
    stacked = jnp.moveaxis(jnp.stack(products), 1, 0)
    owners = lax.broadcasted_iota(jnp.int32, (count, 1), 0)

    def accumulate(total, item):
        values, block_ids = item
        hit = (block_ids[None, :] == owners).astype(jnp.float32)
        added = lax.dot_general(
            values,
            hit,
            (((1,), (1,)), ((), ())),
            precision=lax.Precision.HIGHEST,
            preferred_element_type=jnp.float32,
        )
        return (total + added, None)

    sums, unused = lax.scan(
        accumulate, jnp.zeros((len(products), count), jnp.float32), (stacked, ids)
    )
    entries = {}
    for position, pair in enumerate(PAIRS):
        entry_value = sums[position] + (1.0 if pair[0] == pair[1] else 0.0)
        entries[pair[0], pair[1]] = entry_value
        entries[pair[1], pair[0]] = entry_value
    matrix = [[entries[row_id, col_id] for col_id in range(5)] for row_id in range(5)]
    return small_solve(matrix, [sums[15 + row_id] for row_id in range(5)])


def pick_params(params, ids):
    count = params.shape[1]
    owners = lax.broadcasted_iota(jnp.int32, (count, 1), 0)

    def pick_single(carry, block_ids):
        hit = (block_ids[None, :] == owners).astype(jnp.float32)
        return (
            carry,
            jnp.dot(
                params, hit, precision=lax.Precision.HIGHEST, preferred_element_type=jnp.float32
            ),
        )

    unused, picked = lax.scan(pick_single, 0, ids)
    return jnp.moveaxis(picked, 1, 0)


def spd_solve(matrix, right_side):
    eye = jnp.eye(matrix.shape[-1], dtype=jnp.float32)
    lower = jnp.linalg.cholesky(matrix + eye)
    middle = lax.linalg.triangular_solve(lower, right_side[..., None], left_side=True, lower=True)
    result = lax.linalg.triangular_solve(
        lower, middle, left_side=True, lower=True, transpose_a=True
    )
    return result[..., 0]


def block_normals(terms, knot_base, weighted, resid):
    blocks, slots = knot_base.shape
    spread = jnp.moveaxis(terms.reshape(4, 4, blocks, slots), 2, 0)

    def block_single(item):
        part, base, weights, values = item
        grid = lax.broadcasted_iota(jnp.int32, (KNOTS_DEV, slots), 0)
        design = jnp.zeros((KNOTS_DEV, 4, slots), jnp.float32)
        for knot_step in range(4):
            hit = (grid == base[None, :] + knot_step).astype(jnp.float32)
            design = design + hit[:, None, :] * part[knot_step][None, :, :]
        design = design.reshape(KNOTS_DEV * 4, slots)
        normal = lax.dot_general(
            design * weights[None, :],
            design,
            (((1,), (1,)), ((), ())),
            precision=lax.Precision.HIGHEST,
            preferred_element_type=jnp.float32,
        )
        right = jnp.dot(
            design,
            weights * values,
            precision=lax.Precision.HIGHEST,
            preferred_element_type=jnp.float32,
        )
        return (normal, right)

    return lax.map(block_single, (spread, knot_base, weighted, resid))


def body(
    observed,
    weight_obs,
    present,
    source_partials,
    attitude_partials,
    phase,
    knot_base,
    source_id,
    cal_id,
    attitude,
    calibration,
):
    weighted = present.astype(jnp.float32) * weight_obs
    terms = spline_terms(phase, attitude_partials)
    flat_cal = cal_id.reshape(-1)
    local = attitude
    cal_now = calibration
    params = jnp.zeros((5, SRC_DEV), jnp.float32)
    for sweep in range(ITERS):
        target = observed - attitude_model(local, terms, knot_base) - cal_now[cal_id]
        params = source_solve(source_id, SRC_DEV, weighted, source_partials, target)
        resid = target - jnp.sum(source_partials * pick_params(params, source_id), axis=0)
        normals, rights = block_normals(terms, knot_base, weighted, resid)
        normal, right = (
            lax.psum_scatter(normals, "tm", scatter_dimension=0, tiled=True),
            lax.psum_scatter(rights, "tm", scatter_dimension=0, tiled=True),
        )
        normal, right = lax.psum((normal[0], right[0]), "src")
        local = local + spd_solve(normal, right)
        numer = jax.ops.segment_sum((weighted * resid).reshape(-1), flat_cal, num_segments=CAL)
        denom = jax.ops.segment_sum(weighted.reshape(-1), flat_cal, num_segments=CAL)
        numer, denom = lax.psum((numer, denom), ("src", "tm"))
        cal_now = cal_now + numer / (denom + 1.0)
    final = observed - attitude_model(local, terms, knot_base) - cal_now[cal_id]
    final = final - jnp.sum(source_partials * pick_params(params, source_id), axis=0)
    return (params, local, cal_now, final)


def solution(mesh):
    return jax.shard_map(
        body,
        mesh=mesh,
        in_specs=(
            P(None, ("src", "tm")),
            P(None, ("src", "tm")),
            P(None, ("src", "tm")),
            P(None, None, ("src", "tm")),
            P(None, None, ("src", "tm")),
            P(None, ("src", "tm")),
            P(None, ("src", "tm")),
            P(None, ("src", "tm")),
            P(None, ("src", "tm")),
            P("tm"),
            P(),
        ),
        out_specs=(P(None, ("src", "tm")), P("tm"), P(), P(None, ("src", "tm"))),
        check_vma=False,
    )
```

profile of v0, /device:TPU:0, one launch (start us, length us, event | category | flops | bytes accessed | tf_op | source)
XLA Modules:
  0.0 512.3 jit_solution(8980157615680027577)
XLA Ops:
  8.7 0.7 constant_dynamic-update-slice_fusion.55
  9.6 0.7 copy-done.9
  10.5 0.6 copy-done.16
  11.2 12.5 %all-gather = f32[4,1,128]{2,1,0:T(1,128)S(1)} all-gather(f32[1,1,128]{2,1,0:T(1,128)S(1)} %bitcast.918), channel_id=1, replica_groups=mesh['src'=8,'tm'=4] {'tm'}, dimensions={0}, use_global_device_ids=true | all-gather | bytes 2560 | tf_op jit(solution)/shard_map/all_gather | solution.py:35
  26.5 0.7 copy-done.13
  27.1 6.2 %gather_fusion = f32[1024]{0:T(1024)S(1)} fusion(f32[32768]{0:T(1024)S(1)} %copy-done, s32[1024]{0:T(1024)S(1)} %broadcast_clamp_fusion), kind=kCustom, calls=%fused_computation | custom fusion | bytes 12288 | tf_op jit(solution)/shard_map/gather | solution.py:191
  33.3 0.7 copy-done.12
  34.1 0.7 copy-done.11
  34.8 0.9 while.76
  35.9 0.7 while.74
  36.7 3.4 while.72
  40.2 0.7 copy-done.2
  41.0 6.5 %scatter_custom_fusion = f32[32768]{0:T(1024)} fusion(s32[1024]{0:T(1024)S(1)} %bitcast.912, f32[1024]{0:T(1024)S(1)} %bitcast.915, f32[]{:T(128)} %constant.127.clone.1), kind=kCustom, calls=%fused_computation.185 | custom fusion | flops 1024 | bytes 131076 | tf_op jit(solution)/shard_map/scatter-add | solution.py:201
  47.5 6.5 %scatter_custom_fusion.1 = f32[32768]{0:T(1024)} fusion(s32[1024]{0:T(1024)S(1)} %bitcast.913, f32[1024]{0:T(1024)S(1)} %bitcast.917, f32[]{:T(128)} %constant.127.clone.1), kind=kCustom, calls=%fused_computation.183 | custom fusion | flops 1024 | bytes 131076 | tf_op jit(solution)/shard_map/scatter-add | solution.py:202
  54.2 0.6 copy-done.18
  54.8 0.7 dynamic-slice
  55.5 8.3 %all-reduce = f32[4,128]{1,0:T(4,128)S(1)} all-reduce(f32[4,128]{1,0:T(4,128)S(1)} %get-tuple-element.204), channel_id=3, replica_groups=mesh['src'=8,'tm'=4] {'tm'}, use_global_device_ids=true, to_apply=%region_11.13.clone | all-reduce | flops 512 | bytes 4096
  63.8 0.7 fusion.181
  64.5 11.8 %psum.53 = f32[128,1]{0,1:T(1,128)S(1)} all-reduce(f32[128,1]{0,1:T(1,128)S(1)} %fusion.181), channel_id=1, replica_groups=mesh['src'=8,'tm'=4] {'src'}, use_global_device_ids=true, to_apply=%region_12.14 | all-reduce | flops 128 | bytes 1024 | tf_op jit(solution)/shard_map/psum | solution.py:199
  76.6 100.8 %all-reduce.14.cloned.1.call-done = (f32[32768]{0:T(1024)}, f32[32768]{0:T(1024)}) async-done(((f32[32768]{0:T(1024)}, f32[32768]{0:T(1024)}), (f32[32768]{0:T(1024)}, f32[32768]{0:T(1024)})) %all-reduce.14.cloned.1.call-update) | async-done | bytes 262160 | tf_op jit(solution)/shard_map/psum | solution.py:203
  177.3 1.0 divide_add_fusion.1
  178.3 6.2 %gather_fusion.1 = f32[1024]{0:T(1024)S(1)} fusion(f32[32768]{0:T(1024)S(1)} %divide_add_fusion.1, s32[1024]{0:T(1024)S(1)} %broadcast_clamp_fusion), kind=kCustom, calls=%fused_computation.1 | custom fusion | bytes 12288 | tf_op jit(solution)/shard_map/gather | solution.py:191
  184.5 47.1 %all-reduce.8.cloned.1.call-done = f32[128,128]{0,1:T(8,128)} async-done(((f32[128,128]{0,1:T(8,128)}), f32[128,128]{0,1:T(8,128)}) %all-reduce.8.cloned.1.call-update) | async-done | bytes 65552 | tf_op jit(solution)/shard_map/psum | solution.py:199
  231.7 0.9 convert_add_fusion.1
  232.6 0.7 copy-done.7
  233.4 11.7 %cholesky.44 = f32[128,128]{1,0:T(8,128)S(1)} custom-call(f32[128,128]{1,0:T(8,128)S(1)} %fusion.52), custom_call_target="Cholesky" | custom-call | tf_op jit(solution)/shard_map/jit(cholesky)/cholesky | solution.py:133
  245.8 0.7 fusion.45
  246.4 9.8 %custom-call.13 = f32[1,128,128]{1,2,0:T(8,128)S(1)} custom-call(f32[1,128,128]{2,1,0:T(8,128)S(1)} %fusion.45), custom_call_target="InvertDiagBlocksLowerTriangular" | custom-call | tf_op jit(solution)/shard_map/triangular_solve/custom-call.2 | solution.py:135
  256.6 10.9 %all-gather.1 = f32[4,1,128]{2,1,0:T(1,128)S(1)} all-gather(f32[1,1,128]{2,1,0:T(1,128)S(1)} %bitcast.911), channel_id=1, replica_groups=mesh['src'=8,'tm'=4] {'tm'}, dimensions={0}, use_global_device_ids=true | all-gather | bytes 2560 | tf_op jit(solution)/shard_map/all_gather | solution.py:35
  269.3 1.0 while.77
  270.5 0.7 while.75
  271.8 3.4 while.73
  275.2 0.7 copy-done.3
  276.0 6.5 %scatter_custom_fusion.2 = f32[32768]{0:T(1024)} fusion(s32[1024]{0:T(1024)S(1)} %bitcast.914, f32[1024]{0:T(1024)S(1)} %bitcast.916, f32[]{:T(128)} %constant.127.clone.1), kind=kCustom, calls=%fused_computation.181 | custom fusion | flops 1024 | bytes 131076 | tf_op jit(solution)/shard_map/scatter-add | solution.py:201
  282.5 8.5 %all-reduce.1 = f32[4,128]{1,0:T(4,128)S(1)} all-reduce(f32[4,128]{1,0:T(4,128)S(1)} %get-tuple-element.208), channel_id=5, replica_groups=mesh['src'=8,'tm'=4] {'tm'}, use_global_device_ids=true, to_apply=%region_26.30.clone | all-reduce | flops 512 | bytes 4096
  291.1 0.7 fusion.182
  291.8 12.0 %psum.57 = f32[128,1]{0,1:T(1,128)S(1)} all-reduce(f32[128,1]{0,1:T(1,128)S(1)} %fusion.182), channel_id=1, replica_groups=mesh['src'=8,'tm'=4] {'src'}, use_global_device_ids=true, to_apply=%region_27.31 | all-reduce | flops 128 | bytes 1024 | tf_op jit(solution)/shard_map/psum | solution.py:199
  303.8 107.7 %all-reduce.12.cloned.1.call-done = f32[32768]{0:T(1024)} async-done(((f32[32768]{0:T(1024)}), f32[32768]{0:T(1024)}) %all-reduce.12.cloned.1.call-update) | async-done | bytes 131088 | tf_op jit(solution)/shard_map/psum | solution.py:203
  411.6 0.9 divide_add_fusion
  412.5 6.2 %gather_fusion.2 = f32[1024]{0:T(1024)S(1)} fusion(f32[32768]{0:T(1024)S(1)} %divide_add_fusion, s32[1024]{0:T(1024)S(1)} %broadcast_clamp_fusion), kind=kCustom, calls=%fused_computation.2 | custom fusion | bytes 12288 | tf_op jit(solution)/shard_map/gather | solution.py:205
  418.7 47.4 %all-reduce.10.cloned.1.call-done = f32[128,128]{0,1:T(8,128)} async-done(((f32[128,128]{0,1:T(8,128)}), f32[128,128]{0,1:T(8,128)}) %all-reduce.10.cloned.1.call-update) | async-done | bytes 65552 | tf_op jit(solution)/shard_map/psum | solution.py:199
  466.1 0.9 convert_add_fusion
  467.0 0.7 copy-done.8
  467.8 11.7 %cholesky.55 = f32[128,128]{1,0:T(8,128)S(1)} custom-call(f32[128,128]{1,0:T(8,128)S(1)} %fusion.49), custom_call_target="Cholesky" | custom-call | tf_op jit(solution)/shard_map/jit(cholesky)/cholesky | solution.py:133
  480.2 0.7 fusion.46
  480.8 9.8 %custom-call.15 = f32[1,128,128]{1,2,0:T(8,128)S(1)} custom-call(f32[1,128,128]{2,1,0:T(8,128)S(1)} %fusion.46), custom_call_target="InvertDiagBlocksLowerTriangular" | custom-call | tf_op jit(solution)/shard_map/triangular_solve/custom-call.2 | solution.py:135
  491.6 10.8 %all-gather.2 = f32[4,1,128]{2,1,0:T(1,128)S(1)} all-gather(f32[1,1,128]{2,1,0:T(1,128)S(1)} %bitcast.919), channel_id=1, replica_groups=mesh['src'=8,'tm'=4] {'tm'}, dimensions={0}, use_global_device_ids=true | all-gather | bytes 2560 | tf_op jit(solution)/shard_map/all_gather | solution.py:35
  504.1 0.7 fusion.112
  (292 shorter events, 20.8 us)
Async XLA Ops:
  8.0 0.7 copy-start.15
  8.0 1.4 copy-start.5
  8.0 68.3 %reduce-scatter.3.cloned.1.call-start = ((), (), s32[]{:S(2)}) async-start(), calls=%async_computation.2 | async-start | bytes 327680 | tf_op jit(solution)/shard_map/reduce_scatter | solution.py:196
  9.5 0.7 copy-start.9
  9.6 0.7 copy-start.4
  10.5 0.7 copy-start.16
  24.8 0.7 copy-start.10
  26.0 1.2 copy-start
  26.4 0.7 copy-start.13
  33.3 0.7 copy-start.12
  34.1 0.7 copy-start.11
  40.2 0.7 copy-start.2
  40.9 136.5 %all-reduce.14.cloned.1.call-start = ((), (), s32[]{:S(2)}) async-start(), calls=%async_computation.7 | async-start | bytes 524288 | tf_op jit(solution)/shard_map/psum | solution.py:203
  54.1 177.6 %all-reduce.8.cloned.1.call-start = ((), (), s32[]{:S(2)}) async-start(), calls=%async_computation.3 | async-start | bytes 131072 | tf_op jit(solution)/shard_map/psum | solution.py:199
  54.1 0.7 copy-start.18
  76.3 227.5 %reduce-scatter.5.cloned.1.call-start = ((), (), s32[]{:S(2)}) async-start(), calls=%async_computation.4 | async-start | bytes 327680 | tf_op jit(solution)/shard_map/reduce_scatter | solution.py:196
  232.5 0.8 copy-start.7
  271.1 0.6 copy-start.14
  275.2 0.7 copy-start.3
  275.9 135.6 %all-reduce.12.cloned.1.call-start = ((), (), s32[]{:S(2)}) async-start(), calls=%async_computation.6 | async-start | bytes 262144 | tf_op jit(solution)/shard_map/psum | solution.py:203
  282.5 129.0 %copy-start.6 = (f32[32768]{0:T(1024)S(1)}, f32[32768]{0:T(1024)}, u32[]{:S(2)}) copy-start(f32[32768]{0:T(1024)} %get-tuple-element.348) | copy-start | bytes 393220
  291.0 175.0 %all-reduce.10.cloned.1.call-start = ((), (), s32[]{:S(2)}) async-start(), calls=%async_computation.5 | async-start | bytes 131072 | tf_op jit(solution)/shard_map/psum | solution.py:199
  412.5 6.2 %copy-start.1 = (f32[32768]{0:T(1024)}, f32[32768]{0:T(1024)S(1)}, u32[]{:S(2)}) copy-start(f32[32768]{0:T(1024)S(1)} %divide_add_fusion) | copy-start | bytes 393220
  466.9 0.8 copy-start.8
  491.0 0.6 copy-start.17
Sparse Core Ops, SparseCore 0:
  41.0 17.8 reduce-scatter.2
  276.0 16.4 reduce-scatter.4
Sparse Core Ops, SparseCore 1:
  54.1 123.1 all-reduce.13
  180.5 51.1 all-reduce.7
  291.1 120.4 all-reduce.11
  414.9 51.1 all-reduce.9
where the time goes:
time: 513 us; the launch traced here: 512 us
  waiting for transfers between devices  303 us (59%)
  blocking collectives  74.9 us (15%)
  other arithmetic  74.1 us (14%)
  local copies, waits for them, and re-layouts  32.8 us (6%)
  between operations  16.3 us (3%)
  matrix products  9.64 us (2%)
    psum x2, waiting for transfers between devices, body(): numer, denom = lax.psum((numer, denom), ('src', 'tm'))  208 us
    psum x2, waiting for transfers between devices, body(): normal, right = lax.psum((normal[0], right[0]), 'src')  94.5 us
    all_gather x3, blocking collectives, attitude_model(): coefficients = lax.all_gather(local, 'tm', axis=0, tiled=True)  34.2 us
    another operation x6, other arithmetic, spd_solve(): lower = jnp.linalg.cholesky(matrix + eye)  24.8 us
    psum x2, blocking collectives, body(): normal, right = lax.psum((normal[0], right[0]), 'src')  23.8 us
    another operation x4, other arithmetic, spd_solve(): lax.linalg.triangular_solve(lower, middle, left_side=True, lower=True, tr...  20.9 us
    unnamed x2, blocking collectives  16.8 us
    scatter-add x2, other arithmetic, body(): jax.ops.segment_sum((weighted * resid).reshape(-1), flat_cal, num_segment...  13.1 us
  transfers between devices with their start and end apart: 6, of which 4 were waited for; matrix products, arithmetic and copies ran while one was open for 7% of the time, Pallas kernels for 0%

commit v1 on v0

--- a/solution.py
+++ b/solution.py
@@ -1,12 +1,219 @@
+import functools
+
 import jax
 import jax.numpy as jnp
 from jax import lax
+from jax.experimental import pallas as pl
+from jax.experimental.pallas import tpu as pltpu
 from jax.sharding import PartitionSpec as P
 
 KNOTS_DEV = 32
+WIDTH = 4 * KNOTS_DEV
 SRC_DEV = 128
 CAL = 32768
-ITERS = 2
+LANES = 128
+HIGH = CAL // LANES
+SUB = 8
+VMEM_BYTES = 48 * 1024 * 1024
+
+F32 = jnp.float32
+BF16 = jnp.bfloat16
+EXACT = lax.Precision.HIGHEST
+
+
+def iota(shape, dim):
+    return lax.broadcasted_iota(jnp.int32, shape, dim)
+
+
+def split3(value):
+    first = value.astype(BF16)
+    rest = value - first.astype(F32)
+    second = rest.astype(BF16)
+    third = (rest - second.astype(F32)).astype(BF16)
+    return first, second, third
+
+
+def dot(left, right):
+    return lax.dot_general(left, right, (((1,), (0,)), ((), ())), preferred_element_type=F32)
+
+
+def dot_t(left, right):
+    return lax.dot_general(left, right, (((1,), (1,)), ((), ())), preferred_element_type=F32)
+
+
+def exact_dot(left, right):
+    return lax.dot_general(
+        left, right, (((1,), (0,)), ((), ())), precision=EXACT, preferred_element_type=F32
+    )
+
+
+def exact_dot_t(left, right):
+    return lax.dot_general(
+        left, right, (((1,), (1,)), ((), ())), precision=EXACT, preferred_element_type=F32
+    )
+
+
+def one_hot(ids, count):
+    return jnp.where(iota((count, ids.shape[1]), 0) == ids, 1.0, 0.0).astype(BF16)
+
+
+def flat(value):
+    return jnp.concatenate([value[row : row + 1] for row in range(value.shape[0])], axis=1)
+
+
+def unflat(value, rows):
+    slots = value.shape[1] // rows
+    return [value[:, row * slots : (row + 1) * slots] for row in range(rows)]
+
+
+def cal_pick(table, ids):
+    parts = jnp.concatenate(split3(table.T), axis=0)
+    high = ids // LANES
+    low = ids % LANES
+    found = dot(parts, one_hot(high, HIGH))
+    found = found[:LANES] + found[LANES : 2 * LANES] + found[2 * LANES :]
+    return jnp.sum(jnp.where(iota(found.shape, 0) == low, found, 0.0), axis=0, keepdims=True)
+
+
+def cal_sums(values, ids):
+    high = one_hot(ids // LANES, HIGH)
+    low = iota((LANES, ids.shape[1]), 0) == ids % LANES
+    total = None
+    for part in split3(values):
+        spread = jnp.where(low, part.astype(F32), 0.0).astype(BF16)
+        added = dot_t(high, spread)
+        total = added if total is None else total + added
+    return total
+
+
+def design_of(base, basis, partials):
+    slots = base.shape[1]
+    knot = iota((WIDTH, slots), 0) // 4
+    step = knot - base
+    spread = jnp.zeros((WIDTH, slots), F32)
+    for index in range(4):
+        spread = jnp.where(step == index, basis[index], spread)
+    return spread * jnp.concatenate([partials] * (WIDTH // 8), axis=0)
+
+
+def band_shift(tile, knot):
+    return ((tile % 8) * 16 - (8 * tile + 4 * knot - 12)) % WIDTH
+
+
+def pack_band(normal):
+    place = iota((8, WIDTH), 1) // 16
+    upper = iota((8, WIDTH), 0) < 4
+    groups = []
+    for group in range(2):
+        packed = jnp.zeros((8, WIDTH), F32)
+        for tile in range(8 * group, 8 * group + 8):
+            rows = normal[8 * tile : 8 * tile + 8]
+            rolled = jnp.where(
+                upper,
+                pltpu.roll(rows, band_shift(tile, 0), 1),
+                pltpu.roll(rows, band_shift(tile, 1), 1),
+            )
+            packed = jnp.where(place == tile % 8, rolled, packed)
+        groups.append(packed)
+    return jnp.concatenate(groups, axis=0)
+
+
+def unpack_band(packed):
+    place = iota((8, WIDTH), 1) // 16
+    upper = iota((8, WIDTH), 0) < 4
+    tiles = []
+    for tile in range(16):
+        group = tile // 8
+        rows = jnp.where(place == tile % 8, packed[8 * group : 8 * group + 8], 0.0)
+        tiles.append(
+            jnp.where(
+                upper,
+                pltpu.roll(rows, (-band_shift(tile, 0)) % WIDTH, 1),
+                pltpu.roll(rows, (-band_shift(tile, 1)) % WIDTH, 1),
+            )
+        )
+    full = jnp.concatenate(tiles, axis=0)
+    return jnp.where(iota(full.shape, 0) >= iota(full.shape, 1), full, 0.0)
+
+
+def coefs(first, last):
+    return list(range(4 * first, 4 * last + 4))
+
+
+STAGES = (
+    ((coefs(0, 4), (0, 3)), (coefs(8, 13), (2, 8)), (coefs(17, 22), (7, 12)), (coefs(26, 31), (11, 15))),
+    ((coefs(5, 7), (0, 8)), (coefs(23, 25), (7, 15))),
+    ((coefs(14, 16), (0, 15)),),
+)
+
+
+def spd_inverse(matrix):
+    tiles = [matrix[8 * tile : 8 * tile + 8] for tile in range(WIDTH // 8)]
+    lane = iota((8, WIDTH), 1)
+    lane_row = iota((1, WIDTH), 1)
+    row = iota((8, 1), 0)
+    for stage in STAGES:
+        for step in range(max(len(chain) for chain, reach in stage)):
+            pivots = [(chain[step], reach) for chain, reach in stage if step < len(chain)]
+            held = list(tiles)
+            for pivot, (low, high) in pivots:
+                at, sub = pivot // 8, pivot % 8
+                line = held[at][sub : sub + 1]
+                scale = 1.0 / line[:, pivot : pivot + 1]
+                line = jnp.where(lane_row == pivot, -1.0, line) * scale
+                for tile in range(low, high + 1):
+                    column = held[tile][:, pivot : pivot + 1]
+                    drop = lane == pivot
+                    if tile == at:
+                        column = jnp.where(row == sub, -1.0, column)
+                        drop = drop | (iota((8, WIDTH), 0) == sub)
+                    tiles[tile] = jnp.where(drop, 0.0, tiles[tile]) - column * line
+    return -jnp.concatenate(tiles, axis=0)
+
+
+def small_factor(sums):
+    factor = {}
+    for member in range(5):
+        for column in range(member + 1):
+            running = sums[8 * member + column : 8 * member + column + 1]
+            if member == column:
+                running = running + 1.0
+            for offset in range(column):
+                running = running - factor[member, offset] * factor[column, offset]
+            if member == column:
+                factor[member, member] = jnp.sqrt(running)
+            else:
+                factor[member, column] = running * inverse_of[column]
+        inverse_of = {} if member == 0 else inverse_of
+        inverse_of[member] = 1.0 / factor[member, member]
+    inverse = {}
+    for column in range(5):
+        inverse[column, column] = inverse_of[column]
+        for member in range(column + 1, 5):
+            running = factor[member, column] * inverse[column, column]
+            for offset in range(column + 1, member):
+                running = running + factor[member, offset] * inverse[offset, column]
+            inverse[member, column] = -running * inverse_of[member]
+    return inverse
+
+
+PLACES = [(row_id, col_id) for row_id in range(5) for col_id in range(row_id + 1)]
+
+
+def small_apply(inverse, sides):
+    forward = []
+    for member in range(5):
+        running = inverse[member, 0] * sides[0]
+        for column in range(1, member + 1):
+            running = running + inverse[member, column] * sides[column]
+        forward.append(running)
+    result = []
+    for column in range(5):
+        running = inverse[column, column] * forward[column]
+        for member in range(column + 1, 5):
+            running = running + inverse[member, column] * forward[member]
+        result.append(running)
+    return result
 
 
 PAIRS = [(row_id, col_id) for row_id in range(5) for col_id in range(row_id + 1)]
@@ -168,7 +375,7 @@
     return lax.map(block_single, (spread, knot_base, weighted, resid))
 
 
-def body(
+def plain_body(
     observed,
     weight_obs,
     present,
@@ -187,7 +394,7 @@
     local = attitude
     cal_now = calibration
     params = jnp.zeros((5, SRC_DEV), jnp.float32)
-    for sweep in range(ITERS):
+    for sweep in range(2):
         target = observed - attitude_model(local, terms, knot_base) - cal_now[cal_id]
         params = source_solve(source_id, SRC_DEV, weighted, source_partials, target)
         resid = target - jnp.sum(source_partials * pick_params(params, source_id), axis=0)
@@ -207,9 +414,380 @@
     return (params, local, cal_now, final)
 
 
+BAND = 16
+
+
+def fetch(pairs, sems):
+    copies = [
+        pltpu.make_async_copy(origin, held, sems.at[place])
+        for place, (origin, held) in enumerate(pairs)
+    ]
+    for copy in copies:
+        copy.start()
+    for copy in copies:
+        copy.wait()
+
+
+def lines_of(value):
+    rows, slots = value.shape
+    return [
+        value[row : row + 1, at : at + LANES] for row in range(rows) for at in range(0, slots, LANES)
+    ]
+
+
+def pick_from(table_t, ids):
+    rows = ids.shape[0]
+    ids = flat(ids)
+    found = dot(jnp.concatenate(split3(table_t), axis=0), one_hot(ids // LANES, HIGH))
+    found = found[:LANES] + found[LANES : 2 * LANES] + found[2 * LANES :]
+    hit = iota(found.shape, 0) == ids % LANES
+    return unflat(jnp.sum(jnp.where(hit, found, 0.0), axis=0, keepdims=True), rows)
+
+
+def normals_kernel(
+    observed_in, weight_in, present_in, source_in, attitude_in, phase_in, knot_in, id_in, cal_in,
+    start_in,
+    send_out, design_out, weighted_out, observed, source_id, cal_id, source_partials, start,
+    weight_obs, present, attitude_partials, phase, knot_base, stacked, sems,
+):
+    fetch(
+        [
+            (observed_in, observed), (weight_in, weight_obs), (present_in, present),
+            (source_in, source_partials), (attitude_in, attitude_partials), (phase_in, phase),
+            (knot_in, knot_base), (id_in, source_id), (cal_in, cal_id), (start_in, start),
+        ],
+        sems,
+    )
+    rows, slots = observed.shape
+    weighted = present[...].astype(F32) * weight_obs[...]
+    weighted_out[...] = weighted
+    u = phase[...]
+    other = 1.0 - u
+    square = u * u
+    cube = square * u
+    basis = [
+        other * other * other / 6.0,
+        (3.0 * cube - 6.0 * square + 4.0) / 6.0,
+        (-3.0 * cube + 3.0 * square + 3.0 * u + 1.0) / 6.0,
+        cube / 6.0,
+    ]
+    common = lines_of(cal_id[...].astype(F32)) + lines_of(weighted) + [start[...]]
+    for row in range(rows):
+        at = slice(row, row + 1)
+        for channel in range(4):
+            lines = attitude_partials[channel, at]
+            stacked[row, channel : channel + 1] = lines
+            stacked[row, channel + 4 : channel + 5] = lines
+        design = design_of(knot_base[at], [part[at] for part in basis], stacked[row])
+        design_out[row] = design
+        band = pack_band(exact_dot_t(design * weighted[at], design))
+        for index in range(BAND):
+            send_out[row, index] = band[index : index + 1]
+        for index, line in enumerate(common):
+            send_out[row, BAND + index] = line
+
+
+def sources_kernel(
+    observed, source_partials, source_id, cal_id, weighted, calibration,
+    partials_out, factor_out, target_out, table_out, table, sem,
+):
+    copy = pltpu.make_async_copy(calibration, table, sem)
+    copy.start()
+    rows, slots = observed.shape
+    matrix = jnp.zeros((40, SRC_DEV), F32)
+    for row in range(rows):
+        at = slice(row, row + 1)
+        for index in range(5):
+            partials_out[row, index : index + 1] = source_partials[index, at]
+        partials_out[row, 5:] = jnp.zeros((SUB - 5, slots), F32)
+        partials = partials_out[row]
+        products = jnp.concatenate(
+            [partials * (weighted[at] * partials[index : index + 1]) for index in range(5)], axis=0
+        )
+        found = dot_t(jnp.concatenate(split3(products), axis=0), one_hot(source_id[at], SRC_DEV))
+        matrix = matrix + found[:40] + found[40:80] + found[80:]
+    inverse = small_factor(matrix)
+    for place, pair in enumerate(PLACES):
+        factor_out[place : place + 1] = inverse[pair]
+    factor_out[15:16] = jnp.zeros((1, SRC_DEV), F32)
+    copy.wait()
+    table_t = table[...].T
+    table_out[...] = table_t
+    for row, picked in enumerate(pick_from(table_t, cal_id[...])):
+        target_out[row : row + 1] = observed[row : row + 1] - picked
+
+
+def relay_kernel(received, send_out):
+    line = received.shape[0]
+    count = received.shape[1] - BAND - 1
+    for index in range(BAND):
+        total = received[0, index]
+        for device in range(1, line):
+            total = total + received[device, index]
+        for target in range(send_out.shape[0]):
+            send_out[target, index] = total
+    for device in range(line):
+        for index in range(count):
+            value = received[device, BAND + index]
+            for target in range(send_out.shape[0]):
+                send_out[target, BAND + device * count + index] = value
+
+
+def residual_step(targets, design, partials, factor, weighted, source_id, send_out):
+    rows = len(targets)
+    hits = [one_hot(source_id[row : row + 1], SRC_DEV) for row in range(rows)]
+    inverse = {pair: factor[place : place + 1] for place, pair in enumerate(PLACES)}
+    sides = jnp.zeros((SUB, SRC_DEV), F32)
+    for row in range(rows):
+        products = partials[row] * (weighted[row : row + 1] * targets[row])
+        found = dot_t(jnp.concatenate(split3(products), axis=0), hits[row])
+        sides = sides + found[:SUB] + found[SUB : 2 * SUB] + found[2 * SUB :]
+    params = small_apply(inverse, [sides[index : index + 1] for index in range(5)])
+    table = jnp.concatenate(params + [jnp.zeros((3, SRC_DEV), F32)], axis=0)
+    parts = jnp.concatenate(split3(table), axis=0)
+    explained = []
+    place = 0
+    for row in range(rows):
+        found = dot(parts, hits[row])
+        found = found[:SUB] + found[SUB : 2 * SUB] + found[2 * SUB :]
+        explained.append(jnp.sum(found * partials[row], axis=0, keepdims=True))
+        scaled = weighted[row : row + 1] * (targets[row] - explained[row])
+        for line in lines_of(scaled):
+            for device in range(send_out.shape[0]):
+                send_out[device, place] = line
+            place += 1
+        right = exact_dot_t(scaled, design[row])
+        for device in range(row, send_out.shape[0], rows):
+            send_out[device, send_out.shape[1] - 1] = right
+    return params, explained
+
+
+def first_kernel(received, target, design, partials, factor, weighted, source_id, send_out):
+    last = received.shape[1] - 1
+    targets = [
+        target[row : row + 1] - exact_dot(received[row, last], design[row])
+        for row in range(design.shape[0])
+    ]
+    residual_step(targets, design, partials, factor, weighted, source_id, send_out)
+
+
+def second_kernel(
+    pieces, picked, observed, design, partials, factor, weighted, source_id, send_out, params_out,
+    explained_out,
+):
+    rows = design.shape[0]
+    targets = [
+        observed[row : row + 1] - exact_dot(pieces[row], design[row]) - picked[row : row + 1]
+        for row in range(rows)
+    ]
+    params, explained = residual_step(
+        targets, design, partials, factor, weighted, source_id, send_out
+    )
+    for index in range(5):
+        params_out[index : index + 1] = params[index]
+    for row in range(rows):
+        explained_out[row : row + 1] = explained[row]
+
+
+def inverse_kernel(relayed, inverse_out):
+    rows = []
+    for index in range(BAND):
+        total = relayed[0, index]
+        for device in range(1, relayed.shape[0]):
+            total = total + relayed[device, index]
+        rows.append(total)
+    lower = unpack_band(jnp.concatenate(rows, axis=0))
+    diagonal = iota(lower.shape, 0) == iota(lower.shape, 1)
+    inverse_out[...] = spd_inverse(lower + jnp.where(diagonal, 1.0, lower.T))
+
+
+def wide(row, count):
+    tile = jnp.broadcast_to(row, (16, LANES)).astype(BF16)
+    return jnp.concatenate([tile] * (count // 16), axis=0)
+
+
+def unit_sums(relayed, line, value_of, total):
+    groups = relayed.shape[0]
+    count = (relayed.shape[1] - BAND) // (2 * line)
+    low_row = iota((LANES, LANES), 0).astype(F32).astype(BF16)
+    high_row = iota((HIGH, LANES), 0).astype(F32).astype(BF16)
+    one, none = jnp.ones((), BF16), jnp.zeros((), BF16)
+    for device in range(groups * line):
+        group, member = device // line, device % line
+        lefts, rights = [], []
+        for index in range(count):
+            unit = relayed[group, BAND + 2 * count * member + index]
+            high = jnp.floor(unit * (1.0 / LANES))
+            hit = low_row == wide(unit - LANES * high, LANES)
+            value = value_of(group, member, index)
+            first = value.astype(BF16).astype(F32)
+            lefts.append(
+                jnp.concatenate(
+                    [
+                        jnp.where(hit, wide(first, LANES), none),
+                        jnp.where(hit, wide(value - first, LANES), none),
+                    ],
+                    axis=0,
+                )
+            )
+            rights.append(jnp.where(high_row == wide(high, HIGH), one, none))
+        found = dot_t(jnp.concatenate(lefts, axis=1), jnp.concatenate(rights, axis=1))
+        if device == 0:
+            total[...] = found[:LANES] + found[LANES:]
+        else:
+            total[...] += found[:LANES] + found[LANES:]
+
+
+def scale_kernel(line, relayed, scale_out):
+    count = (relayed.shape[1] - BAND) // (2 * line)
+    unit_sums(
+        relayed,
+        line,
+        lambda group, member, index: relayed[group, BAND + count * (2 * member + 1) + index],
+        scale_out,
+    )
+    scale_out[...] = 1.0 / (scale_out[...] + 1.0)
+
+
+def update_kernel(line, values, relayed, table, scale, cal_id, picked_out, table_out):
+    unit_sums(
+        relayed, line, lambda group, member, index: values[group * line + member, index], table_out
+    )
+    table_t = table[...] + table_out[...] * scale[...]
+    table_out[...] = table_t
+    for row, picked in enumerate(pick_from(table_t, cal_id[...])):
+        picked_out[row : row + 1] = picked
+
+
+def attitude_kernel(values, inverse, attitude, send_out, attitude_out):
+    last = values.shape[1] - 1
+    total = values[0, last]
+    for device in range(1, values.shape[0]):
+        total = total + values[device, last]
+    line = attitude[...] + exact_dot(total, inverse[...])
+    attitude_out[...] = line
+    for target in range(send_out.shape[0]):
+        send_out[target] = line
+
+
+def final_kernel(pieces, picked, observed, design, explained, table, cal_out, resid_out):
+    cal_out[...] = table[...].T
+    for row in range(design.shape[0]):
+        at = slice(row, row + 1)
+        model = exact_dot(pieces[row], design[row])
+        resid_out[at] = observed[at] - model - picked[at] - explained[at]
+
+
+VMEM = pl.BlockSpec(memory_space=pltpu.VMEM)
+ANY = pl.BlockSpec(memory_space=pltpu.HBM)
+
+
+def call(kernel, outs, *args, away=0, scratch=()):
+    near = args[: len(args) - away]
+    far = [pltpu.with_memory_space_constraint(arg, pltpu.HBM) for arg in args[len(args) - away :]]
+    return pl.pallas_call(
+        kernel,
+        out_shape=outs,
+        in_specs=[VMEM] * len(near) + [ANY] * away,
+        out_specs=[VMEM] * len(outs),
+        scratch_shapes=scratch,
+        compiler_params=pltpu.CompilerParams(vmem_limit_bytes=VMEM_BYTES),
+    )(*near, *far)
+
+
+def stay(*shape, dtype=F32):
+    return pltpu.VMEM(shape, dtype)
+
+
+def leave(*shape):
+    return jax.ShapeDtypeStruct(shape, F32)
+
+
+def exchange(value, axes):
+    return lax.all_to_all(value, axes, 0, 0, tiled=True)
+
+
+def body(
+    observed, weight_obs, present, source_partials, attitude_partials, phase, knot_base, source_id,
+    cal_id, attitude, calibration,
+):
+    rows, slots = observed.shape
+    line, groups = lax.axis_size("tm"), lax.axis_size("src")
+    devices = line * groups
+    count = rows * slots // LANES
+    everyone = ("src", "tm")
+    first_q = attitude.reshape(1, WIDTH)
+    held = [weight_obs, present, attitude_partials, phase, knot_base]
+    send, design, weighted, seen, source_id, cal_id, source_partials, now = call(
+        normals_kernel,
+        [
+            leave(rows, BAND + 2 * count + 1, 1, LANES), stay(rows, WIDTH, slots),
+            stay(rows, slots), stay(rows, slots), stay(rows, slots, dtype=jnp.int32),
+            stay(rows, slots, dtype=jnp.int32), stay(*source_partials.shape), stay(1, WIDTH),
+        ],
+        observed, weight_obs, present, source_partials, attitude_partials, phase, knot_base,
+        source_id, cal_id, first_q,
+        away=10,
+        scratch=[pltpu.VMEM(each.shape, each.dtype) for each in held]
+        + [pltpu.VMEM((rows, SUB, slots), F32), pltpu.SemaphoreType.DMA((10,))],
+    )
+    received = exchange(send, "tm")
+    partials, factor, target, table = call(
+        sources_kernel,
+        [stay(rows, SUB, slots), stay(16, SRC_DEV), stay(rows, slots), stay(LANES, HIGH)],
+        seen, source_partials, source_id, cal_id, weighted, calibration.reshape(HIGH, LANES),
+        away=1,
+        scratch=[pltpu.VMEM((HIGH, LANES), F32), pltpu.SemaphoreType.DMA],
+    )
+    (relayed,) = call(
+        relay_kernel, [leave(groups, BAND + 2 * count * line, 1, LANES)], received
+    )
+    relayed, received = lax.optimization_barrier((relayed, received))
+    relayed = exchange(relayed, "src")
+    block = leave(devices, count + 1, 1, LANES)
+    (values,) = call(
+        first_kernel, [block], received, target, design, partials, factor, weighted, source_id
+    )
+    values = exchange(values, everyone)
+    (inverse,) = call(inverse_kernel, [stay(WIDTH, WIDTH)], relayed)
+    (scale,) = call(
+        functools.partial(scale_kernel, line), [stay(LANES, HIGH)], relayed
+    )
+
+    def solve_attitude(values, now, out):
+        return call(attitude_kernel, [leave(line, 1, WIDTH), out], values, inverse, now)
+
+    def solve_units(values, table):
+        return call(
+            functools.partial(update_kernel, line),
+            [stay(rows, slots), stay(LANES, HIGH)],
+            values, relayed, table, scale, cal_id,
+        )
+
+    send, now = solve_attitude(values, now, stay(1, WIDTH))
+    pieces = exchange(send, "tm")
+    picked, table = solve_units(values, table)
+    values, params, explained = call(
+        second_kernel,
+        [block, leave(5, SRC_DEV), stay(rows, slots)],
+        pieces, picked, seen, design, partials, factor, weighted, source_id,
+    )
+    values = exchange(values, everyone)
+    send, now = solve_attitude(values, now, leave(1, WIDTH))
+    pieces = exchange(send, "tm")
+    picked, table = solve_units(values, table)
+    cal, final = call(
+        final_kernel,
+        [leave(HIGH, LANES), leave(rows, slots)],
+        pieces, picked, seen, design, explained, table,
+    )
+    return (params, now.reshape(WIDTH), cal.reshape(CAL), final)
+
+
 def solution(mesh):
+    many = mesh.shape["src"] * mesh.shape["tm"]
     return jax.shard_map(
-        body,
+        body if many <= 64 else plain_body,
         mesh=mesh,
         in_specs=(
             P(None, ("src", "tm")),

time: 513 us -> 76.7 us (0.15)
  waiting for transfers between devices: 303 us -> 8.64 us
  other arithmetic: 74.1 us -> 0 us
  blocking collectives: 74.9 us -> 24.5 us
  local copies, waits for them, and re-layouts: 32.8 us -> 0 us
  Pallas kernels: 0 us -> 29.1 us
  between operations: 16.3 us -> 0.72 us
  starting transfers between devices: 0.43 us -> 13.1 us
  matrix products: 9.64 us -> 0 us
    psum x4 -> x0, waiting for transfers between devices: 303 us -> none  [the longest x2 208 us: body(): numer, denom = lax.psum((numer, denom), ('src', 'tm'))]
    another operation x13 -> x0, other arithmetic: 45.7 us -> none  [the longest x6 24.8 us: spd_solve(): lower = jnp.linalg.cholesky(matrix + eye)]
    all_gather x3 -> x0, blocking collectives: 34.2 us -> none  [attitude_model(): coefficients = lax.all_gather(local, 'tm', axis=0, tiled=True)]
    pallas_call x0 -> x12, Pallas kernels: none -> 29.1 us  [call(): pl.pallas_call(kernel, out_shape=outs, in_specs=[VMEM] * len(near) + [ANY...]
    all_to_all x0 -> x2, blocking collectives: none -> 24.5 us  [exchange(): return lax.all_to_all(value, axes, 0, 0, tiled=True)]
    psum x2 -> x0, blocking collectives: 23.8 us -> none  [body(): normal, right = lax.psum((normal[0], right[0]), 'src')]
    scatter-add x3 -> x0, other arithmetic: 19.6 us -> none  [the longest x2 13.1 us: body(): jax.ops.segment_sum((weighted * resid).reshape(-1), flat_cal, num_segment...]
    gather x6 -> x0, local copies, waits for them, and re-layouts: 18.5 us -> none  [the longest x4 12.3 us: body(): cal_now[cal_id]]
  transfers between devices with their start and end apart: 6 -> 4, of which waited for: 4 -> 2; matrix products, arithmetic and copies ran while one was open for 7% -> 0% of each run, Pallas kernels for 0% -> 30%
where the time goes in v1:
time: 76.7 us; the launch traced here: 76.2 us
  Pallas kernels  29.1 us (38%)
  blocking collectives  24.5 us (32%)
  starting transfers between devices  13.1 us (17%)
  waiting for transfers between devices  8.64 us (11%)
    pallas_call x12, Pallas kernels, call(): pl.pallas_call(kernel, out_shape=outs, in_specs=[VMEM] * len(near) + [ANY...  29.1 us
    all_to_all x2, blocking collectives, exchange(): return lax.all_to_all(value, axes, 0, 0, tiled=True)  24.5 us
    all_to_all x4, starting transfers between devices, exchange(): return lax.all_to_all(value, axes, 0, 0, tiled=True)  13.1 us
    all_to_all x4, waiting for transfers between devices, exchange(): return lax.all_to_all(value, axes, 0, 0, tiled=True)  8.64 us
  transfers between devices with their start and end apart: 4, of which 2 were waited for; matrix products, arithmetic and copies ran while one was open for 0% of the time, Pallas kernels for 30%

profile of v1, /device:TPU:0, one launch (start us, length us, event | category | flops | bytes accessed | tf_op | source)
XLA Modules:
  0.0 76.2 jit_solution(1859003873938401845)
XLA Ops:
  0.6 1.8 %shard_map.138 = (f32[4,33,1,128]{3,2,1,0:T(1,128)S(1)}, f32[4,128,256]{2,1,0:T(8,128)S(1)}, f32[4,256]{1,0:T(4,128)S(1)}, f32[4,256]{1,0:T(4,128)S(1)}, s32[4,2...) custom-call(f32[4,256]{1,0:T(4,128)} %observed_in.1, ...), custom_call_target="tpu_custom_call" | custom-call | tf_op jit(solution)/shard_map/pallas_call | solution.py:688
  2.5 11.9 %all_to_all.30.received = f32[4,33,1,128]{3,2,1,0:T(1,128)S(1)} all-to-all(f32[4,33,1,128]{3,2,1,0:T(1,128)S(1)} %get-tuple-element.31), channel_id=1, replica_groups=mesh['src'=8,'tm'=4] {'tm'}, dimensions={0} | all-to-all | bytes 135168 | tf_op jit(solution)/shard_map/all_to_all | solution.py:707
  14.3 0.9 %shard_map.139 = f32[8,80,1,128]{3,2,1,0:T(1,128)} custom-call(f32[4,33,1,128]{3,2,1,0:T(1,128)S(1)} %all_to_all.30.received), custom_call_target="tpu_custom_call" | custom-call | tf_op jit(solution)/shard_map/pallas_call | solution.py:688
  15.2 3.7 %all-to-all-start.2 = ((f32[8,80,1,128]{3,2,1,0:T(1,128)}), f32[8,80,1,128]{3,2,1,0:T(1,128)S(1)}, u32[]{:S(2)}, u32[]{:S(2)}) async-start(f32[8,80,1,128]{3,2,1,0:T(1,128)} %shard_map.139), calls=%async_computation.2 | async-start | bytes 655360 | tf_op jit(solution)/shard_map/all_to_all | solution.py:707
  18.9 1.4 %shard_map.140 = (f32[4,8,256]{2,1,0:T(8,128)S(1)}, f32[16,128]{1,0:T(8,128)S(1)}, f32[4,256]{1,0:T(4,128)S(1)}, f32[128,256]{1,0:T(8,128)S(1)}) custom-call(f32[4,256]{1,0:T(4,128)S(1)} %get-tuple-element.33.observed, f32[5,4,256]{2,1,0:T(4,128)S(1)} %get-tuple-element.34.source_partials, s32[4,256]{1,0:T(4,128)S(1)} %get-tuple-element.35.source_id, ...), custom_call_target="tpu_custom_call" | custom-call | tf_op jit(solution)/shard_map/pallas_call | solution.py:688
  20.4 2.0 %shard_map.141 = f32[32,9,1,128]{3,2,1,0:T(1,128)} custom-call(f32[4,33,1,128]{3,2,1,0:T(1,128)S(1)} %all_to_all.30.received, f32[4,256]{1,0:T(4,128)S(1)} %get-tuple-element.38.target, f32[4,128,256]{2,1,0:T(8,128)S(1)} %get-tuple-element.39.design, f32[4,8,256]{2,1,0:T(8,128)S(1)} %get-tuple-element.40.partials, f32[16,128]{1,0:T(8,128)S(1)} %get-tuple-element.41.factor, ...), custom_call_target="tpu_custom_call" | custom-call | tf_op jit(solution)/shard_map/pallas_call | solution.py:688
  22.4 4.2 %all-to-all-done.2.relayed = f32[8,80,1,128]{3,2,1,0:T(1,128)S(1)} async-done(((f32[8,80,1,128]{3,2,1,0:T(1,128)}), f32[8,80,1,128]{3,2,1,0:T(1,128)S(1)}, u32[]{:S(2)}, u32[]{:S(2)}) %all-to-all-start.2) | async-done | bytes 327712 | tf_op jit(solution)/shard_map/all_to_all | solution.py:707
  26.6 2.6 %all-to-all-start.1 = ((f32[32,9,1,128]{3,2,1,0:T(1,128)}), f32[32,9,1,128]{3,2,1,0:T(1,128)S(1)}, u32[]{:S(2)}, u32[]{:S(2)}) async-start(f32[32,9,1,128]{3,2,1,0:T(1,128)} %shard_map.141), calls=%async_computation.1 | async-start | bytes 294912 | tf_op jit(solution)/shard_map/all_to_all | solution.py:707
  29.2 4.2 %shard_map.142.inverse = f32[128,128]{1,0:T(8,128)S(1)} custom-call(f32[8,80,1,128]{3,2,1,0:T(1,128)S(1)} %all-to-all-done.2.relayed), custom_call_target="tpu_custom_call" | custom-call | tf_op jit(solution)/shard_map/pallas_call | solution.py:688
  33.4 4.4 %all-to-all-done.1.values = f32[32,9,1,128]{3,2,1,0:T(1,128)S(1)} async-done(((f32[32,9,1,128]{3,2,1,0:T(1,128)}), f32[32,9,1,128]{3,2,1,0:T(1,128)S(1)}, u32[]{:S(2)}, u32[]{:S(2)}) %all-to-all-start.1) | async-done | bytes 147488 | tf_op jit(solution)/shard_map/all_to_all | solution.py:707
  37.8 0.8 %shard_map.143 = (f32[4,1,128]{2,1,0:T(1,128)}, f32[1,128]{1,0:T(1,128)S(1)}) custom-call(f32[32,9,1,128]{3,2,1,0:T(1,128)S(1)} %all-to-all-done.1.values, f32[128,128]{1,0:T(8,128)S(1)} %shard_map.142.inverse, f32[1,128]{1,0:T(1,128)S(1)} %get-tuple-element.43.attitude), custom_call_target="tpu_custom_call" | custom-call | tf_op jit(solution)/shard_map/pallas_call | solution.py:688
  38.6 3.4 %all-to-all-start.3 = ((f32[4,1,128]{2,1,0:T(1,128)}), f32[4,1,128]{2,1,0:T(1,128)S(1)}, u32[]{:S(2)}, u32[]{:S(2)}) async-start(f32[4,1,128]{2,1,0:T(1,128)} %get-tuple-element.44), calls=%async_computation.3 | async-start | bytes 4096 | tf_op jit(solution)/shard_map/all_to_all | solution.py:707
  42.0 4.5 %shard_map.144.scale = f32[128,256]{1,0:T(8,128)S(1)} custom-call(f32[8,80,1,128]{3,2,1,0:T(1,128)S(1)} %all-to-all-done.2.relayed), custom_call_target="tpu_custom_call" | custom-call | tf_op jit(solution)/shard_map/pallas_call | solution.py:688
  46.5 5.2 %shard_map.145 = (f32[4,256]{1,0:T(4,128)S(1)}, f32[128,256]{1,0:T(8,128)S(1)}) custom-call(f32[32,9,1,128]{3,2,1,0:T(1,128)S(1)} %all-to-all-done.1.values, f32[8,80,1,128]{3,2,1,0:T(1,128)S(1)} %all-to-all-done.2.relayed, f32[128,256]{1,0:T(8,128)S(1)} %get-tuple-element.45.table, f32[128,256]{1,0:T(8,128)S(1)} %shard_map.144.scale, ...), custom_call_target="tpu_custom_call" | custom-call | tf_op jit(solution)/shard_map/pallas_call | solution.py:688
  51.8 0.0 all-to-all-done.3.pieces
  51.8 1.3 %shard_map.146 = (f32[32,9,1,128]{3,2,1,0:T(1,128)S(1)}, f32[5,128]{1,0:T(8,128)}, f32[4,256]{1,0:T(4,128)S(1)}) custom-call(f32[4,1,128]{2,1,0:T(1,128)S(1)} %all-to-all-done.3.pieces, f32[4,256]{1,0:T(4,128)S(1)} %get-tuple-element.46.picked, f32[4,256]{1,0:T(4,128)S(1)} %get-tuple-element.33.observed, f32[4,128,256]{2,1,0:T(8,128)S(1)} %get-tuple-element.39.design, ...), custom_call_target="tpu_custom_call" | custom-call | tf_op jit(solution)/shard_map/pallas_call | solution.py:688
  53.1 12.7 %all_to_all.31.values = f32[32,9,1,128]{3,2,1,0:T(1,128)S(1)} all-to-all(f32[32,9,1,128]{3,2,1,0:T(1,128)S(1)} %get-tuple-element.48), channel_id=1, replica_groups=mesh['src'=8,'tm'=4] {'src','tm'}, dimensions={0} | all-to-all | bytes 294912 | tf_op jit(solution)/shard_map/all_to_all | solution.py:707
  65.7 0.8 %shard_map.147 = (f32[4,1,128]{2,1,0:T(1,128)}, f32[1,128]{1,0:T(1,128)}) custom-call(f32[32,9,1,128]{3,2,1,0:T(1,128)S(1)} %all_to_all.31.values, f32[128,128]{1,0:T(8,128)S(1)} %shard_map.142.inverse, f32[1,128]{1,0:T(1,128)S(1)} %get-tuple-element.49.attitude), custom_call_target="tpu_custom_call" | custom-call | tf_op jit(solution)/shard_map/pallas_call | solution.py:688
  66.5 3.4 %all-to-all-start.5 = ((f32[4,1,128]{2,1,0:T(1,128)}), f32[4,1,128]{2,1,0:T(1,128)S(1)}, u32[]{:S(2)}, u32[]{:S(2)}) async-start(f32[4,1,128]{2,1,0:T(1,128)} %get-tuple-element.51), calls=%async_computation.5 | async-start | bytes 4096 | tf_op jit(solution)/shard_map/all_to_all | solution.py:707
  70.0 5.2 %shard_map.148 = (f32[4,256]{1,0:T(4,128)S(1)}, f32[128,256]{1,0:T(8,128)S(1)}) custom-call(f32[32,9,1,128]{3,2,1,0:T(1,128)S(1)} %all_to_all.31.values, f32[8,80,1,128]{3,2,1,0:T(1,128)S(1)} %all-to-all-done.2.relayed, f32[128,256]{1,0:T(8,128)S(1)} %get-tuple-element.52.table, f32[128,256]{1,0:T(8,128)S(1)} %shard_map.144.scale, ...), custom_call_target="tpu_custom_call" | custom-call | tf_op jit(solution)/shard_map/pallas_call | solution.py:688
  75.2 0.0 all-to-all-done.5.pieces
  75.2 1.0 %shard_map.149 = (f32[256,128]{1,0:T(8,128)}, f32[4,256]{1,0:T(4,128)}) custom-call(f32[4,1,128]{2,1,0:T(1,128)S(1)} %all-to-all-done.5.pieces, f32[4,256]{1,0:T(4,128)S(1)} %get-tuple-element.53.picked, f32[4,256]{1,0:T(4,128)S(1)} %get-tuple-element.33.observed, f32[4,128,256]{2,1,0:T(8,128)S(1)} %get-tuple-element.39.design, ...), custom_call_target="tpu_custom_call" | custom-call | tf_op jit(solution)/shard_map/pallas_call | solution.py:688
Async XLA Ops:
  15.2 11.4 %all-to-all-start.2 = ((f32[8,80,1,128]{3,2,1,0:T(1,128)}), f32[8,80,1,128]{3,2,1,0:T(1,128)S(1)}, u32[]{:S(2)}, u32[]{:S(2)}) async-start(f32[8,80,1,128]{3,2,1,0:T(1,128)} %shard_map.139), calls=%async_computation.2 | async-start | bytes 655360 | tf_op jit(solution)/shard_map/all_to_all | solution.py:707
  26.6 11.2 %all-to-all-start.1 = ((f32[32,9,1,128]{3,2,1,0:T(1,128)}), f32[32,9,1,128]{3,2,1,0:T(1,128)S(1)}, u32[]{:S(2)}, u32[]{:S(2)}) async-start(f32[32,9,1,128]{3,2,1,0:T(1,128)} %shard_map.141), calls=%async_computation.1 | async-start | bytes 294912 | tf_op jit(solution)/shard_map/all_to_all | solution.py:707
  38.6 13.2 %all-to-all-start.3 = ((f32[4,1,128]{2,1,0:T(1,128)}), f32[4,1,128]{2,1,0:T(1,128)S(1)}, u32[]{:S(2)}, u32[]{:S(2)}) async-start(f32[4,1,128]{2,1,0:T(1,128)} %get-tuple-element.44), calls=%async_computation.3 | async-start | bytes 4096 | tf_op jit(solution)/shard_map/all_to_all | solution.py:707
  66.5 8.7 %all-to-all-start.5 = ((f32[4,1,128]{2,1,0:T(1,128)}), f32[4,1,128]{2,1,0:T(1,128)S(1)}, u32[]{:S(2)}, u32[]{:S(2)}) async-start(f32[4,1,128]{2,1,0:T(1,128)} %get-tuple-element.51), calls=%async_computation.5 | async-start | bytes 4096 | tf_op jit(solution)/shard_map/all_to_all | solution.py:707

commit v2 on v1

--- a/solution.py
+++ b/solution.py
@@ -147,7 +147,7 @@
 )
 
 
-def spd_inverse(matrix):
+def spd_inverse(matrix, inverse_out):
     tiles = [matrix[8 * tile : 8 * tile + 8] for tile in range(WIDTH // 8)]
     lane = iota((8, WIDTH), 1)
     lane_row = iota((1, WIDTH), 1)
@@ -168,7 +168,9 @@
                         column = jnp.where(row == sub, -1.0, column)
                         drop = drop | (iota((8, WIDTH), 0) == sub)
                     tiles[tile] = jnp.where(drop, 0.0, tiles[tile]) - column * line
-    return -jnp.concatenate(tiles, axis=0)
+            yield
+    for tile, value in enumerate(tiles):
+        inverse_out[8 * tile : 8 * tile + 8] = -value
 
 
 def small_factor(sums):
@@ -415,6 +417,7 @@
 
 
 BAND = 16
+PIECE = 2
 
 
 def fetch(pairs, sems):
@@ -428,11 +431,10 @@
         copy.wait()
 
 
-def lines_of(value):
-    rows, slots = value.shape
-    return [
-        value[row : row + 1, at : at + LANES] for row in range(rows) for at in range(0, slots, LANES)
-    ]
+def tile_of(value):
+    return jnp.concatenate(
+        [value[:, at : at + LANES] for at in range(0, value.shape[1], LANES)], axis=0
+    )
 
 
 def pick_from(table_t, ids):
@@ -447,8 +449,8 @@
 def normals_kernel(
     observed_in, weight_in, present_in, source_in, attitude_in, phase_in, knot_in, id_in, cal_in,
     start_in,
-    send_out, design_out, weighted_out, observed, source_id, cal_id, source_partials, start,
-    weight_obs, present, attitude_partials, phase, knot_base, stacked, sems,
+    send_out, design_out, weighted_out, observed, source_id, cal_id, source_partials,
+    weight_obs, present, attitude_partials, phase, knot_base, start, stacked, sems,
 ):
     fetch(
         [
@@ -471,7 +473,15 @@
         (-3.0 * cube + 3.0 * square + 3.0 * u + 1.0) / 6.0,
         cube / 6.0,
     ]
-    common = lines_of(cal_id[...].astype(F32)) + lines_of(weighted) + [start[...]]
+    first, second = tile_of(cal_id[...].astype(F32)), tile_of(weighted)
+    count = first.shape[0]
+    devices = send_out.shape[0]
+    for index in range(count):
+        for device in range(devices):
+            send_out[device, PIECE + index] = first[index : index + 1]
+            send_out[device, PIECE + count + index] = second[index : index + 1]
+    for device in range(devices):
+        send_out[device, PIECE + 2 * count] = start[...]
     for row in range(rows):
         at = slice(row, row + 1)
         for channel in range(4):
@@ -482,9 +492,8 @@
         design_out[row] = design
         band = pack_band(exact_dot_t(design * weighted[at], design))
         for index in range(BAND):
-            send_out[row, index] = band[index : index + 1]
-        for index, line in enumerate(common):
-            send_out[row, BAND + index] = line
+            device, place = divmod(row * BAND + index, PIECE)
+            send_out[device, place] = band[index : index + 1]
 
 
 def sources_kernel(
@@ -517,24 +526,9 @@
         target_out[row : row + 1] = observed[row : row + 1] - picked
 
 
-def relay_kernel(received, send_out):
-    line = received.shape[0]
-    count = received.shape[1] - BAND - 1
-    for index in range(BAND):
-        total = received[0, index]
-        for device in range(1, line):
-            total = total + received[device, index]
-        for target in range(send_out.shape[0]):
-            send_out[target, index] = total
-    for device in range(line):
-        for index in range(count):
-            value = received[device, BAND + index]
-            for target in range(send_out.shape[0]):
-                send_out[target, BAND + device * count + index] = value
-
-
 def residual_step(targets, design, partials, factor, weighted, source_id, send_out):
-    rows = len(targets)
+    rows, slots = len(targets), targets[0].shape[1]
+    count = rows * slots // LANES
     hits = [one_hot(source_id[row : row + 1], SRC_DEV) for row in range(rows)]
     inverse = {pair: factor[place : place + 1] for place, pair in enumerate(PLACES)}
     sides = jnp.zeros((SUB, SRC_DEV), F32)
@@ -546,59 +540,33 @@
     table = jnp.concatenate(params + [jnp.zeros((3, SRC_DEV), F32)], axis=0)
     parts = jnp.concatenate(split3(table), axis=0)
     explained = []
-    place = 0
     for row in range(rows):
         found = dot(parts, hits[row])
         found = found[:SUB] + found[SUB : 2 * SUB] + found[2 * SUB :]
         explained.append(jnp.sum(found * partials[row], axis=0, keepdims=True))
         scaled = weighted[row : row + 1] * (targets[row] - explained[row])
-        for line in lines_of(scaled):
+        for place in range(slots // LANES):
             for device in range(send_out.shape[0]):
-                send_out[device, place] = line
-            place += 1
+                send_out[device, place * rows + row] = scaled[:, place * LANES : (place + 1) * LANES]
         right = exact_dot_t(scaled, design[row])
-        for device in range(row, send_out.shape[0], rows):
-            send_out[device, send_out.shape[1] - 1] = right
+        for device in range(send_out.shape[0]):
+            send_out[device, count + row] = right
     return params, explained
 
 
 def first_kernel(received, target, design, partials, factor, weighted, source_id, send_out):
+    rows = design.shape[0]
     last = received.shape[1] - 1
     targets = [
-        target[row : row + 1] - exact_dot(received[row, last], design[row])
-        for row in range(design.shape[0])
+        target[row : row + 1] - exact_dot(received[row, last], design[row]) for row in range(rows)
     ]
     residual_step(targets, design, partials, factor, weighted, source_id, send_out)
-
-
-def second_kernel(
-    pieces, picked, observed, design, partials, factor, weighted, source_id, send_out, params_out,
-    explained_out,
-):
-    rows = design.shape[0]
-    targets = [
-        observed[row : row + 1] - exact_dot(pieces[row], design[row]) - picked[row : row + 1]
-        for row in range(rows)
-    ]
-    params, explained = residual_step(
-        targets, design, partials, factor, weighted, source_id, send_out
-    )
-    for index in range(5):
-        params_out[index : index + 1] = params[index]
-    for row in range(rows):
-        explained_out[row : row + 1] = explained[row]
-
-
-def inverse_kernel(relayed, inverse_out):
-    rows = []
-    for index in range(BAND):
-        total = relayed[0, index]
-        for device in range(1, relayed.shape[0]):
-            total = total + relayed[device, index]
-        rows.append(total)
-    lower = unpack_band(jnp.concatenate(rows, axis=0))
-    diagonal = iota(lower.shape, 0) == iota(lower.shape, 1)
-    inverse_out[...] = spd_inverse(lower + jnp.where(diagonal, 1.0, lower.T))
+    for place in range(PIECE):
+        total = received[0, place]
+        for device in range(1, received.shape[0]):
+            total = total + received[device, place]
+        for device in range(send_out.shape[0]):
+            send_out[device, send_out.shape[1] - PIECE + place] = total
 
 
 def wide(row, count):
@@ -606,20 +574,18 @@
     return jnp.concatenate([tile] * (count // 16), axis=0)
 
 
-def unit_sums(relayed, line, value_of, total):
-    groups = relayed.shape[0]
-    count = (relayed.shape[1] - BAND) // (2 * line)
+def unit_sums(received, value_of, total):
+    count = (received.shape[1] - PIECE - 1) // 2
     low_row = iota((LANES, LANES), 0).astype(F32).astype(BF16)
     high_row = iota((HIGH, LANES), 0).astype(F32).astype(BF16)
     one, none = jnp.ones((), BF16), jnp.zeros((), BF16)
-    for device in range(groups * line):
-        group, member = device // line, device % line
+    for device in range(received.shape[0]):
         lefts, rights = [], []
         for index in range(count):
-            unit = relayed[group, BAND + 2 * count * member + index]
+            unit = received[device, PIECE + index]
             high = jnp.floor(unit * (1.0 / LANES))
             hit = low_row == wide(unit - LANES * high, LANES)
-            value = value_of(group, member, index)
+            value = value_of(device, index)
             first = value.astype(BF16).astype(F32)
             lefts.append(
                 jnp.concatenate(
@@ -636,46 +602,100 @@
             total[...] = found[:LANES] + found[LANES:]
         else:
             total[...] += found[:LANES] + found[LANES:]
-
-
-def scale_kernel(line, relayed, scale_out):
-    count = (relayed.shape[1] - BAND) // (2 * line)
-    unit_sums(
-        relayed,
-        line,
-        lambda group, member, index: relayed[group, BAND + count * (2 * member + 1) + index],
-        scale_out,
+        yield
+
+
+def matrix_of(band):
+    lower = unpack_band(band)
+    diagonal = iota(lower.shape, 0) == iota(lower.shape, 1)
+    return lower + jnp.where(diagonal, 1.0, lower.T)
+
+
+def together(works):
+    works = list(works)
+    while works:
+        for work in list(works):
+            if next(work, works) is works:
+                works.remove(work)
+
+
+def scale_kernel(received, scale_out):
+    count = (received.shape[1] - PIECE - 1) // 2
+    together(
+        [
+            unit_sums(
+                received,
+                lambda device, index: received[device, PIECE + count + index],
+                scale_out,
+            )
+        ]
     )
     scale_out[...] = 1.0 / (scale_out[...] + 1.0)
 
 
-def update_kernel(line, values, relayed, table, scale, cal_id, picked_out, table_out):
-    unit_sums(
-        relayed, line, lambda group, member, index: values[group * line + member, index], table_out
+def right_side(values, place):
+    total = values[0, place]
+    for device in range(1, values.shape[0]):
+        total = total + values[device, place]
+    return total
+
+
+def second_kernel(
+    values, received, table, scale, cal_id, observed, design, partials, factor, weighted, source_id,
+    send_out, params_out, explained_out, table_out, attitude_out, inverses_out, bands,
+):
+    rows = design.shape[0]
+    count = values.shape[1] - rows - PIECE
+    for device in range(values.shape[0]):
+        for place in range(PIECE):
+            at = PIECE * device + place
+            bands[at : at + 1] = values[device, count + rows + place]
+    together(
+        [unit_sums(received, lambda device, index: values[device, index], table_out)]
+        + [
+            spd_inverse(
+                matrix_of(bands[BAND * row : BAND * (row + 1)]), inverses_out.at[row]
+            )
+            for row in range(rows)
+        ]
     )
     table_t = table[...] + table_out[...] * scale[...]
     table_out[...] = table_t
+    targets = []
     for row, picked in enumerate(pick_from(table_t, cal_id[...])):
-        picked_out[row : row + 1] = picked
-
-
-def attitude_kernel(values, inverse, attitude, send_out, attitude_out):
-    last = values.shape[1] - 1
-    total = values[0, last]
-    for device in range(1, values.shape[0]):
-        total = total + values[device, last]
-    line = attitude[...] + exact_dot(total, inverse[...])
-    attitude_out[...] = line
-    for target in range(send_out.shape[0]):
-        send_out[target] = line
-
-
-def final_kernel(pieces, picked, observed, design, explained, table, cal_out, resid_out):
-    cal_out[...] = table[...].T
-    for row in range(design.shape[0]):
+        new = received[row, received.shape[1] - 1] + exact_dot(
+            right_side(values, count + row), inverses_out[row]
+        )
+        attitude_out[row : row + 1] = new
+        targets.append(observed[row : row + 1] - exact_dot(new, design[row]) - picked)
+    params, explained = residual_step(
+        targets, design, partials, factor, weighted, source_id, send_out
+    )
+    for index in range(5):
+        params_out[index : index + 1] = params[index]
+    for row in range(rows):
+        explained_out[row : row + 1] = explained[row]
+
+
+def final_kernel(
+    axis, values, received, inverses, attitude, table, scale, cal_id, observed, design, explained,
+    cal_out, attitude_out, resid_out, sums,
+):
+    rows = design.shape[0]
+    count = values.shape[1] - rows
+    me = lax.axis_index(axis)
+    models = []
+    for row in range(rows):
+        new = attitude[row : row + 1] + exact_dot(right_side(values, count + row), inverses[row])
+        models.append(exact_dot(new, design[row]))
+        own = new if row == 0 else jnp.where(me == row, new, own)
+    attitude_out[...] = own
+    together([unit_sums(received, lambda device, index: values[device, index], sums)])
+    table_t = table[...] + sums[...] * scale[...]
+    cal_out[...] = table_t.T
+    for row, picked in enumerate(pick_from(table_t, cal_id[...])):
         at = slice(row, row + 1)
-        model = exact_dot(pieces[row], design[row])
-        resid_out[at] = observed[at] - model - picked[at] - explained[at]
+        resid_out[at] = observed[at] - models[row] - picked - explained[at]
 
 
 VMEM = pl.BlockSpec(memory_space=pltpu.VMEM)
@@ -703,8 +723,8 @@
     return jax.ShapeDtypeStruct(shape, F32)
 
 
-def exchange(value, axes):
-    return lax.all_to_all(value, axes, 0, 0, tiled=True)
+def exchange(value):
+    return lax.all_to_all(value, ("src", "tm"), 0, 0, tiled=True)
 
 
 def body(
@@ -712,18 +732,16 @@
     cal_id, attitude, calibration,
 ):
     rows, slots = observed.shape
-    line, groups = lax.axis_size("tm"), lax.axis_size("src")
-    devices = line * groups
+    devices = lax.axis_size("src") * lax.axis_size("tm")
     count = rows * slots // LANES
-    everyone = ("src", "tm")
     first_q = attitude.reshape(1, WIDTH)
-    held = [weight_obs, present, attitude_partials, phase, knot_base]
-    send, design, weighted, seen, source_id, cal_id, source_partials, now = call(
+    held = [weight_obs, present, attitude_partials, phase, knot_base, first_q]
+    received, design, weighted, seen, source_id, cal_id, source_partials = call(
         normals_kernel,
         [
-            leave(rows, BAND + 2 * count + 1, 1, LANES), stay(rows, WIDTH, slots),
+            leave(devices, PIECE + 2 * count + 1, 1, LANES), stay(rows, WIDTH, slots),
             stay(rows, slots), stay(rows, slots), stay(rows, slots, dtype=jnp.int32),
-            stay(rows, slots, dtype=jnp.int32), stay(*source_partials.shape), stay(1, WIDTH),
+            stay(rows, slots, dtype=jnp.int32), stay(*source_partials.shape),
         ],
         observed, weight_obs, present, source_partials, attitude_partials, phase, knot_base,
         source_id, cal_id, first_q,
@@ -731,7 +749,7 @@
         scratch=[pltpu.VMEM(each.shape, each.dtype) for each in held]
         + [pltpu.VMEM((rows, SUB, slots), F32), pltpu.SemaphoreType.DMA((10,))],
     )
-    received = exchange(send, "tm")
+    received = exchange(received)
     partials, factor, target, table = call(
         sources_kernel,
         [stay(rows, SUB, slots), stay(16, SRC_DEV), stay(rows, slots), stay(LANES, HIGH)],
@@ -739,47 +757,29 @@
         away=1,
         scratch=[pltpu.VMEM((HIGH, LANES), F32), pltpu.SemaphoreType.DMA],
     )
-    (relayed,) = call(
-        relay_kernel, [leave(groups, BAND + 2 * count * line, 1, LANES)], received
-    )
-    relayed, received = lax.optimization_barrier((relayed, received))
-    relayed = exchange(relayed, "src")
-    block = leave(devices, count + 1, 1, LANES)
+    received, factor = lax.optimization_barrier((received, factor))
     (values,) = call(
-        first_kernel, [block], received, target, design, partials, factor, weighted, source_id
-    )
-    values = exchange(values, everyone)
-    (inverse,) = call(inverse_kernel, [stay(WIDTH, WIDTH)], relayed)
-    (scale,) = call(
-        functools.partial(scale_kernel, line), [stay(LANES, HIGH)], relayed
-    )
-
-    def solve_attitude(values, now, out):
-        return call(attitude_kernel, [leave(line, 1, WIDTH), out], values, inverse, now)
-
-    def solve_units(values, table):
-        return call(
-            functools.partial(update_kernel, line),
-            [stay(rows, slots), stay(LANES, HIGH)],
-            values, relayed, table, scale, cal_id,
-        )
-
-    send, now = solve_attitude(values, now, stay(1, WIDTH))
-    pieces = exchange(send, "tm")
-    picked, table = solve_units(values, table)
-    values, params, explained = call(
+        first_kernel, [leave(devices, count + rows + PIECE, 1, LANES)],
+        received, target, design, partials, factor, weighted, source_id,
+    )
+    values, received = lax.optimization_barrier((values, received))
+    values = exchange(values)
+    (scale,) = call(scale_kernel, [stay(LANES, HIGH)], received)
+    values, params, explained, table, now, inverses = call(
         second_kernel,
-        [block, leave(5, SRC_DEV), stay(rows, slots)],
-        pieces, picked, seen, design, partials, factor, weighted, source_id,
-    )
-    values = exchange(values, everyone)
-    send, now = solve_attitude(values, now, leave(1, WIDTH))
-    pieces = exchange(send, "tm")
-    picked, table = solve_units(values, table)
-    cal, final = call(
-        final_kernel,
-        [leave(HIGH, LANES), leave(rows, slots)],
-        pieces, picked, seen, design, explained, table,
+        [
+            leave(devices, count + rows, 1, LANES), leave(5, SRC_DEV), stay(rows, slots),
+            stay(LANES, HIGH), stay(rows, WIDTH), stay(rows, WIDTH, WIDTH),
+        ],
+        values, received, table, scale, cal_id, seen, design, partials, factor, weighted, source_id,
+        scratch=[pltpu.VMEM((rows * BAND, WIDTH), F32)],
+    )
+    values = exchange(values)
+    cal, now, final = call(
+        functools.partial(final_kernel, "tm"),
+        [leave(HIGH, LANES), leave(1, WIDTH), leave(rows, slots)],
+        values, received, inverses, now, table, scale, cal_id, seen, design, explained,
+        scratch=[pltpu.VMEM((LANES, HIGH), F32)],
     )
     return (params, now.reshape(WIDTH), cal.reshape(CAL), final)
 
@@ -787,7 +787,7 @@
 def solution(mesh):
     many = mesh.shape["src"] * mesh.shape["tm"]
     return jax.shard_map(
-        body if many <= 64 else plain_body,
+        body if many * PIECE == mesh.shape["tm"] * BAND else plain_body,
         mesh=mesh,
         in_specs=(
             P(None, ("src", "tm")),

time: 76.7 us -> 64.8 us (0.84)
  blocking collectives: 24.5 us -> 11.6 us
  waiting for transfers between devices: 8.64 us -> 14.4 us
  starting transfers between devices: 13.1 us -> 10.6 us
  Pallas kernels: 29.1 us -> 27.1 us
    all_to_all x2 -> x1, blocking collectives: 24.5 us -> 11.6 us  [exchange(): return lax.all_to_all(value, ('src', 'tm'), 0, 0, tiled=True)]
    all_to_all x4 -> x2, waiting for transfers between devices: 8.64 us -> 14.4 us  [exchange(): return lax.all_to_all(value, ('src', 'tm'), 0, 0, tiled=True)]
    all_to_all x4 -> x2, starting transfers between devices: 13.1 us -> 10.6 us  [exchange(): return lax.all_to_all(value, ('src', 'tm'), 0, 0, tiled=True)]
    pallas_call x12 -> x6, Pallas kernels: 29.1 us -> 27.1 us  [call(): pl.pallas_call(kernel, out_shape=outs, in_specs=[VMEM] * len(near) + [ANY...]
  transfers between devices with their start and end apart: 4 -> 2, of which waited for: 2 -> 2; matrix products, arithmetic and copies ran while one was open for 0% -> 0% of each run, Pallas kernels for 30% -> 9%
where the time goes in v2:
time: 64.8 us; the launch traced here: 64.4 us
  Pallas kernels  27.1 us (42%)
  waiting for transfers between devices  14.4 us (22%)
  blocking collectives  11.6 us (18%)
  starting transfers between devices  10.6 us (16%)
  between operations  0.68 us (1%)
    pallas_call x6, Pallas kernels, call(): pl.pallas_call(kernel, out_shape=outs, in_specs=[VMEM] * len(near) + [ANY...  27.1 us
    all_to_all x2, waiting for transfers between devices, exchange(): return lax.all_to_all(value, ('src', 'tm'), 0, 0, tiled=True)  14.4 us
    all_to_all x1, blocking collectives, exchange(): return lax.all_to_all(value, ('src', 'tm'), 0, 0, tiled=True)  11.6 us
    all_to_all x2, starting transfers between devices, exchange(): return lax.all_to_all(value, ('src', 'tm'), 0, 0, tiled=True)  10.6 us
  transfers between devices with their start and end apart: 2, of which 2 were waited for; matrix products, arithmetic and copies ran while one was open for 0% of the time, Pallas kernels for 9%

profile of v2, /device:TPU:0, one launch (start us, length us, event | category | flops | bytes accessed | tf_op | source)
XLA Modules:
  0.0 64.4 jit_solution(11783968300946541496)
XLA Ops:
  0.6 2.5 %shard_map.138 = (f32[32,19,1,128]{3,2,1,0:T(1,128)}, f32[4,128,256]{2,1,0:T(8,128)S(1)}, f32[4,256]{1,0:T(4,128)S(1)}, f32[4,256]{1,0:T(4,128)S(1)}, s32[4,256]...) custom-call(f32[4,256]{1,0:T(4,128)} %observed_in.1, f32[4,256]{1,0:T(4,128)} %weight_in.1, ...), custom_call_target="tpu_custom_call" | custom-call | tf_op jit(solution)/shard_map/pallas_call | solution.py:708
  3.2 7.3 %all-to-all-start = ((f32[32,19,1,128]{3,2,1,0:T(1,128)}), f32[32,19,1,128]{3,2,1,0:T(1,128)S(1)}, u32[]{:S(2)}, u32[]{:S(2)}) async-start(f32[32,19,1,128]{3,2,1,0:T(1,128)} %get-tuple-element.28), calls=%async_computation | async-start | bytes 622592 | tf_op jit(solution)/shard_map/all_to_all | solution.py:727
  10.5 1.4 %shard_map.139 = (f32[4,8,256]{2,1,0:T(8,128)S(1)}, f32[16,128]{1,0:T(8,128)S(1)}, f32[4,256]{1,0:T(4,128)S(1)}, f32[128,256]{1,0:T(8,128)S(1)}) custom-call(f32[4,256]{1,0:T(4,128)S(1)} %get-tuple-element.29.observed, f32[5,4,256]{2,1,0:T(4,128)S(1)} %get-tuple-element.30.source_partials, s32[4,256]{1,0:T(4,128)S(1)} %get-tuple-element.31.source_id, ...), custom_call_target="tpu_custom_call" | custom-call | tf_op jit(solution)/shard_map/pallas_call | solution.py:708
  11.9 9.3 %all-to-all-done.received = f32[32,19,1,128]{3,2,1,0:T(1,128)S(1)} async-done(((f32[32,19,1,128]{3,2,1,0:T(1,128)}), f32[32,19,1,128]{3,2,1,0:T(1,128)S(1)}, u32[]{:S(2)}, u32[]{:S(2)}) %all-to-all-start) | async-done | bytes 311328 | tf_op jit(solution)/shard_map/all_to_all | solution.py:727
  21.3 2.0 %shard_map.140 = f32[32,14,1,128]{3,2,1,0:T(1,128)} custom-call(f32[32,19,1,128]{3,2,1,0:T(1,128)S(1)} %all-to-all-done.received, f32[4,256]{1,0:T(4,128)S(1)} %get-tuple-element.36.target, f32[4,128,256]{2,1,0:T(8,128)S(1)} %get-tuple-element.37.design, f32[4,8,256]{2,1,0:T(8,128)S(1)} %get-tuple-element.38.partials, ...), custom_call_target="tpu_custom_call" | custom-call | tf_op jit(solution)/shard_map/pallas_call | solution.py:708
  23.3 3.3 %all-to-all-start.1 = ((f32[32,14,1,128]{3,2,1,0:T(1,128)}), f32[32,14,1,128]{3,2,1,0:T(1,128)S(1)}, u32[]{:S(2)}, u32[]{:S(2)}) async-start(f32[32,14,1,128]{3,2,1,0:T(1,128)} %shard_map.140), calls=%async_computation.1 | async-start | bytes 458752 | tf_op jit(solution)/shard_map/all_to_all | solution.py:727
  26.6 4.5 %shard_map.141.scale = f32[128,256]{1,0:T(8,128)S(1)} custom-call(f32[32,19,1,128]{3,2,1,0:T(1,128)S(1)} %all-to-all-done.received), custom_call_target="tpu_custom_call" | custom-call | tf_op jit(solution)/shard_map/pallas_call | solution.py:708
  31.2 5.1 %all-to-all-done.1.values = f32[32,14,1,128]{3,2,1,0:T(1,128)S(1)} async-done(((f32[32,14,1,128]{3,2,1,0:T(1,128)}), f32[32,14,1,128]{3,2,1,0:T(1,128)S(1)}, u32[]{:S(2)}, u32[]{:S(2)}) %all-to-all-start.1) | async-done | bytes 229408 | tf_op jit(solution)/shard_map/all_to_all | solution.py:727
  36.3 10.4 %shard_map.142 = (f32[32,12,1,128]{3,2,1,0:T(1,128)S(1)}, f32[5,128]{1,0:T(8,128)}, f32[4,256]{1,0:T(4,128)S(1)}, f32[128,256]{1,0:T(8,128)S(1)}, f32[4,128]{1,0:T(4,128)S(1)}, /*index=5*/f32[4,128,128]{2,1,0:T(8,128)S(1)}) custom-call(f32[32,14,1,128]{3,2,1,0:T(1,128)S(1)} %all-to-all-done.1.values, f32[32,19,1,128]{3,2,1,0:T(1,128)S(1)} %all-to-all-done.received, ...), custom_call_target="tpu_custom_call" | custom-call | tf_op jit(solution)/shard_map/pallas_call | solution.py:708
  46.6 11.6 %all_to_all.15.values = f32[32,12,1,128]{3,2,1,0:T(1,128)S(1)} all-to-all(f32[32,12,1,128]{3,2,1,0:T(1,128)S(1)} %get-tuple-element.44), channel_id=1, replica_groups=mesh['src'=8,'tm'=4] {'src','tm'}, dimensions={0} | all-to-all | bytes 393216 | tf_op jit(solution)/shard_map/all_to_all | solution.py:727
  58.2 6.2 %shard_map.143 = (f32[256,128]{1,0:T(8,128)}, f32[1,128]{1,0:T(1,128)}, f32[4,256]{1,0:T(4,128)}) custom-call(f32[32,12,1,128]{3,2,1,0:T(1,128)S(1)} %all_to_all.15.values, f32[32,19,1,128]{3,2,1,0:T(1,128)S(1)} %all-to-all-done.received, f32[4,128,128]{2,1,0:T(8,128)S(1)} %get-tuple-element.45.inverses, f32[4,128]{1,0:T(4,128)S(1)} %get-tuple-element.46.attitude, ...), custom_call_target="tpu_custom_call" | custom-call | tf_op jit(solution)/shard_map/pallas_call | solution.py:708
Async XLA Ops:
  3.2 18.1 %all-to-all-start = ((f32[32,19,1,128]{3,2,1,0:T(1,128)}), f32[32,19,1,128]{3,2,1,0:T(1,128)S(1)}, u32[]{:S(2)}, u32[]{:S(2)}) async-start(f32[32,19,1,128]{3,2,1,0:T(1,128)} %get-tuple-element.28), calls=%async_computation | async-start | bytes 622592 | tf_op jit(solution)/shard_map/all_to_all | solution.py:727
  23.3 13.0 %all-to-all-start.1 = ((f32[32,14,1,128]{3,2,1,0:T(1,128)}), f32[32,14,1,128]{3,2,1,0:T(1,128)S(1)}, u32[]{:S(2)}, u32[]{:S(2)}) async-start(f32[32,14,1,128]{3,2,1,0:T(1,128)} %shard_map.140), calls=%async_computation.1 | async-start | bytes 458752 | tf_op jit(solution)/shard_map/all_to_all | solution.py:727

commit v3 on v2

--- a/solution.py
+++ b/solution.py
@@ -136,38 +136,92 @@
     return jnp.where(iota(full.shape, 0) >= iota(full.shape, 1), full, 0.0)
 
 
-def coefs(first, last):
-    return list(range(4 * first, 4 * last + 4))
+def knots(first, last):
+    return list(range(first, last + 1))
 
 
 STAGES = (
-    ((coefs(0, 4), (0, 3)), (coefs(8, 13), (2, 8)), (coefs(17, 22), (7, 12)), (coefs(26, 31), (11, 15))),
-    ((coefs(5, 7), (0, 8)), (coefs(23, 25), (7, 15))),
-    ((coefs(14, 16), (0, 15)),),
+    ((knots(0, 4), (0, 3)), (knots(8, 13), (2, 8)), (knots(17, 22), (7, 12)), (knots(26, 31), (11, 15))),
+    ((knots(5, 7), (0, 8)), (knots(23, 25), (7, 15))),
+    ((knots(14, 16), (0, 15)),),
 )
 
 
+def block_rows(entry, lines):
+    scale = 1.0 / (entry[0, 0] * entry[1, 1] - entry[0, 1] * entry[0, 1])
+    low, mid, high = entry[0, 0] * scale, entry[0, 1] * scale, entry[1, 1] * scale
+    turned = {}
+    for column in (2, 3):
+        turned[0, column] = high * entry[0, column] - mid * entry[1, column]
+        turned[1, column] = low * entry[1, column] - mid * entry[0, column]
+    rest = {}
+    for row, column in ((2, 2), (2, 3), (3, 3)):
+        taken = entry[0, row] * turned[0, column] + entry[1, row] * turned[1, column]
+        rest[row, column] = entry[row, column] - taken
+    upper = [high * lines[0] - mid * lines[1], low * lines[1] - mid * lines[0]]
+    lower = [
+        lines[row] - (entry[0, row] * upper[0] + entry[1, row] * upper[1]) for row in (2, 3)
+    ]
+    scale = 1.0 / (rest[2, 2] * rest[3, 3] - rest[2, 3] * rest[2, 3])
+    third = (rest[3, 3] * scale) * lower[0] - (rest[2, 3] * scale) * lower[1]
+    fourth = (rest[2, 2] * scale) * lower[1] - (rest[2, 3] * scale) * lower[0]
+    return [
+        upper[0] - (turned[0, 2] * third + turned[0, 3] * fourth),
+        upper[1] - (turned[1, 2] * third + turned[1, 3] * fourth),
+        third,
+        fourth,
+    ]
+
+
 def spd_inverse(matrix, inverse_out):
+    shape = (8, WIDTH)
     tiles = [matrix[8 * tile : 8 * tile + 8] for tile in range(WIDTH // 8)]
-    lane = iota((8, WIDTH), 1)
-    lane_row = iota((1, WIDTH), 1)
-    row = iota((8, 1), 0)
+    lane, row = iota(shape, 1), iota(shape, 0)
     for stage in STAGES:
         for step in range(max(len(chain) for chain, reach in stage)):
             pivots = [(chain[step], reach) for chain, reach in stage if step < len(chain)]
             held = list(tiles)
-            for pivot, (low, high) in pivots:
-                at, sub = pivot // 8, pivot % 8
-                line = held[at][sub : sub + 1]
-                scale = 1.0 / line[:, pivot : pivot + 1]
-                line = jnp.where(lane_row == pivot, -1.0, line) * scale
+            for knot, (low, high) in pivots:
+                at, sub, first = knot // 2, 4 * (knot % 2), 4 * knot
+                inside = lane // 4 == knot
+                columns = {
+                    tile: [
+                        jnp.broadcast_to(held[tile][:, first + index : first + index + 1], shape)
+                        for index in range(4)
+                    ]
+                    for tile in range(low, high + 1)
+                }
+                entry = {
+                    (one, two): jnp.broadcast_to(
+                        columns[at][two][sub + one : sub + one + 1], shape
+                    )
+                    for one in range(4)
+                    for two in range(one, 4)
+                }
+                lines = [
+                    jnp.where(
+                        inside,
+                        jnp.where(lane == first + index, -1.0, 0.0),
+                        jnp.broadcast_to(held[at][sub + index : sub + index + 1], shape),
+                    )
+                    for index in range(4)
+                ]
+                lines = block_rows(entry, lines)
                 for tile in range(low, high + 1):
-                    column = held[tile][:, pivot : pivot + 1]
-                    drop = lane == pivot
+                    drop, factors = inside, columns[tile]
                     if tile == at:
-                        column = jnp.where(row == sub, -1.0, column)
-                        drop = drop | (iota((8, WIDTH), 0) == sub)
-                    tiles[tile] = jnp.where(drop, 0.0, tiles[tile]) - column * line
+                        drop = drop | (row // 4 == knot % 2)
+                        factors = [
+                            jnp.where(
+                                row // 4 == knot % 2,
+                                jnp.where(row == sub + index, -1.0, 0.0),
+                                factors[index],
+                            )
+                            for index in range(4)
+                        ]
+                    taken = factors[0] * lines[0] + factors[1] * lines[1]
+                    taken = taken + (factors[2] * lines[2] + factors[3] * lines[3])
+                    tiles[tile] = jnp.where(drop, 0.0, tiles[tile]) - taken
             yield
     for tile, value in enumerate(tiles):
         inverse_out[8 * tile : 8 * tile + 8] = -value
@@ -437,13 +491,33 @@
     )
 
 
-def pick_from(table_t, ids):
-    rows = ids.shape[0]
-    ids = flat(ids)
-    found = dot(jnp.concatenate(split3(table_t), axis=0), one_hot(ids // LANES, HIGH))
+def pick_from(table_t, ids, units, rows):
+    found = dot(jnp.concatenate(split3(table_t), axis=0), units)
     found = found[:LANES] + found[LANES : 2 * LANES] + found[2 * LANES :]
     hit = iota(found.shape, 0) == ids % LANES
     return unflat(jnp.sum(jnp.where(hit, found, 0.0), axis=0, keepdims=True), rows)
+
+
+def two_parts(line):
+    first = line.astype(BF16).astype(F32)
+    return first, (line - first).astype(BF16).astype(F32)
+
+
+def model_of(line, parts):
+    first, second = two_parts(line)
+    left = jnp.concatenate([first, first], axis=1)
+    right = jnp.concatenate([second, jnp.zeros_like(second)], axis=1)
+    row = iota((SUB, 2 * WIDTH), 0)
+    both = jnp.where(row == 0, left, jnp.where(row == 1, right, 0.0)).astype(BF16)
+    return jnp.sum(dot(both, parts), axis=0, keepdims=True)
+
+
+def side_of(values, parts):
+    first, second = two_parts(values)
+    row = iota((SUB, values.shape[1]), 0)
+    both = jnp.where(row == 0, first, jnp.where(row == 1, second, 0.0)).astype(BF16)
+    found = dot_t(both, parts)
+    return found[0:1, :WIDTH] + found[1:2, :WIDTH] + found[0:1, WIDTH:]
 
 
 def normals_kernel(
@@ -497,8 +571,8 @@
 
 
 def sources_kernel(
-    observed, source_partials, source_id, cal_id, weighted, calibration,
-    partials_out, factor_out, target_out, table_out, table, sem,
+    observed, source_partials, source_id, cal_id, weighted, design, calibration,
+    partials_out, factor_out, target_out, table_out, hits_out, units_out, parts_out, table, sem,
 ):
     copy = pltpu.make_async_copy(calibration, table, sem)
     copy.start()
@@ -513,8 +587,14 @@
         products = jnp.concatenate(
             [partials * (weighted[at] * partials[index : index + 1]) for index in range(5)], axis=0
         )
-        found = dot_t(jnp.concatenate(split3(products), axis=0), one_hot(source_id[at], SRC_DEV))
+        hits_out[row] = one_hot(source_id[at], SRC_DEV)
+        found = dot_t(jnp.concatenate(split3(products), axis=0), hits_out[row])
         matrix = matrix + found[:40] + found[40:80] + found[80:]
+        first, second, unused = split3(design[row])
+        parts_out[row, :WIDTH] = first
+        parts_out[row, WIDTH:] = second
+    ids = flat(cal_id[...])
+    units_out[...] = one_hot(ids // LANES, HIGH)
     inverse = small_factor(matrix)
     for place, pair in enumerate(PLACES):
         factor_out[place : place + 1] = inverse[pair]
@@ -522,14 +602,13 @@
     copy.wait()
     table_t = table[...].T
     table_out[...] = table_t
-    for row, picked in enumerate(pick_from(table_t, cal_id[...])):
+    for row, picked in enumerate(pick_from(table_t, ids, units_out[...], rows)):
         target_out[row : row + 1] = observed[row : row + 1] - picked
 
 
-def residual_step(targets, design, partials, factor, weighted, source_id, send_out):
+def residual_step(targets, parts, partials, factor, weighted, hits, send_out):
     rows, slots = len(targets), targets[0].shape[1]
     count = rows * slots // LANES
-    hits = [one_hot(source_id[row : row + 1], SRC_DEV) for row in range(rows)]
     inverse = {pair: factor[place : place + 1] for place, pair in enumerate(PLACES)}
     sides = jnp.zeros((SUB, SRC_DEV), F32)
     for row in range(rows):
@@ -538,29 +617,30 @@
         sides = sides + found[:SUB] + found[SUB : 2 * SUB] + found[2 * SUB :]
     params = small_apply(inverse, [sides[index : index + 1] for index in range(5)])
     table = jnp.concatenate(params + [jnp.zeros((3, SRC_DEV), F32)], axis=0)
-    parts = jnp.concatenate(split3(table), axis=0)
+    split = jnp.concatenate(split3(table), axis=0)
     explained = []
     for row in range(rows):
-        found = dot(parts, hits[row])
+        found = dot(split, hits[row])
         found = found[:SUB] + found[SUB : 2 * SUB] + found[2 * SUB :]
         explained.append(jnp.sum(found * partials[row], axis=0, keepdims=True))
+    for row in range(rows):
         scaled = weighted[row : row + 1] * (targets[row] - explained[row])
+        right = side_of(scaled, parts[row])
         for place in range(slots // LANES):
             for device in range(send_out.shape[0]):
                 send_out[device, place * rows + row] = scaled[:, place * LANES : (place + 1) * LANES]
-        right = exact_dot_t(scaled, design[row])
         for device in range(send_out.shape[0]):
             send_out[device, count + row] = right
     return params, explained
 
 
-def first_kernel(received, target, design, partials, factor, weighted, source_id, send_out):
-    rows = design.shape[0]
+def first_kernel(received, target, parts, partials, factor, weighted, hits, send_out):
+    rows = parts.shape[0]
     last = received.shape[1] - 1
     targets = [
-        target[row : row + 1] - exact_dot(received[row, last], design[row]) for row in range(rows)
+        target[row : row + 1] - model_of(received[row, last], parts[row]) for row in range(rows)
     ]
-    residual_step(targets, design, partials, factor, weighted, source_id, send_out)
+    residual_step(targets, parts, partials, factor, weighted, hits, send_out)
     for place in range(PIECE):
         total = received[0, place]
         for device in range(1, received.shape[0]):
@@ -641,36 +721,37 @@
 
 
 def second_kernel(
-    values, received, table, scale, cal_id, observed, design, partials, factor, weighted, source_id,
+    values, received, table, scale, cal_id, units, observed, parts, partials, factor, weighted, hits,
     send_out, params_out, explained_out, table_out, attitude_out, inverses_out, bands,
 ):
-    rows = design.shape[0]
+    rows = parts.shape[0]
     count = values.shape[1] - rows - PIECE
     for device in range(values.shape[0]):
         for place in range(PIECE):
             at = PIECE * device + place
             bands[at : at + 1] = values[device, count + rows + place]
+    models = [None] * rows
+
+    def attitude(row):
+        yield from spd_inverse(
+            matrix_of(bands[BAND * row : BAND * (row + 1)]), inverses_out.at[row]
+        )
+        change = exact_dot(right_side(values, count + row), inverses_out[row])
+        yield
+        new = received[row, received.shape[1] - 1] + change
+        attitude_out[row : row + 1] = new
+        models[row] = model_of(new, parts[row])
+        yield
+
     together(
         [unit_sums(received, lambda device, index: values[device, index], table_out)]
-        + [
-            spd_inverse(
-                matrix_of(bands[BAND * row : BAND * (row + 1)]), inverses_out.at[row]
-            )
-            for row in range(rows)
-        ]
+        + [attitude(row) for row in range(rows)]
     )
     table_t = table[...] + table_out[...] * scale[...]
     table_out[...] = table_t
-    targets = []
-    for row, picked in enumerate(pick_from(table_t, cal_id[...])):
-        new = received[row, received.shape[1] - 1] + exact_dot(
-            right_side(values, count + row), inverses_out[row]
-        )
-        attitude_out[row : row + 1] = new
-        targets.append(observed[row : row + 1] - exact_dot(new, design[row]) - picked)
-    params, explained = residual_step(
-        targets, design, partials, factor, weighted, source_id, send_out
-    )
+    picked = pick_from(table_t, flat(cal_id[...]), units[...], rows)
+    targets = [observed[row : row + 1] - models[row] - picked[row] for row in range(rows)]
+    params, explained = residual_step(targets, parts, partials, factor, weighted, hits, send_out)
     for index in range(5):
         params_out[index : index + 1] = params[index]
     for row in range(rows):
@@ -678,22 +759,32 @@
 
 
 def final_kernel(
-    axis, values, received, inverses, attitude, table, scale, cal_id, observed, design, explained,
-    cal_out, attitude_out, resid_out, sums,
+    axis, values, received, inverses, attitude, table, scale, cal_id, units, observed, parts,
+    explained, cal_out, attitude_out, resid_out, sums,
 ):
-    rows = design.shape[0]
+    rows = parts.shape[0]
     count = values.shape[1] - rows
     me = lax.axis_index(axis)
-    models = []
-    for row in range(rows):
-        new = attitude[row : row + 1] + exact_dot(right_side(values, count + row), inverses[row])
-        models.append(exact_dot(new, design[row]))
-        own = new if row == 0 else jnp.where(me == row, new, own)
+    models, news = [None] * rows, [None] * rows
+
+    def solve(row):
+        change = exact_dot(right_side(values, count + row), inverses[row])
+        yield
+        news[row] = attitude[row : row + 1] + change
+        models[row] = model_of(news[row], parts[row])
+        yield
+
+    together(
+        [unit_sums(received, lambda device, index: values[device, index], sums)]
+        + [solve(row) for row in range(rows)]
+    )
+    own = news[0]
+    for row in range(1, rows):
+        own = jnp.where(me == row, news[row], own)
     attitude_out[...] = own
-    together([unit_sums(received, lambda device, index: values[device, index], sums)])
     table_t = table[...] + sums[...] * scale[...]
     cal_out[...] = table_t.T
-    for row, picked in enumerate(pick_from(table_t, cal_id[...])):
+    for row, picked in enumerate(pick_from(table_t, flat(cal_id[...]), units[...], rows)):
         at = slice(row, row + 1)
         resid_out[at] = observed[at] - models[row] - picked - explained[at]
 
@@ -750,17 +841,21 @@
         + [pltpu.VMEM((rows, SUB, slots), F32), pltpu.SemaphoreType.DMA((10,))],
     )
     received = exchange(received)
-    partials, factor, target, table = call(
+    partials, factor, target, table, hits, units, parts = call(
         sources_kernel,
-        [stay(rows, SUB, slots), stay(16, SRC_DEV), stay(rows, slots), stay(LANES, HIGH)],
-        seen, source_partials, source_id, cal_id, weighted, calibration.reshape(HIGH, LANES),
+        [
+            stay(rows, SUB, slots), stay(16, SRC_DEV), stay(rows, slots), stay(LANES, HIGH),
+            stay(rows, SRC_DEV, slots, dtype=BF16), stay(HIGH, rows * slots, dtype=BF16),
+            stay(rows, 2 * WIDTH, slots, dtype=BF16),
+        ],
+        seen, source_partials, source_id, cal_id, weighted, design, calibration.reshape(HIGH, LANES),
         away=1,
         scratch=[pltpu.VMEM((HIGH, LANES), F32), pltpu.SemaphoreType.DMA],
     )
     received, factor = lax.optimization_barrier((received, factor))
     (values,) = call(
         first_kernel, [leave(devices, count + rows + PIECE, 1, LANES)],
-        received, target, design, partials, factor, weighted, source_id,
+        received, target, parts, partials, factor, weighted, hits,
     )
     values, received = lax.optimization_barrier((values, received))
     values = exchange(values)
@@ -771,14 +866,14 @@
             leave(devices, count + rows, 1, LANES), leave(5, SRC_DEV), stay(rows, slots),
             stay(LANES, HIGH), stay(rows, WIDTH), stay(rows, WIDTH, WIDTH),
         ],
-        values, received, table, scale, cal_id, seen, design, partials, factor, weighted, source_id,
+        values, received, table, scale, cal_id, units, seen, parts, partials, factor, weighted, hits,
         scratch=[pltpu.VMEM((rows * BAND, WIDTH), F32)],
     )
     values = exchange(values)
     cal, now, final = call(
         functools.partial(final_kernel, "tm"),
         [leave(HIGH, LANES), leave(1, WIDTH), leave(rows, slots)],
-        values, received, inverses, now, table, scale, cal_id, seen, design, explained,
+        values, received, inverses, now, table, scale, cal_id, units, seen, parts, explained,
         scratch=[pltpu.VMEM((LANES, HIGH), F32)],
     )
     return (params, now.reshape(WIDTH), cal.reshape(CAL), final)

time: 64.8 us -> 65.5 us (1.011)
  Pallas kernels: 27.1 us -> 28.1 us
    pallas_call x6, Pallas kernels: 27.1 us -> 28.1 us  [call(): pl.pallas_call(kernel, out_shape=outs, in_specs=[VMEM] * len(near) + [ANY...]
  transfers between devices with their start and end apart: 2 -> 2, of which waited for: 2 -> 2; matrix products, arithmetic and copies ran while one was open for 0% -> 0% of each run, Pallas kernels for 9% -> 10%
where the time goes in v3:
time: 65.5 us; the launch traced here: 65.2 us
  Pallas kernels  28.1 us (43%)
  waiting for transfers between devices  14.2 us (22%)
  blocking collectives  11.6 us (18%)
  starting transfers between devices  10.6 us (16%)
  between operations  0.68 us (1%)
    pallas_call x6, Pallas kernels, call(): pl.pallas_call(kernel, out_shape=outs, in_specs=[VMEM] * len(near) + [ANY...  28.1 us
    all_to_all x2, waiting for transfers between devices, exchange(): return lax.all_to_all(value, ('src', 'tm'), 0, 0, tiled=True)  14.2 us
    all_to_all x1, blocking collectives, exchange(): return lax.all_to_all(value, ('src', 'tm'), 0, 0, tiled=True)  11.6 us
    all_to_all x2, starting transfers between devices, exchange(): return lax.all_to_all(value, ('src', 'tm'), 0, 0, tiled=True)  10.6 us
  transfers between devices with their start and end apart: 2, of which 2 were waited for; matrix products, arithmetic and copies ran while one was open for 0% of the time, Pallas kernels for 10%

profile of v3, /device:TPU:0, one launch (start us, length us, event | category | flops | bytes accessed | tf_op | source)
XLA Modules:
  0.0 65.2 jit_solution(68497099346581605)
XLA Ops:
  0.6 2.5 %shard_map.138 = (f32[32,19,1,128]{3,2,1,0:T(1,128)}, f32[4,128,256]{2,1,0:T(8,128)S(1)}, f32[4,256]{1,0:T(4,128)S(1)}, f32[4,256]{1,0:T(4,128)S(1)}, s32[4,256]...) custom-call(f32[4,256]{1,0:T(4,128)} %observed_in.1, f32[4,256]{1,0:T(4,128)} %weight_in.1, ...), custom_call_target="tpu_custom_call" | custom-call | tf_op jit(solution)/shard_map/pallas_call | solution.py:799
  3.2 7.3 %all-to-all-start = ((f32[32,19,1,128]{3,2,1,0:T(1,128)}), f32[32,19,1,128]{3,2,1,0:T(1,128)S(1)}, u32[]{:S(2)}, u32[]{:S(2)}) async-start(f32[32,19,1,128]{3,2,1,0:T(1,128)} %get-tuple-element.31), calls=%async_computation | async-start | bytes 622592 | tf_op jit(solution)/shard_map/all_to_all | solution.py:818
  10.5 1.7 %shard_map.139 = (f32[4,8,256]{2,1,0:T(8,128)S(1)}, f32[16,128]{1,0:T(8,128)S(1)}, f32[4,256]{1,0:T(4,128)S(1)}, f32[128,256]{1,0:T(8,128)S(1)}, bf16[4,128,256]...) custom-call(f32[4,256]{1,0:T(4,128)S(1)} %get-tuple-element.32.observed, ...), custom_call_target="tpu_custom_call" | custom-call | tf_op jit(solution)/shard_map/pallas_call | solution.py:799
  12.2 9.1 %all-to-all-done.received = f32[32,19,1,128]{3,2,1,0:T(1,128)S(1)} async-done(((f32[32,19,1,128]{3,2,1,0:T(1,128)}), f32[32,19,1,128]{3,2,1,0:T(1,128)S(1)}, u32[]{:S(2)}, u32[]{:S(2)}) %all-to-all-start) | async-done | bytes 311328 | tf_op jit(solution)/shard_map/all_to_all | solution.py:818
  21.3 1.4 %shard_map.140 = f32[32,14,1,128]{3,2,1,0:T(1,128)} custom-call(f32[32,19,1,128]{3,2,1,0:T(1,128)S(1)} %all-to-all-done.received, f32[4,256]{1,0:T(4,128)S(1)} %get-tuple-element.40.target, bf16[4,256,256]{2,1,0:T(8,128)(2,1)S(1)} %get-tuple-element.41.parts, f32[4,8,256]{2,1,0:T(8,128)S(1)} %get-tuple-element.42.partials, ...), custom_call_target="tpu_custom_call" | custom-call | tf_op jit(solution)/shard_map/pallas_call | solution.py:799
  22.7 3.3 %all-to-all-start.1 = ((f32[32,14,1,128]{3,2,1,0:T(1,128)}), f32[32,14,1,128]{3,2,1,0:T(1,128)S(1)}, u32[]{:S(2)}, u32[]{:S(2)}) async-start(f32[32,14,1,128]{3,2,1,0:T(1,128)} %shard_map.140), calls=%async_computation.1 | async-start | bytes 458752 | tf_op jit(solution)/shard_map/all_to_all | solution.py:818
  26.1 4.5 %shard_map.141.scale = f32[128,256]{1,0:T(8,128)S(1)} custom-call(f32[32,19,1,128]{3,2,1,0:T(1,128)S(1)} %all-to-all-done.received), custom_call_target="tpu_custom_call" | custom-call | tf_op jit(solution)/shard_map/pallas_call | solution.py:799
  30.6 5.1 %all-to-all-done.1.values = f32[32,14,1,128]{3,2,1,0:T(1,128)S(1)} async-done(((f32[32,14,1,128]{3,2,1,0:T(1,128)}), f32[32,14,1,128]{3,2,1,0:T(1,128)S(1)}, u32[]{:S(2)}, u32[]{:S(2)}) %all-to-all-start.1) | async-done | bytes 229408 | tf_op jit(solution)/shard_map/all_to_all | solution.py:818
  35.7 11.8 %shard_map.142 = (f32[32,12,1,128]{3,2,1,0:T(1,128)S(1)}, f32[5,128]{1,0:T(8,128)}, f32[4,256]{1,0:T(4,128)S(1)}, f32[128,256]{1,0:T(8,128)S(1)}, f32[4,128]{1,0:T(4,128)S(1)}, /*index=5*/f32[4,128,128]{2,1,0:T(8,128)S(1)}) custom-call(f32[32,14,1,128]{3,2,1,0:T(1,128)S(1)} %all-to-all-done.1.values, f32[32,19,1,128]{3,2,1,0:T(1,128)S(1)} %all-to-all-done.received, ...), custom_call_target="tpu_custom_call" | custom-call | tf_op jit(solution)/shard_map/pallas_call | solution.py:799
  47.4 11.6 %all_to_all.15.values = f32[32,12,1,128]{3,2,1,0:T(1,128)S(1)} all-to-all(f32[32,12,1,128]{3,2,1,0:T(1,128)S(1)} %get-tuple-element.50), channel_id=1, replica_groups=mesh['src'=8,'tm'=4] {'src','tm'}, dimensions={0} | all-to-all | bytes 393216 | tf_op jit(solution)/shard_map/all_to_all | solution.py:818
  59.0 6.2 %shard_map.143 = (f32[256,128]{1,0:T(8,128)}, f32[1,128]{1,0:T(1,128)}, f32[4,256]{1,0:T(4,128)}) custom-call(f32[32,12,1,128]{3,2,1,0:T(1,128)S(1)} %all_to_all.15.values, f32[32,19,1,128]{3,2,1,0:T(1,128)S(1)} %all-to-all-done.received, f32[4,128,128]{2,1,0:T(8,128)S(1)} %get-tuple-element.51.inverses, f32[4,128]{1,0:T(4,128)S(1)} %get-tuple-element.52.attitude, ...), custom_call_target="tpu_custom_call" | custom-call | tf_op jit(solution)/shard_map/pallas_call | solution.py:799
Async XLA Ops:
  3.2 18.1 %all-to-all-start = ((f32[32,19,1,128]{3,2,1,0:T(1,128)}), f32[32,19,1,128]{3,2,1,0:T(1,128)S(1)}, u32[]{:S(2)}, u32[]{:S(2)}) async-start(f32[32,19,1,128]{3,2,1,0:T(1,128)} %get-tuple-element.31), calls=%async_computation | async-start | bytes 622592 | tf_op jit(solution)/shard_map/all_to_all | solution.py:818
  22.7 13.0 %all-to-all-start.1 = ((f32[32,14,1,128]{3,2,1,0:T(1,128)}), f32[32,14,1,128]{3,2,1,0:T(1,128)S(1)}, u32[]{:S(2)}, u32[]{:S(2)}) async-start(f32[32,14,1,128]{3,2,1,0:T(1,128)} %shard_map.140), calls=%async_computation.1 | async-start | bytes 458752 | tf_op jit(solution)/shard_map/all_to_all | solution.py:818

commit v4 on v3

--- a/solution.py
+++ b/solution.py
@@ -136,15 +136,28 @@
     return jnp.where(iota(full.shape, 0) >= iota(full.shape, 1), full, 0.0)
 
 
-def knots(first, last):
-    return list(range(first, last + 1))
-
-
-STAGES = (
-    ((knots(0, 4), (0, 3)), (knots(8, 13), (2, 8)), (knots(17, 22), (7, 12)), (knots(26, 31), (11, 15))),
-    ((knots(5, 7), (0, 8)), (knots(23, 25), (7, 15))),
-    ((knots(14, 16), (0, 15)),),
+ORDER = (
+    (0, 8, 17, 31), (1, 9, 18, 30), (2, 10, 19, 29), (3, 11, 20, 28), (4, 12, 21, 27), (13, 22, 26),
+    (5, 23), (6, 24), (7, 25), (14,), (15,), (16,),
 )
+
+
+def plan_of(order):
+    near = {
+        knot: {other for other in range(KNOTS_DEV) if 0 < abs(other - knot) <= 3}
+        for knot in range(KNOTS_DEV)
+    }
+    plan = []
+    for step in order:
+        plan.append([(knot, sorted({other // 2 for other in near[knot]})) for knot in step])
+        for knot in step:
+            assert not near[knot] & set(step)
+            for other in near[knot]:
+                near[other] = (near[other] | near[knot]) - {other, knot}
+    return plan
+
+
+PLAN = plan_of(ORDER)
 
 
 def block_rows(entry, lines):
@@ -173,58 +186,65 @@
     ]
 
 
-def spd_inverse(matrix, inverse_out):
+def eliminate(matrix, right, lines_out):
     shape = (8, WIDTH)
     tiles = [matrix[8 * tile : 8 * tile + 8] for tile in range(WIDTH // 8)]
-    lane, row = iota(shape, 1), iota(shape, 0)
-    for stage in STAGES:
-        for step in range(max(len(chain) for chain, reach in stage)):
-            pivots = [(chain[step], reach) for chain, reach in stage if step < len(chain)]
-            held = list(tiles)
-            for knot, (low, high) in pivots:
-                at, sub, first = knot // 2, 4 * (knot % 2), 4 * knot
-                inside = lane // 4 == knot
-                columns = {
-                    tile: [
-                        jnp.broadcast_to(held[tile][:, first + index : first + index + 1], shape)
-                        for index in range(4)
-                    ]
-                    for tile in range(low, high + 1)
-                }
-                entry = {
-                    (one, two): jnp.broadcast_to(
-                        columns[at][two][sub + one : sub + one + 1], shape
-                    )
-                    for one in range(4)
-                    for two in range(one, 4)
-                }
-                lines = [
-                    jnp.where(
-                        inside,
-                        jnp.where(lane == first + index, -1.0, 0.0),
-                        jnp.broadcast_to(held[at][sub + index : sub + index + 1], shape),
-                    )
+    lane = iota(shape, 1)
+    for step in PLAN:
+        held = list(tiles)
+        border = right
+        for knot, reach in step:
+            at, sub, first = knot // 2, 4 * (knot % 2), 4 * knot
+            inside = lane // 4 == knot
+            columns = {
+                tile: [
+                    jnp.broadcast_to(held[tile][:, first + index : first + index + 1], shape)
                     for index in range(4)
                 ]
-                lines = block_rows(entry, lines)
-                for tile in range(low, high + 1):
-                    drop, factors = inside, columns[tile]
-                    if tile == at:
-                        drop = drop | (row // 4 == knot % 2)
-                        factors = [
-                            jnp.where(
-                                row // 4 == knot % 2,
-                                jnp.where(row == sub + index, -1.0, 0.0),
-                                factors[index],
-                            )
-                            for index in range(4)
-                        ]
-                    taken = factors[0] * lines[0] + factors[1] * lines[1]
-                    taken = taken + (factors[2] * lines[2] + factors[3] * lines[3])
-                    tiles[tile] = jnp.where(drop, 0.0, tiles[tile]) - taken
-            yield
-    for tile, value in enumerate(tiles):
-        inverse_out[8 * tile : 8 * tile + 8] = -value
+                for tile in sorted({at, *reach})
+            }
+            entry = {
+                (one, two): jnp.broadcast_to(columns[at][two][sub + one : sub + one + 1], shape)
+                for one in range(4)
+                for two in range(one, 4)
+            }
+            lines = [
+                jnp.where(
+                    inside,
+                    jnp.where(lane == first + index, -1.0, 0.0),
+                    jnp.broadcast_to(held[at][sub + index : sub + index + 1], shape),
+                )
+                for index in range(4)
+            ]
+            lines = block_rows(entry, lines)
+            for index in range(4):
+                lines_out[first + index : first + index + 1] = lines[index][0:1]
+            for tile in reach:
+                factors = columns[tile]
+                taken = factors[0] * lines[0] + factors[1] * lines[1]
+                taken = taken + (factors[2] * lines[2] + factors[3] * lines[3])
+                tiles[tile] = jnp.where(inside, 0.0, tiles[tile]) - taken
+            right = swept(right, border, knot, [line[0:1] for line in lines])
+        yield
+    return right
+
+
+def swept(right, border, knot, lines):
+    first = 4 * knot
+    right = jnp.where(iota(right.shape, 1) // 4 == knot, 0.0, right)
+    factors = [border[:, first + index : first + index + 1] for index in range(4)]
+    taken = factors[0] * lines[0] + factors[1] * lines[1]
+    return right - (taken + (factors[2] * lines[2] + factors[3] * lines[3]))
+
+
+def substitute(right, lines):
+    for step in PLAN:
+        border = right
+        for knot, unused in step:
+            kept = [lines[4 * knot + index : 4 * knot + index + 1] for index in range(4)]
+            right = swept(right, border, knot, kept)
+        yield
+    return right
 
 
 def small_factor(sums):
@@ -550,12 +570,11 @@
     first, second = tile_of(cal_id[...].astype(F32)), tile_of(weighted)
     count = first.shape[0]
     devices = send_out.shape[0]
-    for index in range(count):
-        for device in range(devices):
-            send_out[device, PIECE + index] = first[index : index + 1]
-            send_out[device, PIECE + count + index] = second[index : index + 1]
     for device in range(devices):
-        send_out[device, PIECE + 2 * count] = start[...]
+        part = second if device // rows % 2 else first
+        for index in range(count):
+            send_out[device, PIECE + index] = part[index : index + 1]
+        send_out[device, PIECE + count] = start[...]
     for row in range(rows):
         at = slice(row, row + 1)
         for channel in range(4):
@@ -654,15 +673,14 @@
     return jnp.concatenate([tile] * (count // 16), axis=0)
 
 
-def unit_sums(received, value_of, total):
-    count = (received.shape[1] - PIECE - 1) // 2
+def unit_sums(units, value_of, total):
     low_row = iota((LANES, LANES), 0).astype(F32).astype(BF16)
     high_row = iota((HIGH, LANES), 0).astype(F32).astype(BF16)
     one, none = jnp.ones((), BF16), jnp.zeros((), BF16)
-    for device in range(received.shape[0]):
+    for device in range(units.shape[0]):
         lefts, rights = [], []
-        for index in range(count):
-            unit = received[device, PIECE + index]
+        for index in range(units.shape[1]):
+            unit = units[device, index]
             high = jnp.floor(unit * (1.0 / LANES))
             hit = low_row == wide(unit - LANES * high, LANES)
             value = value_of(device, index)
@@ -699,17 +717,18 @@
                 works.remove(work)
 
 
-def scale_kernel(received, scale_out):
-    count = (received.shape[1] - PIECE - 1) // 2
-    together(
-        [
-            unit_sums(
-                received,
-                lambda device, index: received[device, PIECE + count + index],
-                scale_out,
+def scale_kernel(axis, received, other, units_out, scale_out):
+    first = lax.rem(lax.axis_index(axis), 2) == 0
+
+    def weight(device, index):
+        return jnp.where(first, other[device, PIECE + index], received[device, PIECE + index])
+
+    for device in range(received.shape[0]):
+        for index in range(units_out.shape[1]):
+            units_out[device, index] = jnp.where(
+                first, received[device, PIECE + index], other[device, PIECE + index]
             )
-        ]
-    )
+    together([unit_sums(units_out, weight, scale_out)])
     scale_out[...] = 1.0 / (scale_out[...] + 1.0)
 
 
@@ -721,8 +740,9 @@
 
 
 def second_kernel(
-    values, received, table, scale, cal_id, units, observed, parts, partials, factor, weighted, hits,
-    send_out, params_out, explained_out, table_out, attitude_out, inverses_out, bands,
+    values, received, owners, table, scale, cal_id, units, observed, parts, partials, factor, weighted,
+    hits,
+    send_out, params_out, explained_out, table_out, attitude_out, lines_out, bands,
 ):
     rows = parts.shape[0]
     count = values.shape[1] - rows - PIECE
@@ -733,19 +753,20 @@
     models = [None] * rows
 
     def attitude(row):
-        yield from spd_inverse(
-            matrix_of(bands[BAND * row : BAND * (row + 1)]), inverses_out.at[row]
-        )
-        change = exact_dot(right_side(values, count + row), inverses_out[row])
-        yield
+        matrix = matrix_of(bands[BAND * row : BAND * (row + 1)])
+        change = yield from eliminate(matrix, right_side(values, count + row), lines_out.at[row])
         new = received[row, received.shape[1] - 1] + change
         attitude_out[row : row + 1] = new
         models[row] = model_of(new, parts[row])
         yield
 
+    def attitudes(first):
+        for row in range(first, rows, 2):
+            yield from attitude(row)
+
     together(
-        [unit_sums(received, lambda device, index: values[device, index], table_out)]
-        + [attitude(row) for row in range(rows)]
+        [unit_sums(owners, lambda device, index: values[device, index], table_out)]
+        + [attitudes(first) for first in range(2)]
     )
     table_t = table[...] + table_out[...] * scale[...]
     table_out[...] = table_t
@@ -759,7 +780,7 @@
 
 
 def final_kernel(
-    axis, values, received, inverses, attitude, table, scale, cal_id, units, observed, parts,
+    axis, values, owners, lines, attitude, table, scale, cal_id, units, observed, parts,
     explained, cal_out, attitude_out, resid_out, sums,
 ):
     rows = parts.shape[0]
@@ -768,14 +789,13 @@
     models, news = [None] * rows, [None] * rows
 
     def solve(row):
-        change = exact_dot(right_side(values, count + row), inverses[row])
-        yield
+        change = yield from substitute(right_side(values, count + row), lines.at[row])
         news[row] = attitude[row : row + 1] + change
         models[row] = model_of(news[row], parts[row])
         yield
 
     together(
-        [unit_sums(received, lambda device, index: values[device, index], sums)]
+        [unit_sums(owners, lambda device, index: values[device, index], sums)]
         + [solve(row) for row in range(rows)]
     )
     own = news[0]
@@ -830,7 +850,7 @@
     received, design, weighted, seen, source_id, cal_id, source_partials = call(
         normals_kernel,
         [
-            leave(devices, PIECE + 2 * count + 1, 1, LANES), stay(rows, WIDTH, slots),
+            leave(devices, PIECE + count + 1, 1, LANES), stay(rows, WIDTH, slots),
             stay(rows, slots), stay(rows, slots), stay(rows, slots, dtype=jnp.int32),
             stay(rows, slots, dtype=jnp.int32), stay(*source_partials.shape),
         ],
@@ -859,21 +879,28 @@
     )
     values, received = lax.optimization_barrier((values, received))
     values = exchange(values)
-    (scale,) = call(scale_kernel, [stay(LANES, HIGH)], received)
-    values, params, explained, table, now, inverses = call(
+    sources = lax.axis_size("src")
+    other = lax.ppermute(received, "src", [(at, at ^ 1) for at in range(sources)])
+    owners, scale = call(
+        functools.partial(scale_kernel, "src"),
+        [stay(devices, count, 1, LANES), stay(LANES, HIGH)],
+        received, other,
+    )
+    values, params, explained, table, now, lines = call(
         second_kernel,
         [
             leave(devices, count + rows, 1, LANES), leave(5, SRC_DEV), stay(rows, slots),
             stay(LANES, HIGH), stay(rows, WIDTH), stay(rows, WIDTH, WIDTH),
         ],
-        values, received, table, scale, cal_id, units, seen, parts, partials, factor, weighted, hits,
+        values, received, owners, table, scale, cal_id, units, seen, parts, partials, factor, weighted,
+        hits,
         scratch=[pltpu.VMEM((rows * BAND, WIDTH), F32)],
     )
     values = exchange(values)
     cal, now, final = call(
         functools.partial(final_kernel, "tm"),
         [leave(HIGH, LANES), leave(1, WIDTH), leave(rows, slots)],
-        values, received, inverses, now, table, scale, cal_id, units, seen, parts, explained,
+        values, owners, lines, now, table, scale, cal_id, units, seen, parts, explained,
         scratch=[pltpu.VMEM((LANES, HIGH), F32)],
     )
     return (params, now.reshape(WIDTH), cal.reshape(CAL), final)

time: 65.5 us -> 60.5 us (0.924)
  Pallas kernels: 28.1 us -> 25.4 us
  waiting for transfers between devices: 14.2 us -> 12.4 us
    all_to_all x2, waiting for transfers between devices: 14.2 us -> 11 us  [exchange(): return lax.all_to_all(value, ('src', 'tm'), 0, 0, tiled=True)]
    pallas_call x6, Pallas kernels: 28.1 us -> 25.4 us  [call(): pl.pallas_call(kernel, out_shape=outs, in_specs=[VMEM] * len(near) + [ANY...]
    ppermute x0 -> x1, waiting for transfers between devices: none -> 1.4 us  [body(): lax.ppermute(received, 'src', [(at, at ^ 1) for at in range(sources)])]
  transfers between devices with their start and end apart: 2 -> 3, of which waited for: 2 -> 3; matrix products, arithmetic and copies ran while one was open for 0% -> 0% of each run, Pallas kernels for 10% -> 10%
where the time goes in v4:
time: 60.5 us; the launch traced here: 60.1 us
  Pallas kernels  25.4 us (42%)
  waiting for transfers between devices  12.4 us (20%)
  blocking collectives  11.5 us (19%)
  starting transfers between devices  10.1 us (17%)
  between operations  0.69 us (1%)
    pallas_call x6, Pallas kernels, call(): pl.pallas_call(kernel, out_shape=outs, in_specs=[VMEM] * len(near) + [ANY...  25.4 us
    all_to_all x1, blocking collectives, exchange(): return lax.all_to_all(value, ('src', 'tm'), 0, 0, tiled=True)  11.5 us
    all_to_all x2, waiting for transfers between devices, exchange(): return lax.all_to_all(value, ('src', 'tm'), 0, 0, tiled=True)  11 us
    all_to_all x2, starting transfers between devices, exchange(): return lax.all_to_all(value, ('src', 'tm'), 0, 0, tiled=True)  10.1 us
    ppermute x1, waiting for transfers between devices, body(): lax.ppermute(received, 'src', [(at, at ^ 1) for at in range(sources)])  1.4 us
  transfers between devices with their start and end apart: 3, of which 3 were waited for; matrix products, arithmetic and copies ran while one was open for 0% of the time, Pallas kernels for 10%

profile of v4, /device:TPU:0, one launch (start us, length us, event | category | flops | bytes accessed | tf_op | source)
XLA Modules:
  0.0 60.1 jit_solution(263539468743163993)
XLA Ops:
  0.6 2.5 %shard_map.138 = (f32[32,11,1,128]{3,2,1,0:T(1,128)}, f32[4,128,256]{2,1,0:T(8,128)S(1)}, f32[4,256]{1,0:T(4,128)S(1)}, f32[4,256]{1,0:T(4,128)S(1)}, s32[4,256]...) custom-call(f32[4,256]{1,0:T(4,128)} %observed_in.1, f32[4,256]{1,0:T(4,128)} %weight_in.1, ...), custom_call_target="tpu_custom_call" | custom-call | tf_op jit(solution)/shard_map/pallas_call | solution.py:819
  3.1 7.3 %all-to-all-start = ((f32[32,11,1,128]{3,2,1,0:T(1,128)}), f32[32,11,1,128]{3,2,1,0:T(1,128)S(1)}, u32[]{:S(2)}, u32[]{:S(2)}) async-start(f32[32,11,1,128]{3,2,1,0:T(1,128)} %get-tuple-element.33), calls=%async_computation | async-start | bytes 360448 | tf_op jit(solution)/shard_map/all_to_all | solution.py:838
  10.4 1.7 %shard_map.139 = (f32[4,8,256]{2,1,0:T(8,128)S(1)}, f32[16,128]{1,0:T(8,128)S(1)}, f32[4,256]{1,0:T(4,128)S(1)}, f32[128,256]{1,0:T(8,128)S(1)}, bf16[4,128,256]...) custom-call(f32[4,256]{1,0:T(4,128)S(1)} %get-tuple-element.34.observed, ...), custom_call_target="tpu_custom_call" | custom-call | tf_op jit(solution)/shard_map/pallas_call | solution.py:819
  12.1 7.4 %all-to-all-done.received = f32[32,11,1,128]{3,2,1,0:T(1,128)S(1)} async-done(((f32[32,11,1,128]{3,2,1,0:T(1,128)}), f32[32,11,1,128]{3,2,1,0:T(1,128)S(1)}, u32[]{:S(2)}, u32[]{:S(2)}) %all-to-all-start) | async-done | bytes 180256 | tf_op jit(solution)/shard_map/all_to_all | solution.py:838
  19.5 1.4 %shard_map.140 = f32[32,14,1,128]{3,2,1,0:T(1,128)} custom-call(f32[32,11,1,128]{3,2,1,0:T(1,128)S(1)} %all-to-all-done.received, f32[4,256]{1,0:T(4,128)S(1)} %get-tuple-element.42.target, bf16[4,256,256]{2,1,0:T(8,128)(2,1)S(1)} %get-tuple-element.43.parts, f32[4,8,256]{2,1,0:T(8,128)S(1)} %get-tuple-element.44.partials, ...), custom_call_target="tpu_custom_call" | custom-call | tf_op jit(solution)/shard_map/pallas_call | solution.py:819
  20.9 2.8 %all-to-all-start.1 = ((f32[32,14,1,128]{3,2,1,0:T(1,128)}), f32[32,14,1,128]{3,2,1,0:T(1,128)S(1)}, u32[]{:S(2)}, u32[]{:S(2)}) async-start(f32[32,14,1,128]{3,2,1,0:T(1,128)} %shard_map.140), calls=%async_computation.1 | async-start | bytes 458752 | tf_op jit(solution)/shard_map/all_to_all | solution.py:838
  23.7 0.1 collective-permute-start
  23.8 1.4 %collective-permute-done.other = f32[32,11,1,128]{3,2,1,0:T(1,128)S(1)} collective-permute-done((f32[32,11,1,128]{3,2,1,0:T(1,128)S(1)}, f32[32,11,1,128]{3,2,1,0:T(1,128)S(1)}, u32[]{:S(2)}, u32[]{:S(2)}) %collective-permute-start) | collective-permute-done | bytes 180256 | tf_op jit(solution)/shard_map/ppermute | solution.py:883
  25.2 4.5 %shard_map.141 = (f32[32,8,1,128]{3,2,1,0:T(1,128)S(1)}, f32[128,256]{1,0:T(8,128)S(1)}) custom-call(f32[32,11,1,128]{3,2,1,0:T(1,128)S(1)} %all-to-all-done.received, f32[32,11,1,128]{3,2,1,0:T(1,128)S(1)} %collective-permute-done.other), custom_call_target="tpu_custom_call" | custom-call | tf_op jit(solution)/shard_map/pallas_call | solution.py:819
  29.7 3.6 %all-to-all-done.1.values = f32[32,14,1,128]{3,2,1,0:T(1,128)S(1)} async-done(((f32[32,14,1,128]{3,2,1,0:T(1,128)}), f32[32,14,1,128]{3,2,1,0:T(1,128)S(1)}, u32[]{:S(2)}, u32[]{:S(2)}) %all-to-all-start.1) | async-done | bytes 229408 | tf_op jit(solution)/shard_map/all_to_all | solution.py:838
  33.3 9.3 %shard_map.142 = (f32[32,12,1,128]{3,2,1,0:T(1,128)S(1)}, f32[5,128]{1,0:T(8,128)}, f32[4,256]{1,0:T(4,128)S(1)}, f32[128,256]{1,0:T(8,128)S(1)}, f32[4,128]{1,0:T(4,128)S(1)}, /*index=5*/f32[4,128,128]{2,1,0:T(8,128)S(1)}) custom-call(f32[32,14,1,128]{3,2,1,0:T(1,128)S(1)} %all-to-all-done.1.values, f32[32,11,1,128]{3,2,1,0:T(1,128)S(1)} %all-to-all-done.received, ...), custom_call_target="tpu_custom_call" | custom-call | tf_op jit(solution)/shard_map/pallas_call | solution.py:819
  42.6 11.5 %all_to_all.15.values = f32[32,12,1,128]{3,2,1,0:T(1,128)S(1)} all-to-all(f32[32,12,1,128]{3,2,1,0:T(1,128)S(1)} %get-tuple-element.54), channel_id=1, replica_groups=mesh['src'=8,'tm'=4] {'src','tm'}, dimensions={0} | all-to-all | bytes 393216 | tf_op jit(solution)/shard_map/all_to_all | solution.py:838
  54.2 6.0 %shard_map.143 = (f32[256,128]{1,0:T(8,128)}, f32[1,128]{1,0:T(1,128)}, f32[4,256]{1,0:T(4,128)}) custom-call(f32[32,12,1,128]{3,2,1,0:T(1,128)S(1)} %all_to_all.15.values, f32[32,8,1,128]{3,2,1,0:T(1,128)S(1)} %get-tuple-element.49.owners, f32[4,128,128]{2,1,0:T(8,128)S(1)} %get-tuple-element.55.lines, f32[4,128]{1,0:T(4,128)S(1)} %get-tuple-element.56.attitude, ...), custom_call_target="tpu_custom_call" | custom-call | tf_op jit(solution)/shard_map/pallas_call | solution.py:819
Async XLA Ops:
  3.1 16.4 %all-to-all-start = ((f32[32,11,1,128]{3,2,1,0:T(1,128)}), f32[32,11,1,128]{3,2,1,0:T(1,128)S(1)}, u32[]{:S(2)}, u32[]{:S(2)}) async-start(f32[32,11,1,128]{3,2,1,0:T(1,128)} %get-tuple-element.33), calls=%async_computation | async-start | bytes 360448 | tf_op jit(solution)/shard_map/all_to_all | solution.py:838
  20.9 12.4 %all-to-all-start.1 = ((f32[32,14,1,128]{3,2,1,0:T(1,128)}), f32[32,14,1,128]{3,2,1,0:T(1,128)S(1)}, u32[]{:S(2)}, u32[]{:S(2)}) async-start(f32[32,14,1,128]{3,2,1,0:T(1,128)} %shard_map.140), calls=%async_computation.1 | async-start | bytes 458752 | tf_op jit(solution)/shard_map/all_to_all | solution.py:838
  23.7 1.5 %collective-permute-start = (f32[32,11,1,128]{3,2,1,0:T(1,128)S(1)}, f32[32,11,1,128]{3,2,1,0:T(1,128)S(1)}, u32[]{:S(2)}, u32[]{:S(2)}) collective-permute-start(f32[32,11,1,128]{3,2,1,0:T(1,128)S(1)} %all-to-all-done.received), channel_id=1, source_target_pairs={{0,4},{4,0},{8,12},{12,8},{16,20},{20,16},{24,28},{28,24},{1,5},{5... | collective-permute-start | bytes 540680 | tf_op jit(solution)/shard_map/ppermute | solution.py:883

commit v5 on v4

--- a/solution.py
+++ b/solution.py
@@ -492,6 +492,7 @@
 
 BAND = 16
 PIECE = 2
+EARLY = 22
 
 
 def fetch(pairs, sems):
@@ -571,7 +572,7 @@
     count = first.shape[0]
     devices = send_out.shape[0]
     for device in range(devices):
-        part = second if device // rows % 2 else first
+        part = second if core_of(device, rows) else first
         for index in range(count):
             send_out[device, PIECE + index] = part[index : index + 1]
         send_out[device, PIECE + count] = start[...]
@@ -584,9 +585,9 @@
         design = design_of(knot_base[at], [part[at] for part in basis], stacked[row])
         design_out[row] = design
         band = pack_band(exact_dot_t(design * weighted[at], design))
+        half, place = divmod(row, rows // PIECE)
         for index in range(BAND):
-            device, place = divmod(row * BAND + index, PIECE)
-            send_out[device, place] = band[index : index + 1]
+            send_out[place * BAND + index, half] = band[index : index + 1]
 
 
 def sources_kernel(
@@ -625,9 +626,12 @@
         target_out[row : row + 1] = observed[row : row + 1] - picked
 
 
-def residual_step(targets, parts, partials, factor, weighted, hits, send_out):
+def core_of(device, line):
+    return device // line % 2
+
+
+def residual_step(targets, parts, partials, factor, weighted, hits, send_out, shared):
     rows, slots = len(targets), targets[0].shape[1]
-    count = rows * slots // LANES
     inverse = {pair: factor[place : place + 1] for place, pair in enumerate(PLACES)}
     sides = jnp.zeros((SUB, SRC_DEV), F32)
     for row in range(rows):
@@ -637,19 +641,24 @@
     params = small_apply(inverse, [sides[index : index + 1] for index in range(5)])
     table = jnp.concatenate(params + [jnp.zeros((3, SRC_DEV), F32)], axis=0)
     split = jnp.concatenate(split3(table), axis=0)
-    explained = []
+    explained, scaled, rights = [], [], []
     for row in range(rows):
         found = dot(split, hits[row])
         found = found[:SUB] + found[SUB : 2 * SUB] + found[2 * SUB :]
         explained.append(jnp.sum(found * partials[row], axis=0, keepdims=True))
     for row in range(rows):
-        scaled = weighted[row : row + 1] * (targets[row] - explained[row])
-        right = side_of(scaled, parts[row])
-        for place in range(slots // LANES):
-            for device in range(send_out.shape[0]):
-                send_out[device, place * rows + row] = scaled[:, place * LANES : (place + 1) * LANES]
-        for device in range(send_out.shape[0]):
-            send_out[device, count + row] = right
+        scaled.append(weighted[row : row + 1] * (targets[row] - explained[row]))
+        rights.append(side_of(scaled[row], parts[row]))
+    half = rows // PIECE
+    for device in range(send_out.shape[0]):
+        core = core_of(device, rows)
+        lines = [
+            scaled[row][:, place * LANES : (place + 1) * LANES]
+            for place in ((core,) if shared else range(slots // LANES))
+            for row in range(rows)
+        ]
+        for index, line in enumerate(lines + rights[half * core : half * core + half]):
+            send_out[device, index] = line
     return params, explained
 
 
@@ -659,13 +668,10 @@
     targets = [
         target[row : row + 1] - model_of(received[row, last], parts[row]) for row in range(rows)
     ]
-    residual_step(targets, parts, partials, factor, weighted, hits, send_out)
-    for place in range(PIECE):
-        total = received[0, place]
-        for device in range(1, received.shape[0]):
-            total = total + received[device, place]
-        for device in range(send_out.shape[0]):
-            send_out[device, send_out.shape[1] - PIECE + place] = total
+    residual_step(targets, parts, partials, factor, weighted, hits, send_out, False)
+    totals = [right_side(received, place) for place in range(PIECE)]
+    for device in range(send_out.shape[0]):
+        send_out[device, send_out.shape[1] - 1] = totals[core_of(device, rows)]
 
 
 def wide(row, count):
@@ -673,14 +679,14 @@
     return jnp.concatenate([tile] * (count // 16), axis=0)
 
 
-def unit_sums(units, value_of, total):
+def unit_sums(units, devices, lines, value_of, total):
     low_row = iota((LANES, LANES), 0).astype(F32).astype(BF16)
     high_row = iota((HIGH, LANES), 0).astype(F32).astype(BF16)
     one, none = jnp.ones((), BF16), jnp.zeros((), BF16)
-    for device in range(units.shape[0]):
+    for device in devices:
         lefts, rights = [], []
-        for index in range(units.shape[1]):
-            unit = units[device, index]
+        for index, at in enumerate(lines):
+            unit = units[device, at]
             high = jnp.floor(unit * (1.0 / LANES))
             hit = low_row == wide(unit - LANES * high, LANES)
             value = value_of(device, index)
@@ -696,10 +702,7 @@
             )
             rights.append(jnp.where(high_row == wide(high, HIGH), one, none))
         found = dot_t(jnp.concatenate(lefts, axis=1), jnp.concatenate(rights, axis=1))
-        if device == 0:
-            total[...] = found[:LANES] + found[LANES:]
-        else:
-            total[...] += found[:LANES] + found[LANES:]
+        total[...] += found[:LANES] + found[LANES:]
         yield
 
 
@@ -728,7 +731,9 @@
             units_out[device, index] = jnp.where(
                 first, received[device, PIECE + index], other[device, PIECE + index]
             )
-    together([unit_sums(units_out, weight, scale_out)])
+    scale_out[...] = jnp.zeros_like(scale_out)
+    devices, count = units_out.shape[:2]
+    together([unit_sums(units_out, range(devices), range(count), weight, scale_out)])
     scale_out[...] = 1.0 / (scale_out[...] + 1.0)
 
 
@@ -739,74 +744,139 @@
     return total
 
 
+def core(axis):
+    return lax.rem(lax.axis_index(axis), 2)
+
+
+def solve_kernel(axis, values, received, units, news_out, lines_out, sums_out, bands):
+    count = units.shape[1]
+    half = news_out.shape[0]
+    for device in range(values.shape[0]):
+        bands[device : device + 1] = values[device, count + half]
+
+    def attitude(place):
+        matrix = matrix_of(bands[BAND * place : BAND * (place + 1)])
+        change = yield from eliminate(matrix, right_side(values, count + place), lines_out.at[place])
+        news_out[place] = received[half * core(axis) + place, received.shape[1] - 1] + change
+        yield
+
+    sums_out[...] = jnp.zeros_like(sums_out)
+    together(
+        [
+            unit_sums(
+                units, range(EARLY), range(count), lambda device, index: values[device, index], sums_out
+            )
+        ]
+        + [attitude(place) for place in range(half)]
+    )
+
+
+def units_kernel(values, units, sums, table, scale, cal_id, hits, table_out, picked_out):
+    rows = cal_id.shape[0]
+    table_out[...] = sums[...]
+    devices, count = units.shape[:2]
+    together(
+        [
+            unit_sums(
+                units,
+                range(EARLY, devices),
+                range(count),
+                lambda device, index: values[device, index],
+                table_out,
+            )
+        ]
+    )
+    table_t = table[...] + table_out[...] * scale[...]
+    table_out[...] = table_t
+    for row, picked in enumerate(pick_from(table_t, flat(cal_id[...]), hits[...], rows)):
+        picked_out[row : row + 1] = picked
+
+
+def both_halves(axis, own, other):
+    half = own.shape[0]
+    first = core(axis) == 0
+    lines = [jnp.where(first, own[place], other[place]) for place in range(half)]
+    return lines + [jnp.where(first, other[place], own[place]) for place in range(half)]
+
+
 def second_kernel(
-    values, received, owners, table, scale, cal_id, units, observed, parts, partials, factor, weighted,
-    hits,
-    send_out, params_out, explained_out, table_out, attitude_out, lines_out, bands,
+    axis, news, other, picked, observed, parts, partials, factor, weighted, hits,
+    send_out, params_out, explained_out,
 ):
     rows = parts.shape[0]
-    count = values.shape[1] - rows - PIECE
-    for device in range(values.shape[0]):
-        for place in range(PIECE):
-            at = PIECE * device + place
-            bands[at : at + 1] = values[device, count + rows + place]
-    models = [None] * rows
-
-    def attitude(row):
-        matrix = matrix_of(bands[BAND * row : BAND * (row + 1)])
-        change = yield from eliminate(matrix, right_side(values, count + row), lines_out.at[row])
-        new = received[row, received.shape[1] - 1] + change
-        attitude_out[row : row + 1] = new
-        models[row] = model_of(new, parts[row])
-        yield
-
-    def attitudes(first):
-        for row in range(first, rows, 2):
-            yield from attitude(row)
-
-    together(
-        [unit_sums(owners, lambda device, index: values[device, index], table_out)]
-        + [attitudes(first) for first in range(2)]
-    )
-    table_t = table[...] + table_out[...] * scale[...]
-    table_out[...] = table_t
-    picked = pick_from(table_t, flat(cal_id[...]), units[...], rows)
-    targets = [observed[row : row + 1] - models[row] - picked[row] for row in range(rows)]
-    params, explained = residual_step(targets, parts, partials, factor, weighted, hits, send_out)
+    lines = both_halves(axis, news, other)
+    targets = [
+        observed[row : row + 1] - model_of(lines[row], parts[row]) - picked[row : row + 1]
+        for row in range(rows)
+    ]
+    params, explained = residual_step(
+        targets, parts, partials, factor, weighted, hits, send_out, True
+    )
     for index in range(5):
         params_out[index : index + 1] = params[index]
     for row in range(rows):
         explained_out[row : row + 1] = explained[row]
 
 
+def own_kernel(axis, values, units, lines, attitude, news_out, sums_out):
+    half = attitude.shape[0]
+    count = values.shape[1] - half
+
+    def solve(place):
+        change = yield from substitute(right_side(values, count + place), lines.at[place])
+        news_out[place] = attitude[place] + change
+        yield
+
+    sums_out[...] = jnp.zeros_like(sums_out)
+    together(
+        [
+            unit_sums(
+                units,
+                range(units.shape[0]),
+                [count * core(axis) + index for index in range(count)],
+                lambda device, index: values[device, index],
+                sums_out,
+            )
+        ]
+        + [solve(place) for place in range(half)]
+    )
+
+
+def other_kernel(
+    axis, values, units, sums, table, scale, cal_id, hits, cal_out, picked_out, total
+):
+    count = units.shape[1] // 2
+    total[...] = sums[...]
+    together(
+        [
+            unit_sums(
+                units,
+                range(units.shape[0]),
+                [count * (1 - core(axis)) + index for index in range(count)],
+                lambda device, index: values[device, index],
+                total,
+            )
+        ]
+    )
+    table_t = table[...] + total[...] * scale[...]
+    cal_out[...] = table_t.T
+    rows = cal_id.shape[0]
+    for row, picked in enumerate(pick_from(table_t, flat(cal_id[...]), hits[...], rows)):
+        picked_out[row : row + 1] = picked
+
+
 def final_kernel(
-    axis, values, owners, lines, attitude, table, scale, cal_id, units, observed, parts,
-    explained, cal_out, attitude_out, resid_out, sums,
+    axis, line, news, other, picked, observed, parts, explained, attitude_out, resid_out
 ):
-    rows = parts.shape[0]
-    count = values.shape[1] - rows
-    me = lax.axis_index(axis)
-    models, news = [None] * rows, [None] * rows
-
-    def solve(row):
-        change = yield from substitute(right_side(values, count + row), lines.at[row])
-        news[row] = attitude[row : row + 1] + change
-        models[row] = model_of(news[row], parts[row])
-        yield
-
-    together(
-        [unit_sums(owners, lambda device, index: values[device, index], sums)]
-        + [solve(row) for row in range(rows)]
-    )
-    own = news[0]
-    for row in range(1, rows):
-        own = jnp.where(me == row, news[row], own)
+    me = lax.axis_index(line)
+    lines = both_halves(axis, news, other)
+    own = lines[0]
+    for row in range(1, len(lines)):
+        own = jnp.where(me == row, lines[row], own)
     attitude_out[...] = own
-    table_t = table[...] + sums[...] * scale[...]
-    cal_out[...] = table_t.T
-    for row, picked in enumerate(pick_from(table_t, flat(cal_id[...]), units[...], rows)):
+    for row, new in enumerate(lines):
         at = slice(row, row + 1)
-        resid_out[at] = observed[at] - models[row] - picked - explained[at]
+        resid_out[at] = observed[at] - model_of(new, parts[row]) - picked[at] - explained[at]
 
 
 VMEM = pl.BlockSpec(memory_space=pltpu.VMEM)
@@ -834,6 +904,10 @@
     return jax.ShapeDtypeStruct(shape, F32)
 
 
+def swap(value):
+    return lax.ppermute(value, "src", [(at, at ^ 1) for at in range(lax.axis_size("src"))])
+
+
 def exchange(value):
     return lax.all_to_all(value, ("src", "tm"), 0, 0, tiled=True)
 
@@ -845,6 +919,7 @@
     rows, slots = observed.shape
     devices = lax.axis_size("src") * lax.axis_size("tm")
     count = rows * slots // LANES
+    half = rows // PIECE
     first_q = attitude.reshape(1, WIDTH)
     held = [weight_obs, present, attitude_partials, phase, knot_base, first_q]
     received, design, weighted, seen, source_id, cal_id, source_partials = call(
@@ -874,34 +949,51 @@
     )
     received, factor = lax.optimization_barrier((received, factor))
     (values,) = call(
-        first_kernel, [leave(devices, count + rows + PIECE, 1, LANES)],
+        first_kernel, [leave(devices, count + half + 1, 1, LANES)],
         received, target, parts, partials, factor, weighted, hits,
     )
     values, received = lax.optimization_barrier((values, received))
     values = exchange(values)
-    sources = lax.axis_size("src")
-    other = lax.ppermute(received, "src", [(at, at ^ 1) for at in range(sources)])
+    other = swap(received)
     owners, scale = call(
         functools.partial(scale_kernel, "src"),
         [stay(devices, count, 1, LANES), stay(LANES, HIGH)],
         received, other,
     )
-    values, params, explained, table, now, lines = call(
-        second_kernel,
-        [
-            leave(devices, count + rows, 1, LANES), leave(5, SRC_DEV), stay(rows, slots),
-            stay(LANES, HIGH), stay(rows, WIDTH), stay(rows, WIDTH, WIDTH),
-        ],
-        values, received, owners, table, scale, cal_id, units, seen, parts, partials, factor, weighted,
-        hits,
-        scratch=[pltpu.VMEM((rows * BAND, WIDTH), F32)],
+    news, lines, sums = call(
+        functools.partial(solve_kernel, "src"),
+        [leave(half, 1, WIDTH), stay(half, WIDTH, WIDTH), stay(LANES, HIGH)],
+        values, received, owners,
+        scratch=[pltpu.VMEM((half * BAND, WIDTH), F32)],
+    )
+    other = swap(news)
+    table, picked = call(
+        units_kernel, [stay(LANES, HIGH), stay(rows, slots)],
+        values, owners, sums, table, scale, cal_id, units,
+    )
+    values, params, explained = call(
+        functools.partial(second_kernel, "src"),
+        [leave(devices, rows + half, 1, LANES), leave(5, SRC_DEV), stay(rows, slots)],
+        news, other, picked, seen, parts, partials, factor, weighted, hits,
     )
     values = exchange(values)
-    cal, now, final = call(
-        functools.partial(final_kernel, "tm"),
-        [leave(HIGH, LANES), leave(1, WIDTH), leave(rows, slots)],
-        values, owners, lines, now, table, scale, cal_id, units, seen, parts, explained,
+    rest = swap(values)
+    news, sums = call(
+        functools.partial(own_kernel, "src"),
+        [leave(half, 1, WIDTH), stay(LANES, HIGH)],
+        values, owners, lines, news,
+    )
+    other = swap(news)
+    cal, picked = call(
+        functools.partial(other_kernel, "src"),
+        [leave(HIGH, LANES), stay(rows, slots)],
+        rest, owners, sums, table, scale, cal_id, units,
         scratch=[pltpu.VMEM((LANES, HIGH), F32)],
+    )
+    now, final = call(
+        functools.partial(final_kernel, "src", "tm"),
+        [leave(1, WIDTH), leave(rows, slots)],
+        news, other, picked, seen, parts, explained,
     )
     return (params, now.reshape(WIDTH), cal.reshape(CAL), final)
 

time: 60.5 us -> 58.5 us (0.967)
  Pallas kernels: 25.4 us -> 24.3 us
  blocking collectives: 11.5 us -> 10.7 us
    pallas_call x6 -> x10, Pallas kernels: 25.4 us -> 24.3 us  [call(): pl.pallas_call(kernel, out_shape=outs, in_specs=[VMEM] * len(near) + [ANY...]
    all_to_all x1, blocking collectives: 11.5 us -> 10.7 us  [exchange(): return lax.all_to_all(value, ('src', 'tm'), 0, 0, tiled=True)]
    ppermute x1 -> x4, starting transfers between devices: 0.07 us -> 0.82 us  [swap(): lax.ppermute(value, 'src', [(at, at ^ 1) for at in range(lax.axis_size('s...]
    ppermute x1 -> x4, waiting for transfers between devices: 1.4 us -> 1.31 us  [swap(): lax.ppermute(value, 'src', [(at, at ^ 1) for at in range(lax.axis_size('s...]
  transfers between devices with their start and end apart: 3 -> 6, of which waited for: 3 -> 3; matrix products, arithmetic and copies ran while one was open for 0% -> 0% of each run, Pallas kernels for 10% -> 25%
where the time goes in v5:
time: 58.5 us; the launch traced here: 58.2 us
  Pallas kernels  24.3 us (42%)
  waiting for transfers between devices  11.8 us (20%)
  starting transfers between devices  10.7 us (18%)
  blocking collectives  10.7 us (18%)
  between operations  0.71 us (1%)
    pallas_call x10, Pallas kernels, call(): pl.pallas_call(kernel, out_shape=outs, in_specs=[VMEM] * len(near) + [ANY...  24.3 us
    all_to_all x1, blocking collectives, exchange(): return lax.all_to_all(value, ('src', 'tm'), 0, 0, tiled=True)  10.7 us
    all_to_all x2, waiting for transfers between devices, exchange(): return lax.all_to_all(value, ('src', 'tm'), 0, 0, tiled=True)  10.5 us
    all_to_all x2, starting transfers between devices, exchange(): return lax.all_to_all(value, ('src', 'tm'), 0, 0, tiled=True)  9.88 us
    ppermute x4, waiting for transfers between devices, swap(): lax.ppermute(value, 'src', [(at, at ^ 1) for at in range(lax.axis_size('s...  1.31 us
  transfers between devices with their start and end apart: 6, of which 3 were waited for; matrix products, arithmetic and copies ran while one was open for 0% of the time, Pallas kernels for 25%

profile of v5, /device:TPU:0, one launch (start us, length us, event | category | flops | bytes accessed | tf_op | source)
XLA Modules:
  0.0 58.2 jit_solution(1406271662991857407)
XLA Ops:
  0.6 2.5 %shard_map.138 = (f32[32,11,1,128]{3,2,1,0:T(1,128)}, f32[4,128,256]{2,1,0:T(8,128)S(1)}, f32[4,256]{1,0:T(4,128)S(1)}, f32[4,256]{1,0:T(4,128)S(1)}, s32[4,256]...) custom-call(f32[4,256]{1,0:T(4,128)} %observed_in.1, f32[4,256]{1,0:T(4,128)} %weight_in.1, ...), custom_call_target="tpu_custom_call" | custom-call | tf_op jit(solution)/shard_map/pallas_call | solution.py:889
  3.1 7.3 %all-to-all-start = ((f32[32,11,1,128]{3,2,1,0:T(1,128)}), f32[32,11,1,128]{3,2,1,0:T(1,128)S(1)}, u32[]{:S(2)}, u32[]{:S(2)}) async-start(f32[32,11,1,128]{3,2,1,0:T(1,128)} %get-tuple-element.38), calls=%async_computation | async-start | bytes 360448 | tf_op jit(solution)/shard_map/all_to_all | solution.py:912
  10.4 1.7 %shard_map.139 = (f32[4,8,256]{2,1,0:T(8,128)S(1)}, f32[16,128]{1,0:T(8,128)S(1)}, f32[4,256]{1,0:T(4,128)S(1)}, f32[128,256]{1,0:T(8,128)S(1)}, bf16[4,128,256]...) custom-call(f32[4,256]{1,0:T(4,128)S(1)} %get-tuple-element.39.observed, ...), custom_call_target="tpu_custom_call" | custom-call | tf_op jit(solution)/shard_map/pallas_call | solution.py:889
  12.1 7.4 %all-to-all-done.received = f32[32,11,1,128]{3,2,1,0:T(1,128)S(1)} async-done(((f32[32,11,1,128]{3,2,1,0:T(1,128)}), f32[32,11,1,128]{3,2,1,0:T(1,128)S(1)}, u32[]{:S(2)}, u32[]{:S(2)}) %all-to-all-start) | async-done | bytes 180256 | tf_op jit(solution)/shard_map/all_to_all | solution.py:912
  19.5 1.4 %shard_map.140 = f32[32,11,1,128]{3,2,1,0:T(1,128)} custom-call(f32[32,11,1,128]{3,2,1,0:T(1,128)S(1)} %all-to-all-done.received, f32[4,256]{1,0:T(4,128)S(1)} %get-tuple-element.47.target, bf16[4,256,256]{2,1,0:T(8,128)(2,1)S(1)} %get-tuple-element.48.parts, f32[4,8,256]{2,1,0:T(8,128)S(1)} %get-tuple-element.49.partials, ...), custom_call_target="tpu_custom_call" | custom-call | tf_op jit(solution)/shard_map/pallas_call | solution.py:889
  20.9 2.6 %all-to-all-start.1 = ((f32[32,11,1,128]{3,2,1,0:T(1,128)}), f32[32,11,1,128]{3,2,1,0:T(1,128)S(1)}, u32[]{:S(2)}, u32[]{:S(2)}) async-start(f32[32,11,1,128]{3,2,1,0:T(1,128)} %shard_map.140), calls=%async_computation.1 | async-start | bytes 360448 | tf_op jit(solution)/shard_map/all_to_all | solution.py:912
  23.5 0.2 collective-permute-start
  23.7 1.3 %collective-permute-done.other = f32[32,11,1,128]{3,2,1,0:T(1,128)S(1)} collective-permute-done((f32[32,11,1,128]{3,2,1,0:T(1,128)S(1)}, f32[32,11,1,128]{3,2,1,0:T(1,128)S(1)}, u32[]{:S(2)}, u32[]{:S(2)}) %collective-permute-start) | collective-permute-done | bytes 180256 | tf_op jit(solution)/shard_map/ppermute | solution.py:908
  25.0 4.5 %shard_map.141 = (f32[32,8,1,128]{3,2,1,0:T(1,128)S(1)}, f32[128,256]{1,0:T(8,128)S(1)}) custom-call(f32[32,11,1,128]{3,2,1,0:T(1,128)S(1)} %all-to-all-done.received, f32[32,11,1,128]{3,2,1,0:T(1,128)S(1)} %collective-permute-done.other), custom_call_target="tpu_custom_call" | custom-call | tf_op jit(solution)/shard_map/pallas_call | solution.py:889
  29.6 3.1 %all-to-all-done.1.values = f32[32,11,1,128]{3,2,1,0:T(1,128)S(1)} async-done(((f32[32,11,1,128]{3,2,1,0:T(1,128)}), f32[32,11,1,128]{3,2,1,0:T(1,128)S(1)}, u32[]{:S(2)}, u32[]{:S(2)}) %all-to-all-start.1) | async-done | bytes 180256 | tf_op jit(solution)/shard_map/all_to_all | solution.py:912
  32.6 4.0 %shard_map.142 = (f32[2,1,128]{2,1,0:T(1,128)S(1)}, f32[2,128,128]{2,1,0:T(8,128)S(1)}, f32[128,256]{1,0:T(8,128)S(1)}) custom-call(f32[32,11,1,128]{3,2,1,0:T(1,128)S(1)} %all-to-all-done.1.values, f32[32,11,1,128]{3,2,1,0:T(1,128)S(1)} %all-to-all-done.received, f32[32,8,1,128]{3,2,1,0:T(1,128)S(1)} %get-tuple-element.54.units), custom_call_target="tpu_custom_call" | custom-call | tf_op jit(solution)/shard_map/pallas_call | solution.py:889
  36.6 0.1 collective-permute-start.1
  36.7 2.3 %shard_map.143 = (f32[128,256]{1,0:T(8,128)S(1)}, f32[4,256]{1,0:T(4,128)S(1)}) custom-call(f32[32,11,1,128]{3,2,1,0:T(1,128)S(1)} %all-to-all-done.1.values, f32[32,8,1,128]{3,2,1,0:T(1,128)S(1)} %get-tuple-element.54.units, f32[128,256]{1,0:T(8,128)S(1)} %get-tuple-element.56.sums, f32[128,256]{1,0:T(8,128)S(1)} %get-tuple-element.57.table, ...), custom_call_target="tpu_custom_call" | custom-call | tf_op jit(solution)/shard_map/pallas_call | solution.py:889
  39.0 0.0 collective-permute-done.1.other
  39.0 1.1 %shard_map.144 = (f32[32,6,1,128]{3,2,1,0:T(1,128)S(1)}, f32[5,128]{1,0:T(8,128)}, f32[4,256]{1,0:T(4,128)S(1)}) custom-call(f32[2,1,128]{2,1,0:T(1,128)S(1)} %get-tuple-element.55.news.attitude, f32[2,1,128]{2,1,0:T(1,128)S(1)} %collective-permute-done.1.other, f32[4,256]{1,0:T(4,128)S(1)} %get-tuple-element.60.picked, ...), custom_call_target="tpu_custom_call" | custom-call | tf_op jit(solution)/shard_map/pallas_call | solution.py:889
  40.1 10.7 %all_to_all.15.values = f32[32,6,1,128]{3,2,1,0:T(1,128)S(1)} all-to-all(f32[32,6,1,128]{3,2,1,0:T(1,128)S(1)} %get-tuple-element.62), channel_id=1, replica_groups=mesh['src'=8,'tm'=4] {'src','tm'}, dimensions={0} | all-to-all | bytes 196608 | tf_op jit(solution)/shard_map/all_to_all | solution.py:912
  50.8 0.0 collective-permute-start.3
  50.8 2.4 %shard_map.145 = (f32[2,1,128]{2,1,0:T(1,128)S(1)}, f32[128,256]{1,0:T(8,128)S(1)}) custom-call(f32[32,6,1,128]{3,2,1,0:T(1,128)S(1)} %all_to_all.15.values, f32[32,8,1,128]{3,2,1,0:T(1,128)S(1)} %get-tuple-element.54.units, f32[2,128,128]{2,1,0:T(8,128)S(1)} %get-tuple-element.63.lines, f32[2,1,128]{2,1,0:T(1,128)S(1)} %get-tuple-element.55.news.attitude), custom_call_target="tpu_custom_call" | custom-call | tf_op jit(solution)/shard_map/pallas_call | solution.py:889
  53.1 0.6 collective-permute-start.2
  53.7 0.0 collective-permute-done.3.values
  53.7 3.7 %shard_map.146 = (f32[256,128]{1,0:T(8,128)}, f32[4,256]{1,0:T(4,128)S(1)}) custom-call(f32[32,6,1,128]{3,2,1,0:T(1,128)S(1)} %collective-permute-done.3.values, f32[32,8,1,128]{3,2,1,0:T(1,128)S(1)} %get-tuple-element.54.units, f32[128,256]{1,0:T(8,128)S(1)} %get-tuple-element.65.sums, f32[128,256]{1,0:T(8,128)S(1)} %get-tuple-element.66.table, ...), custom_call_target="tpu_custom_call" | custom-call | tf_op jit(solution)/shard_map/pallas_call | solution.py:889
  57.4 0.0 collective-permute-done.2.other
  57.4 0.8 %shard_map.147 = (f32[1,128]{1,0:T(1,128)}, f32[4,256]{1,0:T(4,128)}) custom-call(f32[2,1,128]{2,1,0:T(1,128)S(1)} %get-tuple-element.64.news, f32[2,1,128]{2,1,0:T(1,128)S(1)} %collective-permute-done.2.other, f32[4,256]{1,0:T(4,128)S(1)} %get-tuple-element.67.picked, f32[4,256]{1,0:T(4,128)S(1)} %get-tuple-element.39.observed, ...), custom_call_target="tpu_custom_call" | custom-call | tf_op jit(solution)/shard_map/pallas_call | solution.py:889
Async XLA Ops:
  3.1 16.4 %all-to-all-start = ((f32[32,11,1,128]{3,2,1,0:T(1,128)}), f32[32,11,1,128]{3,2,1,0:T(1,128)S(1)}, u32[]{:S(2)}, u32[]{:S(2)}) async-start(f32[32,11,1,128]{3,2,1,0:T(1,128)} %get-tuple-element.38), calls=%async_computation | async-start | bytes 360448 | tf_op jit(solution)/shard_map/all_to_all | solution.py:912
  20.9 11.7 %all-to-all-start.1 = ((f32[32,11,1,128]{3,2,1,0:T(1,128)}), f32[32,11,1,128]{3,2,1,0:T(1,128)S(1)}, u32[]{:S(2)}, u32[]{:S(2)}) async-start(f32[32,11,1,128]{3,2,1,0:T(1,128)} %shard_map.140), calls=%async_computation.1 | async-start | bytes 360448 | tf_op jit(solution)/shard_map/all_to_all | solution.py:912
  23.5 1.5 %collective-permute-start = (f32[32,11,1,128]{3,2,1,0:T(1,128)S(1)}, f32[32,11,1,128]{3,2,1,0:T(1,128)S(1)}, u32[]{:S(2)}, u32[]{:S(2)}) collective-permute-start(f32[32,11,1,128]{3,2,1,0:T(1,128)S(1)} %all-to-all-done.received), channel_id=1, source_target_pairs={{0,4},{4,0},{8,12},{12,8},{16,20},{20,16},{24,28},{28,24},{1,5},{5... | collective-permute-start | bytes 540680 | tf_op jit(solution)/shard_map/ppermute | solution.py:908
  36.6 2.4 %collective-permute-start.1 = (f32[2,1,128]{2,1,0:T(1,128)S(1)}, f32[2,1,128]{2,1,0:T(1,128)S(1)}, u32[]{:S(2)}, u32[]{:S(2)}) collective-permute-start(f32[2,1,128]{2,1,0:T(1,128)S(1)} %get-tuple-element.55.news.attitude), channel_id=1, source_target_pairs={{0,4},{4,0},{8,12},{12,8},{16,20},{20,16},{24,28},{28,24},{1,5},{5... | collective-permute-start | bytes 3080 | tf_op jit(solution)/shard_map/ppermute | solution.py:908
  50.8 3.0 %collective-permute-start.3 = (f32[32,6,1,128]{3,2,1,0:T(1,128)S(1)}, f32[32,6,1,128]{3,2,1,0:T(1,128)S(1)}, u32[]{:S(2)}, u32[]{:S(2)}) collective-permute-start(f32[32,6,1,128]{3,2,1,0:T(1,128)S(1)} %all_to_all.15.values), channel_id=1, source_target_pairs={{0,4},{4,0},{8,12},{12,8},{16,20},{20,16},{24,28},{28,24},{1,5},{5... | collective-permute-start | bytes 294920 | tf_op jit(solution)/shard_map/ppermute | solution.py:908
  53.1 4.2 %collective-permute-start.2 = (f32[2,1,128]{2,1,0:T(1,128)S(1)}, f32[2,1,128]{2,1,0:T(1,128)S(1)}, u32[]{:S(2)}, u32[]{:S(2)}) collective-permute-start(f32[2,1,128]{2,1,0:T(1,128)S(1)} %get-tuple-element.64.news), channel_id=1, source_target_pairs={{0,4},{4,0},{8,12},{12,8},{16,20},{20,16},{24,28},{28,24},{1,5},{5... | collective-permute-start | bytes 3080 | tf_op jit(solution)/shard_map/ppermute | solution.py:908

commit v6 on v4

--- a/solution.py
+++ b/solution.py
@@ -568,13 +568,14 @@
         cube / 6.0,
     ]
     first, second = tile_of(cal_id[...].astype(F32)), tile_of(weighted)
-    count = first.shape[0]
     devices = send_out.shape[0]
     for device in range(devices):
-        part = second if device // rows % 2 else first
-        for index in range(count):
-            send_out[device, PIECE + index] = part[index : index + 1]
-        send_out[device, PIECE + count] = start[...]
+        core = core_of(device, rows)
+        for index in range(rows):
+            at = rows * core + index
+            send_out[device, PIECE + index] = first[at : at + 1]
+            send_out[device, PIECE + rows + index] = second[at : at + 1]
+        send_out[device, PIECE + 2 * rows] = start[...]
     for row in range(rows):
         at = slice(row, row + 1)
         for channel in range(4):
@@ -584,9 +585,9 @@
         design = design_of(knot_base[at], [part[at] for part in basis], stacked[row])
         design_out[row] = design
         band = pack_band(exact_dot_t(design * weighted[at], design))
+        half, place = divmod(row, rows // PIECE)
         for index in range(BAND):
-            device, place = divmod(row * BAND + index, PIECE)
-            send_out[device, place] = band[index : index + 1]
+            send_out[place * BAND + index, half] = band[index : index + 1]
 
 
 def sources_kernel(
@@ -625,9 +626,12 @@
         target_out[row : row + 1] = observed[row : row + 1] - picked
 
 
+def core_of(device, line):
+    return device // line % 2
+
+
 def residual_step(targets, parts, partials, factor, weighted, hits, send_out):
-    rows, slots = len(targets), targets[0].shape[1]
-    count = rows * slots // LANES
+    rows = len(targets)
     inverse = {pair: factor[place : place + 1] for place, pair in enumerate(PLACES)}
     sides = jnp.zeros((SUB, SRC_DEV), F32)
     for row in range(rows):
@@ -637,19 +641,20 @@
     params = small_apply(inverse, [sides[index : index + 1] for index in range(5)])
     table = jnp.concatenate(params + [jnp.zeros((3, SRC_DEV), F32)], axis=0)
     split = jnp.concatenate(split3(table), axis=0)
-    explained = []
+    explained, scaled, rights = [], [], []
     for row in range(rows):
         found = dot(split, hits[row])
         found = found[:SUB] + found[SUB : 2 * SUB] + found[2 * SUB :]
         explained.append(jnp.sum(found * partials[row], axis=0, keepdims=True))
     for row in range(rows):
-        scaled = weighted[row : row + 1] * (targets[row] - explained[row])
-        right = side_of(scaled, parts[row])
-        for place in range(slots // LANES):
-            for device in range(send_out.shape[0]):
-                send_out[device, place * rows + row] = scaled[:, place * LANES : (place + 1) * LANES]
-        for device in range(send_out.shape[0]):
-            send_out[device, count + row] = right
+        scaled.append(weighted[row : row + 1] * (targets[row] - explained[row]))
+        rights.append(side_of(scaled[row], parts[row]))
+    half = rows // PIECE
+    for device in range(send_out.shape[0]):
+        core = core_of(device, rows)
+        lines = [line[:, core * LANES : (core + 1) * LANES] for line in scaled]
+        for index, line in enumerate(lines + rights[half * core : half * core + half]):
+            send_out[device, index] = line
     return params, explained
 
 
@@ -660,12 +665,9 @@
         target[row : row + 1] - model_of(received[row, last], parts[row]) for row in range(rows)
     ]
     residual_step(targets, parts, partials, factor, weighted, hits, send_out)
-    for place in range(PIECE):
-        total = received[0, place]
-        for device in range(1, received.shape[0]):
-            total = total + received[device, place]
-        for device in range(send_out.shape[0]):
-            send_out[device, send_out.shape[1] - PIECE + place] = total
+    totals = [right_side(received, place) for place in range(PIECE)]
+    for device in range(send_out.shape[0]):
+        send_out[device, send_out.shape[1] - 1] = totals[core_of(device, rows)]
 
 
 def wide(row, count):
@@ -673,33 +675,35 @@
     return jnp.concatenate([tile] * (count // 16), axis=0)
 
 
-def unit_sums(units, value_of, total):
+def unit_sums(received, value_of, total):
+    rows = (received.shape[1] - PIECE - 1) // 2
     low_row = iota((LANES, LANES), 0).astype(F32).astype(BF16)
     high_row = iota((HIGH, LANES), 0).astype(F32).astype(BF16)
     one, none = jnp.ones((), BF16), jnp.zeros((), BF16)
-    for device in range(units.shape[0]):
+    for begin in range(0, received.shape[0], 2):
         lefts, rights = [], []
-        for index in range(units.shape[1]):
-            unit = units[device, index]
-            high = jnp.floor(unit * (1.0 / LANES))
-            hit = low_row == wide(unit - LANES * high, LANES)
-            value = value_of(device, index)
-            first = value.astype(BF16).astype(F32)
-            lefts.append(
-                jnp.concatenate(
-                    [
-                        jnp.where(hit, wide(first, LANES), none),
-                        jnp.where(hit, wide(value - first, LANES), none),
-                    ],
-                    axis=0,
+        for device in (begin, begin + 1):
+            for index in range(rows):
+                unit = received[device, PIECE + index]
+                high = jnp.floor(unit * (1.0 / LANES))
+                hit = low_row == wide(unit - LANES * high, LANES)
+                value = value_of(device, index)
+                first = value.astype(BF16).astype(F32)
+                lefts.append(
+                    jnp.concatenate(
+                        [
+                            jnp.where(hit, wide(first, LANES), none),
+                            jnp.where(hit, wide(value - first, LANES), none),
+                        ],
+                        axis=0,
+                    )
                 )
-            )
-            rights.append(jnp.where(high_row == wide(high, HIGH), one, none))
+                rights.append(jnp.where(high_row == wide(high, HIGH), one, none))
         found = dot_t(jnp.concatenate(lefts, axis=1), jnp.concatenate(rights, axis=1))
-        if device == 0:
-            total[...] = found[:LANES] + found[LANES:]
+        if begin == 0:
+            total[:LANES] = found[:LANES] + found[LANES:]
         else:
-            total[...] += found[:LANES] + found[LANES:]
+            total[:LANES] += found[:LANES] + found[LANES:]
         yield
 
 
@@ -717,19 +721,15 @@
                 works.remove(work)
 
 
-def scale_kernel(axis, received, other, units_out, scale_out):
-    first = lax.rem(lax.axis_index(axis), 2) == 0
-
-    def weight(device, index):
-        return jnp.where(first, other[device, PIECE + index], received[device, PIECE + index])
-
-    for device in range(received.shape[0]):
-        for index in range(units_out.shape[1]):
-            units_out[device, index] = jnp.where(
-                first, received[device, PIECE + index], other[device, PIECE + index]
+def weights_kernel(received, sums_out):
+    rows = (received.shape[1] - PIECE - 1) // 2
+    together(
+        [
+            unit_sums(
+                received, lambda device, index: received[device, PIECE + rows + index], sums_out
             )
-    together([unit_sums(units_out, weight, scale_out)])
-    scale_out[...] = 1.0 / (scale_out[...] + 1.0)
+        ]
+    )
 
 
 def right_side(values, place):
@@ -739,39 +739,61 @@
     return total
 
 
+def core(axis):
+    return lax.rem(lax.axis_index(axis), 2)
+
+
+def coefficients(bundle, place):
+    return bundle[LANES + place : LANES + place + 1, :WIDTH]
+
+
+def put(bundle, place, line):
+    bundle[LANES + place : LANES + place + 1] = jnp.concatenate([line, line], axis=1)
+
+
+def solve_kernel(axis, values, received, bundle_out, lines_out, bands):
+    half = lines_out.shape[0]
+    rows = values.shape[1] - half - 1
+    for device in range(values.shape[0]):
+        bands[device : device + 1] = values[device, rows + half]
+    bundle_out[LANES:] = jnp.zeros((SUB, HIGH), F32)
+
+    def attitude(place):
+        matrix = matrix_of(bands[BAND * place : BAND * (place + 1)])
+        change = yield from eliminate(matrix, right_side(values, rows + place), lines_out.at[place])
+        start = received[half * core(axis) + place, received.shape[1] - 1]
+        put(bundle_out, place, start + change)
+        yield
+
+    together(
+        [unit_sums(received, lambda device, index: values[device, index], bundle_out)]
+        + [attitude(place) for place in range(half)]
+    )
+
+
+def both_halves(axis, own, other, half):
+    first = core(axis) == 0
+    pairs = [(coefficients(own, place), coefficients(other, place)) for place in range(half)]
+    lines = [jnp.where(first, one, two) for one, two in pairs]
+    return lines + [jnp.where(first, two, one) for one, two in pairs]
+
+
 def second_kernel(
-    values, received, owners, table, scale, cal_id, units, observed, parts, partials, factor, weighted,
-    hits,
-    send_out, params_out, explained_out, table_out, attitude_out, lines_out, bands,
+    axis, bundle, other, weights, other_weights, table, ids, units, observed, parts, partials, factor,
+    weighted, hits,
+    send_out, params_out, explained_out, table_out, scale_out,
 ):
     rows = parts.shape[0]
-    count = values.shape[1] - rows - PIECE
-    for device in range(values.shape[0]):
-        for place in range(PIECE):
-            at = PIECE * device + place
-            bands[at : at + 1] = values[device, count + rows + place]
-    models = [None] * rows
-
-    def attitude(row):
-        matrix = matrix_of(bands[BAND * row : BAND * (row + 1)])
-        change = yield from eliminate(matrix, right_side(values, count + row), lines_out.at[row])
-        new = received[row, received.shape[1] - 1] + change
-        attitude_out[row : row + 1] = new
-        models[row] = model_of(new, parts[row])
-        yield
-
-    def attitudes(first):
-        for row in range(first, rows, 2):
-            yield from attitude(row)
-
-    together(
-        [unit_sums(owners, lambda device, index: values[device, index], table_out)]
-        + [attitudes(first) for first in range(2)]
-    )
-    table_t = table[...] + table_out[...] * scale[...]
+    scale = 1.0 / (weights[...] + other_weights[...] + 1.0)
+    scale_out[...] = scale
+    table_t = table[...] + (bundle[:LANES] + other[:LANES]) * scale
     table_out[...] = table_t
-    picked = pick_from(table_t, flat(cal_id[...]), units[...], rows)
-    targets = [observed[row : row + 1] - models[row] - picked[row] for row in range(rows)]
+    picked = pick_from(table_t, flat(ids[...]), units[...], rows)
+    lines = both_halves(axis, bundle, other, rows // PIECE)
+    targets = [
+        observed[row : row + 1] - model_of(lines[row], parts[row]) - picked[row]
+        for row in range(rows)
+    ]
     params, explained = residual_step(targets, parts, partials, factor, weighted, hits, send_out)
     for index in range(5):
         params_out[index : index + 1] = params[index]
@@ -779,34 +801,38 @@
         explained_out[row : row + 1] = explained[row]
 
 
+def last_kernel(values, received, bundle, lines, bundle_out):
+    half = lines.shape[0]
+    rows = values.shape[1] - half
+    bundle_out[LANES:] = jnp.zeros((SUB, HIGH), F32)
+
+    def solve(place):
+        change = yield from substitute(right_side(values, rows + place), lines.at[place])
+        put(bundle_out, place, coefficients(bundle, place) + change)
+        yield
+
+    together(
+        [unit_sums(received, lambda device, index: values[device, index], bundle_out)]
+        + [solve(place) for place in range(half)]
+    )
+
+
 def final_kernel(
-    axis, values, owners, lines, attitude, table, scale, cal_id, units, observed, parts,
-    explained, cal_out, attitude_out, resid_out, sums,
+    axis, line, bundle, other, table, scale, ids, units, observed, parts, explained,
+    cal_out, attitude_out, resid_out,
 ):
     rows = parts.shape[0]
-    count = values.shape[1] - rows
-    me = lax.axis_index(axis)
-    models, news = [None] * rows, [None] * rows
-
-    def solve(row):
-        change = yield from substitute(right_side(values, count + row), lines.at[row])
-        news[row] = attitude[row : row + 1] + change
-        models[row] = model_of(news[row], parts[row])
-        yield
-
-    together(
-        [unit_sums(owners, lambda device, index: values[device, index], sums)]
-        + [solve(row) for row in range(rows)]
-    )
-    own = news[0]
-    for row in range(1, rows):
-        own = jnp.where(me == row, news[row], own)
+    table_t = table[...] + (bundle[:LANES] + other[:LANES]) * scale[...]
+    cal_out[...] = table_t.T
+    picked = pick_from(table_t, flat(ids[...]), units[...], rows)
+    me = lax.axis_index(line)
+    lines = both_halves(axis, bundle, other, rows // PIECE)
+    own = lines[0]
+    for row in range(rows):
+        own = jnp.where(me == row, lines[row], own)
+        at = slice(row, row + 1)
+        resid_out[at] = observed[at] - model_of(lines[row], parts[row]) - picked[row] - explained[at]
     attitude_out[...] = own
-    table_t = table[...] + sums[...] * scale[...]
-    cal_out[...] = table_t.T
-    for row, picked in enumerate(pick_from(table_t, flat(cal_id[...]), units[...], rows)):
-        at = slice(row, row + 1)
-        resid_out[at] = observed[at] - models[row] - picked - explained[at]
 
 
 VMEM = pl.BlockSpec(memory_space=pltpu.VMEM)
@@ -834,6 +860,10 @@
     return jax.ShapeDtypeStruct(shape, F32)
 
 
+def swap(value):
+    return lax.ppermute(value, "src", [(at, at ^ 1) for at in range(lax.axis_size("src"))])
+
+
 def exchange(value):
     return lax.all_to_all(value, ("src", "tm"), 0, 0, tiled=True)
 
@@ -844,13 +874,13 @@
 ):
     rows, slots = observed.shape
     devices = lax.axis_size("src") * lax.axis_size("tm")
-    count = rows * slots // LANES
+    half = rows // PIECE
     first_q = attitude.reshape(1, WIDTH)
     held = [weight_obs, present, attitude_partials, phase, knot_base, first_q]
     received, design, weighted, seen, source_id, cal_id, source_partials = call(
         normals_kernel,
         [
-            leave(devices, PIECE + count + 1, 1, LANES), stay(rows, WIDTH, slots),
+            leave(devices, PIECE + 2 * rows + 1, 1, LANES), stay(rows, WIDTH, slots),
             stay(rows, slots), stay(rows, slots), stay(rows, slots, dtype=jnp.int32),
             stay(rows, slots, dtype=jnp.int32), stay(*source_partials.shape),
         ],
@@ -874,34 +904,37 @@
     )
     received, factor = lax.optimization_barrier((received, factor))
     (values,) = call(
-        first_kernel, [leave(devices, count + rows + PIECE, 1, LANES)],
+        first_kernel, [leave(devices, rows + half + 1, 1, LANES)],
         received, target, parts, partials, factor, weighted, hits,
     )
     values, received = lax.optimization_barrier((values, received))
     values = exchange(values)
-    sources = lax.axis_size("src")
-    other = lax.ppermute(received, "src", [(at, at ^ 1) for at in range(sources)])
-    owners, scale = call(
-        functools.partial(scale_kernel, "src"),
-        [stay(devices, count, 1, LANES), stay(LANES, HIGH)],
-        received, other,
-    )
-    values, params, explained, table, now, lines = call(
-        second_kernel,
+    (weights,) = call(weights_kernel, [leave(LANES, HIGH)], received)
+    weights, received = lax.optimization_barrier((weights, received))
+    other_weights = swap(weights)
+    bundle, lines = call(
+        functools.partial(solve_kernel, "src"),
+        [leave(LANES + SUB, HIGH), stay(half, WIDTH, WIDTH)],
+        values, received,
+        scratch=[pltpu.VMEM((half * BAND, WIDTH), F32)],
+    )
+    values, params, explained, table, scale = call(
+        functools.partial(second_kernel, "src"),
         [
-            leave(devices, count + rows, 1, LANES), leave(5, SRC_DEV), stay(rows, slots),
-            stay(LANES, HIGH), stay(rows, WIDTH), stay(rows, WIDTH, WIDTH),
+            leave(devices, rows + half, 1, LANES), leave(5, SRC_DEV), stay(rows, slots),
+            stay(LANES, HIGH), stay(LANES, HIGH),
         ],
-        values, received, owners, table, scale, cal_id, units, seen, parts, partials, factor, weighted,
-        hits,
-        scratch=[pltpu.VMEM((rows * BAND, WIDTH), F32)],
+        bundle, swap(bundle), weights, other_weights, table, cal_id, units, seen, parts, partials,
+        factor, weighted, hits,
     )
     values = exchange(values)
+    (bundle,) = call(
+        last_kernel, [leave(LANES + SUB, HIGH)], values, received, bundle, lines
+    )
     cal, now, final = call(
-        functools.partial(final_kernel, "tm"),
+        functools.partial(final_kernel, "src", "tm"),
         [leave(HIGH, LANES), leave(1, WIDTH), leave(rows, slots)],
-        values, owners, lines, now, table, scale, cal_id, units, seen, parts, explained,
-        scratch=[pltpu.VMEM((LANES, HIGH), F32)],
+        bundle, swap(bundle), table, scale, cal_id, units, seen, parts, explained,
     )
     return (params, now.reshape(WIDTH), cal.reshape(CAL), final)
 

time: 60.5 us -> 53.3 us (0.88)
  Pallas kernels: 25.4 us -> 16.5 us
  waiting for transfers between devices: 12.4 us -> 15.6 us
  blocking collectives: 11.5 us -> 9.62 us
    pallas_call x6 -> x8, Pallas kernels: 25.4 us -> 16.5 us  [call(): pl.pallas_call(kernel, out_shape=outs, in_specs=[VMEM] * len(near) + [ANY...]
    all_to_all x2, waiting for transfers between devices: 11 us -> 13.2 us  [exchange(): return lax.all_to_all(value, ('src', 'tm'), 0, 0, tiled=True)]
    all_to_all x1, blocking collectives: 11.5 us -> 9.62 us  [exchange(): return lax.all_to_all(value, ('src', 'tm'), 0, 0, tiled=True)]
    ppermute x1 -> x3, waiting for transfers between devices: 1.4 us -> 2.39 us  [swap(): lax.ppermute(value, 'src', [(at, at ^ 1) for at in range(lax.axis_size('s...]
  transfers between devices with their start and end apart: 3 -> 5, of which waited for: 3 -> 4; matrix products, arithmetic and copies ran while one was open for 0% -> 0% of each run, Pallas kernels for 10% -> 8%
where the time goes in v6:
time: 53.3 us; the launch traced here: 53 us
  Pallas kernels  16.5 us (31%)
  waiting for transfers between devices  15.6 us (29%)
  starting transfers between devices  10.5 us (20%)
  blocking collectives  9.62 us (18%)
  between operations  0.71 us (1%)
    pallas_call x8, Pallas kernels, call(): pl.pallas_call(kernel, out_shape=outs, in_specs=[VMEM] * len(near) + [ANY...  16.5 us
    all_to_all x2, waiting for transfers between devices, exchange(): return lax.all_to_all(value, ('src', 'tm'), 0, 0, tiled=True)  13.2 us
    all_to_all x2, starting transfers between devices, exchange(): return lax.all_to_all(value, ('src', 'tm'), 0, 0, tiled=True)  9.88 us
    all_to_all x1, blocking collectives, exchange(): return lax.all_to_all(value, ('src', 'tm'), 0, 0, tiled=True)  9.62 us
    ppermute x3, waiting for transfers between devices, swap(): lax.ppermute(value, 'src', [(at, at ^ 1) for at in range(lax.axis_size('s...  2.39 us
  transfers between devices with their start and end apart: 5, of which 4 were waited for; matrix products, arithmetic and copies ran while one was open for 0% of the time, Pallas kernels for 8%

profile of v6, /device:TPU:0, one launch (start us, length us, event | category | flops | bytes accessed | tf_op | source)
XLA Modules:
  0.0 53.0 jit_solution(2192239414033492792)
XLA Ops:
  0.6 2.5 %shard_map.138 = (f32[32,11,1,128]{3,2,1,0:T(1,128)}, f32[4,128,256]{2,1,0:T(8,128)S(1)}, f32[4,256]{1,0:T(4,128)S(1)}, f32[4,256]{1,0:T(4,128)S(1)}, s32[4,256]...) custom-call(f32[4,256]{1,0:T(4,128)} %observed_in.1, f32[4,256]{1,0:T(4,128)} %weight_in.1, ...), custom_call_target="tpu_custom_call" | custom-call | tf_op jit(solution)/shard_map/pallas_call | solution.py:845
  3.1 7.3 %all-to-all-start = ((f32[32,11,1,128]{3,2,1,0:T(1,128)}), f32[32,11,1,128]{3,2,1,0:T(1,128)S(1)}, u32[]{:S(2)}, u32[]{:S(2)}) async-start(f32[32,11,1,128]{3,2,1,0:T(1,128)} %get-tuple-element.34), calls=%async_computation | async-start | bytes 360448 | tf_op jit(solution)/shard_map/all_to_all | solution.py:868
  10.4 1.7 %shard_map.139 = (f32[4,8,256]{2,1,0:T(8,128)S(1)}, f32[16,128]{1,0:T(8,128)S(1)}, f32[4,256]{1,0:T(4,128)S(1)}, f32[128,256]{1,0:T(8,128)S(1)}, bf16[4,128,256]...) custom-call(f32[4,256]{1,0:T(4,128)S(1)} %get-tuple-element.35.observed, ...), custom_call_target="tpu_custom_call" | custom-call | tf_op jit(solution)/shard_map/pallas_call | solution.py:845
  12.1 7.4 %all-to-all-done.received = f32[32,11,1,128]{3,2,1,0:T(1,128)S(1)} async-done(((f32[32,11,1,128]{3,2,1,0:T(1,128)}), f32[32,11,1,128]{3,2,1,0:T(1,128)S(1)}, u32[]{:S(2)}, u32[]{:S(2)}) %all-to-all-start) | async-done | bytes 180256 | tf_op jit(solution)/shard_map/all_to_all | solution.py:868
  19.5 1.4 %shard_map.140 = f32[32,7,1,128]{3,2,1,0:T(1,128)} custom-call(f32[32,11,1,128]{3,2,1,0:T(1,128)S(1)} %all-to-all-done.received, f32[4,256]{1,0:T(4,128)S(1)} %get-tuple-element.43.target, bf16[4,256,256]{2,1,0:T(8,128)(2,1)S(1)} %get-tuple-element.44.parts, f32[4,8,256]{2,1,0:T(8,128)S(1)} %get-tuple-element.45.partials, ...), custom_call_target="tpu_custom_call" | custom-call | tf_op jit(solution)/shard_map/pallas_call | solution.py:845
  20.9 2.6 %all-to-all-start.1 = ((f32[32,7,1,128]{3,2,1,0:T(1,128)}), f32[32,7,1,128]{3,2,1,0:T(1,128)S(1)}, u32[]{:S(2)}, u32[]{:S(2)}) async-start(f32[32,7,1,128]{3,2,1,0:T(1,128)} %shard_map.140), calls=%async_computation.1 | async-start | bytes 229376 | tf_op jit(solution)/shard_map/all_to_all | solution.py:868
  23.5 2.4 %shard_map.141.weights = f32[128,256]{1,0:T(8,128)S(1)} custom-call(f32[32,11,1,128]{3,2,1,0:T(1,128)S(1)} %all-to-all-done.received), custom_call_target="tpu_custom_call" | custom-call | tf_op jit(solution)/shard_map/pallas_call | solution.py:845
  25.8 5.8 %all-to-all-done.1.values = f32[32,7,1,128]{3,2,1,0:T(1,128)S(1)} async-done(((f32[32,7,1,128]{3,2,1,0:T(1,128)}), f32[32,7,1,128]{3,2,1,0:T(1,128)S(1)}, u32[]{:S(2)}, u32[]{:S(2)}) %all-to-all-start.1) | async-done | bytes 114720 | tf_op jit(solution)/shard_map/all_to_all | solution.py:868
  31.6 3.8 %shard_map.142 = (f32[136,256]{1,0:T(8,128)S(1)}, f32[2,128,128]{2,1,0:T(8,128)S(1)}) custom-call(f32[32,7,1,128]{3,2,1,0:T(1,128)S(1)} %all-to-all-done.1.values, f32[32,11,1,128]{3,2,1,0:T(1,128)S(1)} %all-to-all-done.received), custom_call_target="tpu_custom_call" | custom-call | tf_op jit(solution)/shard_map/pallas_call | solution.py:845
  35.5 0.1 collective-permute-start
  35.6 0.5 collective-permute-start.1
  36.1 1.0 %collective-permute-done.1.other_weights = f32[128,256]{1,0:T(8,128)S(1)} collective-permute-done((f32[128,256]{1,0:T(8,128)S(1)}, f32[128,256]{1,0:T(8,128)S(1)}, u32[]{:S(2)}, u32[]{:S(2)}) %collective-permute-start.1) | collective-permute-done | bytes 131104 | tf_op jit(solution)/shard_map/ppermute | solution.py:864
  37.1 0.0 collective-permute-done.other
  37.1 1.4 %shard_map.143 = (f32[32,6,1,128]{3,2,1,0:T(1,128)S(1)}, f32[5,128]{1,0:T(8,128)}, f32[4,256]{1,0:T(4,128)S(1)}, f32[128,256]{1,0:T(8,128)S(1)}, f32[128,256]{1,0:T(8,128)S(1)}) custom-call(f32[136,256]{1,0:T(8,128)S(1)} %get-tuple-element.51.bundle, f32[136,256]{1,0:T(8,128)S(1)} %collective-permute-done.other, f32[128,256]{1,0:T(8,128)S(1)} %shard_map.141.weights, ...), custom_call_target="tpu_custom_call" | custom-call | tf_op jit(solution)/shard_map/pallas_call | solution.py:845
  38.5 9.6 %all_to_all.15.values = f32[32,6,1,128]{3,2,1,0:T(1,128)S(1)} all-to-all(f32[32,6,1,128]{3,2,1,0:T(1,128)S(1)} %get-tuple-element.56), channel_id=1, replica_groups=mesh['src'=8,'tm'=4] {'src','tm'}, dimensions={0} | all-to-all | bytes 196608 | tf_op jit(solution)/shard_map/all_to_all | solution.py:868
  48.1 2.4 %shard_map.144.bundle = f32[136,256]{1,0:T(8,128)S(1)} custom-call(f32[32,6,1,128]{3,2,1,0:T(1,128)S(1)} %all_to_all.15.values, f32[32,11,1,128]{3,2,1,0:T(1,128)S(1)} %all-to-all-done.received, f32[136,256]{1,0:T(8,128)S(1)} %get-tuple-element.51.bundle, f32[2,128,128]{2,1,0:T(8,128)S(1)} %get-tuple-element.57.lines), custom_call_target="tpu_custom_call" | custom-call | tf_op jit(solution)/shard_map/pallas_call | solution.py:845
  50.5 0.1 collective-permute-start.2
  50.6 1.3 %collective-permute-done.2.other = f32[136,256]{1,0:T(8,128)S(1)} collective-permute-done((f32[136,256]{1,0:T(8,128)S(1)}, f32[136,256]{1,0:T(8,128)S(1)}, u32[]{:S(2)}, u32[]{:S(2)}) %collective-permute-start.2) | collective-permute-done | bytes 139296 | tf_op jit(solution)/shard_map/ppermute | solution.py:864
  51.9 1.0 %shard_map.145 = (f32[256,128]{1,0:T(8,128)}, f32[1,128]{1,0:T(1,128)}, f32[4,256]{1,0:T(4,128)}) custom-call(f32[136,256]{1,0:T(8,128)S(1)} %shard_map.144.bundle, f32[136,256]{1,0:T(8,128)S(1)} %collective-permute-done.2.other, f32[128,256]{1,0:T(8,128)S(1)} %get-tuple-element.58.table, f32[128,256]{1,0:T(8,128)S(1)} %get-tuple-element.59.scale, ...), custom_call_target="tpu_custom_call" | custom-call | tf_op jit(solution)/shard_map/pallas_call | solution.py:845
Async XLA Ops:
  3.1 16.4 %all-to-all-start = ((f32[32,11,1,128]{3,2,1,0:T(1,128)}), f32[32,11,1,128]{3,2,1,0:T(1,128)S(1)}, u32[]{:S(2)}, u32[]{:S(2)}) async-start(f32[32,11,1,128]{3,2,1,0:T(1,128)} %get-tuple-element.34), calls=%async_computation | async-start | bytes 360448 | tf_op jit(solution)/shard_map/all_to_all | solution.py:868
  20.9 10.8 %all-to-all-start.1 = ((f32[32,7,1,128]{3,2,1,0:T(1,128)}), f32[32,7,1,128]{3,2,1,0:T(1,128)S(1)}, u32[]{:S(2)}, u32[]{:S(2)}) async-start(f32[32,7,1,128]{3,2,1,0:T(1,128)} %shard_map.140), calls=%async_computation.1 | async-start | bytes 229376 | tf_op jit(solution)/shard_map/all_to_all | solution.py:868
  35.5 1.6 %collective-permute-start = (f32[136,256]{1,0:T(8,128)S(1)}, f32[136,256]{1,0:T(8,128)S(1)}, u32[]{:S(2)}, u32[]{:S(2)}) collective-permute-start(f32[136,256]{1,0:T(8,128)S(1)} %get-tuple-element.51.bundle), channel_id=1, source_target_pairs={{0,4},{4,0},{8,12},{12,8},{16,20},{20,16},{24,28},{28,24},{1,5},{5... | collective-permute-start | bytes 417800 | tf_op jit(solution)/shard_map/ppermute | solution.py:864
  35.6 1.5 %collective-permute-start.1 = (f32[128,256]{1,0:T(8,128)S(1)}, f32[128,256]{1,0:T(8,128)S(1)}, u32[]{:S(2)}, u32[]{:S(2)}) collective-permute-start(f32[128,256]{1,0:T(8,128)S(1)} %shard_map.141.weights), channel_id=1, source_target_pairs={{0,4},{4,0},{8,12},{12,8},{16,20},{20,16},{24,28},{28,24},{1,5},{5... | collective-permute-start | bytes 393224 | tf_op jit(solution)/shard_map/ppermute | solution.py:864
  50.5 1.4 %collective-permute-start.2 = (f32[136,256]{1,0:T(8,128)S(1)}, f32[136,256]{1,0:T(8,128)S(1)}, u32[]{:S(2)}, u32[]{:S(2)}) collective-permute-start(f32[136,256]{1,0:T(8,128)S(1)} %shard_map.144.bundle), channel_id=1, source_target_pairs={{0,4},{4,0},{8,12},{12,8},{16,20},{20,16},{24,28},{28,24},{1,5},{5... | collective-permute-start | bytes 417800 | tf_op jit(solution)/shard_map/ppermute | solution.py:864

commit v7 on v6

--- a/solution.py
+++ b/solution.py
@@ -160,8 +160,14 @@
 PLAN = plan_of(ORDER)
 
 
+def reciprocal(value):
+    found = pl.reciprocal(value, approx=True)
+    found = found * (2.0 - value * found)
+    return found * (2.0 - value * found)
+
+
 def block_rows(entry, lines):
-    scale = 1.0 / (entry[0, 0] * entry[1, 1] - entry[0, 1] * entry[0, 1])
+    scale = reciprocal(entry[0, 0] * entry[1, 1] - entry[0, 1] * entry[0, 1])
     low, mid, high = entry[0, 0] * scale, entry[0, 1] * scale, entry[1, 1] * scale
     turned = {}
     for column in (2, 3):
@@ -175,7 +181,7 @@
     lower = [
         lines[row] - (entry[0, row] * upper[0] + entry[1, row] * upper[1]) for row in (2, 3)
     ]
-    scale = 1.0 / (rest[2, 2] * rest[3, 3] - rest[2, 3] * rest[2, 3])
+    scale = reciprocal(rest[2, 2] * rest[3, 3] - rest[2, 3] * rest[2, 3])
     third = (rest[3, 3] * scale) * lower[0] - (rest[2, 3] * scale) * lower[1]
     fourth = (rest[2, 2] * scale) * lower[1] - (rest[2, 3] * scale) * lower[0]
     return [
@@ -512,8 +518,8 @@
 
 
 def pick_from(table_t, ids, units, rows):
-    found = dot(jnp.concatenate(split3(table_t), axis=0), units)
-    found = found[:LANES] + found[LANES : 2 * LANES] + found[2 * LANES :]
+    found = dot(jnp.concatenate(split3(table_t)[:2], axis=0), units)
+    found = found[:LANES] + found[LANES:]
     hit = iota(found.shape, 0) == ids % LANES
     return unflat(jnp.sum(jnp.where(hit, found, 0.0), axis=0, keepdims=True), rows)
 
@@ -541,20 +547,18 @@
 
 
 def normals_kernel(
-    observed_in, weight_in, present_in, source_in, attitude_in, phase_in, knot_in, id_in, cal_in,
-    start_in,
-    send_out, design_out, weighted_out, observed, source_id, cal_id, source_partials,
+    weight_in, present_in, attitude_in, phase_in, knot_in, cal_in, start_in,
+    send_out, design_out, weighted_out, cal_id,
     weight_obs, present, attitude_partials, phase, knot_base, start, stacked, sems,
 ):
     fetch(
         [
-            (observed_in, observed), (weight_in, weight_obs), (present_in, present),
-            (source_in, source_partials), (attitude_in, attitude_partials), (phase_in, phase),
-            (knot_in, knot_base), (id_in, source_id), (cal_in, cal_id), (start_in, start),
+            (phase_in, phase), (knot_in, knot_base), (attitude_in, attitude_partials),
+            (weight_in, weight_obs), (present_in, present), (cal_in, cal_id), (start_in, start),
         ],
         sems,
     )
-    rows, slots = observed.shape
+    rows = weight_obs.shape[0]
     weighted = present[...].astype(F32) * weight_obs[...]
     weighted_out[...] = weighted
     u = phase[...]
@@ -591,11 +595,17 @@
 
 
 def sources_kernel(
-    observed, source_partials, source_id, cal_id, weighted, design, calibration,
-    partials_out, factor_out, target_out, table_out, hits_out, units_out, parts_out, table, sem,
+    cal_id, weighted, design, observed_in, source_in, id_in, calibration_in,
+    partials_out, factor_out, target_out, table_out, hits_out, units_out, parts_out, observed,
+    source_partials, source_id, table, sems,
 ):
-    copy = pltpu.make_async_copy(calibration, table, sem)
-    copy.start()
+    fetch(
+        [
+            (observed_in, observed), (source_in, source_partials), (id_in, source_id),
+            (calibration_in, table),
+        ],
+        sems,
+    )
     rows, slots = observed.shape
     matrix = jnp.zeros((40, SRC_DEV), F32)
     for row in range(rows):
@@ -619,7 +629,6 @@
     for place, pair in enumerate(PLACES):
         factor_out[place : place + 1] = inverse[pair]
     factor_out[15:16] = jnp.zeros((1, SRC_DEV), F32)
-    copy.wait()
     table_t = table[...].T
     table_out[...] = table_t
     for row, picked in enumerate(pick_from(table_t, ids, units_out[...], rows)):
@@ -819,11 +828,13 @@
 
 def final_kernel(
     axis, line, bundle, other, table, scale, ids, units, observed, parts, explained,
-    cal_out, attitude_out, resid_out,
+    cal_out, attitude_out, resid_out, new_cal, sem,
 ):
     rows = parts.shape[0]
     table_t = table[...] + (bundle[:LANES] + other[:LANES]) * scale[...]
-    cal_out[...] = table_t.T
+    new_cal[...] = table_t.T
+    copy = pltpu.make_async_copy(new_cal, cal_out, sem)
+    copy.start()
     picked = pick_from(table_t, flat(ids[...]), units[...], rows)
     me = lax.axis_index(line)
     lines = both_halves(axis, bundle, other, rows // PIECE)
@@ -833,20 +844,21 @@
         at = slice(row, row + 1)
         resid_out[at] = observed[at] - model_of(lines[row], parts[row]) - picked[row] - explained[at]
     attitude_out[...] = own
+    copy.wait()
 
 
 VMEM = pl.BlockSpec(memory_space=pltpu.VMEM)
 ANY = pl.BlockSpec(memory_space=pltpu.HBM)
 
 
-def call(kernel, outs, *args, away=0, scratch=()):
+def call(kernel, outs, *args, away=0, scratch=(), specs=None):
     near = args[: len(args) - away]
     far = [pltpu.with_memory_space_constraint(arg, pltpu.HBM) for arg in args[len(args) - away :]]
     return pl.pallas_call(
         kernel,
         out_shape=outs,
         in_specs=[VMEM] * len(near) + [ANY] * away,
-        out_specs=[VMEM] * len(outs),
+        out_specs=specs or [VMEM] * len(outs),
         scratch_shapes=scratch,
         compiler_params=pltpu.CompilerParams(vmem_limit_bytes=VMEM_BYTES),
     )(*near, *far)
@@ -877,30 +889,33 @@
     half = rows // PIECE
     first_q = attitude.reshape(1, WIDTH)
     held = [weight_obs, present, attitude_partials, phase, knot_base, first_q]
-    received, design, weighted, seen, source_id, cal_id, source_partials = call(
+    received, design, weighted, units_seen = call(
         normals_kernel,
         [
             leave(devices, PIECE + 2 * rows + 1, 1, LANES), stay(rows, WIDTH, slots),
-            stay(rows, slots), stay(rows, slots), stay(rows, slots, dtype=jnp.int32),
-            stay(rows, slots, dtype=jnp.int32), stay(*source_partials.shape),
+            stay(rows, slots), stay(rows, slots, dtype=jnp.int32),
         ],
-        observed, weight_obs, present, source_partials, attitude_partials, phase, knot_base,
-        source_id, cal_id, first_q,
-        away=10,
+        weight_obs, present, attitude_partials, phase, knot_base, cal_id, first_q,
+        away=7,
         scratch=[pltpu.VMEM(each.shape, each.dtype) for each in held]
-        + [pltpu.VMEM((rows, SUB, slots), F32), pltpu.SemaphoreType.DMA((10,))],
+        + [pltpu.VMEM((rows, SUB, slots), F32), pltpu.SemaphoreType.DMA((7,))],
     )
     received = exchange(received)
-    partials, factor, target, table, hits, units, parts = call(
+    cal_id = units_seen
+    partials, factor, target, table, hits, units, parts, seen = call(
         sources_kernel,
         [
             stay(rows, SUB, slots), stay(16, SRC_DEV), stay(rows, slots), stay(LANES, HIGH),
             stay(rows, SRC_DEV, slots, dtype=BF16), stay(HIGH, rows * slots, dtype=BF16),
-            stay(rows, 2 * WIDTH, slots, dtype=BF16),
+            stay(rows, 2 * WIDTH, slots, dtype=BF16), stay(rows, slots),
         ],
-        seen, source_partials, source_id, cal_id, weighted, design, calibration.reshape(HIGH, LANES),
-        away=1,
-        scratch=[pltpu.VMEM((HIGH, LANES), F32), pltpu.SemaphoreType.DMA],
+        cal_id, weighted, design, observed, source_partials, source_id,
+        calibration.reshape(HIGH, LANES),
+        away=4,
+        scratch=[
+            pltpu.VMEM(source_partials.shape, F32), pltpu.VMEM((rows, slots), jnp.int32),
+            pltpu.VMEM((HIGH, LANES), F32), pltpu.SemaphoreType.DMA((4,)),
+        ],
     )
     received, factor = lax.optimization_barrier((received, factor))
     (values,) = call(
@@ -935,6 +950,8 @@
         functools.partial(final_kernel, "src", "tm"),
         [leave(HIGH, LANES), leave(1, WIDTH), leave(rows, slots)],
         bundle, swap(bundle), table, scale, cal_id, units, seen, parts, explained,
+        scratch=[pltpu.VMEM((HIGH, LANES), F32), pltpu.SemaphoreType.DMA],
+        specs=[ANY, VMEM, VMEM],
     )
     return (params, now.reshape(WIDTH), cal.reshape(CAL), final)
 

time: 53.3 us -> 54 us (1.013)
  transfers between devices with their start and end apart: 5 -> 5, of which waited for: 4 -> 4; matrix products, arithmetic and copies ran while one was open for 0% -> 0% of each run, Pallas kernels for 8% -> 7%
where the time goes in v7:
time: 54 us; the launch traced here: 53.6 us
  Pallas kernels  17 us (31%)
  waiting for transfers between devices  15.7 us (29%)
  starting transfers between devices  10.5 us (19%)
  blocking collectives  9.62 us (18%)
  between operations  0.7 us (1%)
    pallas_call x8, Pallas kernels, call(): pl.pallas_call(kernel, out_shape=outs, in_specs=[VMEM] * len(near) + [ANY...  17 us
    all_to_all x2, waiting for transfers between devices, exchange(): return lax.all_to_all(value, ('src', 'tm'), 0, 0, tiled=True)  13.3 us
    all_to_all x2, starting transfers between devices, exchange(): return lax.all_to_all(value, ('src', 'tm'), 0, 0, tiled=True)  9.88 us
    all_to_all x1, blocking collectives, exchange(): return lax.all_to_all(value, ('src', 'tm'), 0, 0, tiled=True)  9.62 us
    ppermute x3, waiting for transfers between devices, swap(): lax.ppermute(value, 'src', [(at, at ^ 1) for at in range(lax.axis_size('s...  2.39 us
  transfers between devices with their start and end apart: 5, of which 4 were waited for; matrix products, arithmetic and copies ran while one was open for 0% of the time, Pallas kernels for 7%

profile of v7, /device:TPU:0, one launch (start us, length us, event | category | flops | bytes accessed | tf_op | source)
XLA Modules:
  0.0 53.6 jit_solution(905465336121599607)
XLA Ops:
  0.6 2.4 %shard_map.138 = (f32[32,11,1,128]{3,2,1,0:T(1,128)}, f32[4,128,256]{2,1,0:T(8,128)S(1)}, f32[4,256]{1,0:T(4,128)S(1)}, s32[4,256]{1,0:T(4,128)S(1)}) custom-call(f32[4,256]{1,0:T(4,128)} %weight_in.1, s32[4,256]{1,0:T(4,128)} %present_in.1, f32[4,4,256]{2,1,0:T(4,128)} %attitude_in.1, f32[4,256]{1,0:T(4,128)} %phase_in.1, s32[4,256]{1,0:T(4,128)} %knot_in.1, ...), custom_call_target="tpu_custom_call" | custom-call | tf_op jit(solution)/shard_map/pallas_call | solution.py:857
  3.0 7.3 %all-to-all-start = ((f32[32,11,1,128]{3,2,1,0:T(1,128)}), f32[32,11,1,128]{3,2,1,0:T(1,128)S(1)}, u32[]{:S(2)}, u32[]{:S(2)}) async-start(f32[32,11,1,128]{3,2,1,0:T(1,128)} %get-tuple-element.32), calls=%async_computation | async-start | bytes 360448 | tf_op jit(solution)/shard_map/all_to_all | solution.py:880
  10.3 1.5 %shard_map.139 = (f32[4,8,256]{2,1,0:T(8,128)S(1)}, f32[16,128]{1,0:T(8,128)S(1)}, f32[4,256]{1,0:T(4,128)S(1)}, f32[128,256]{1,0:T(8,128)S(1)}, bf16[4,128,256]...) custom-call(s32[4,256]{1,0:T(4,128)S(1)} %get-tuple-element.33.cal_i, ...), custom_call_target="tpu_custom_call" | custom-call | tf_op jit(solution)/shard_map/pallas_call | solution.py:857
  11.9 7.5 %all-to-all-done.received = f32[32,11,1,128]{3,2,1,0:T(1,128)S(1)} async-done(((f32[32,11,1,128]{3,2,1,0:T(1,128)}), f32[32,11,1,128]{3,2,1,0:T(1,128)S(1)}, u32[]{:S(2)}, u32[]{:S(2)}) %all-to-all-start) | async-done | bytes 180256 | tf_op jit(solution)/shard_map/all_to_all | solution.py:880
  19.5 1.4 %shard_map.140 = f32[32,7,1,128]{3,2,1,0:T(1,128)} custom-call(f32[32,11,1,128]{3,2,1,0:T(1,128)S(1)} %all-to-all-done.received, f32[4,256]{1,0:T(4,128)S(1)} %get-tuple-element.38.target, bf16[4,256,256]{2,1,0:T(8,128)(2,1)S(1)} %get-tuple-element.39.parts, f32[4,8,256]{2,1,0:T(8,128)S(1)} %get-tuple-element.40.partials, ...), custom_call_target="tpu_custom_call" | custom-call | tf_op jit(solution)/shard_map/pallas_call | solution.py:857
  20.8 2.6 %all-to-all-start.1 = ((f32[32,7,1,128]{3,2,1,0:T(1,128)}), f32[32,7,1,128]{3,2,1,0:T(1,128)S(1)}, u32[]{:S(2)}, u32[]{:S(2)}) async-start(f32[32,7,1,128]{3,2,1,0:T(1,128)} %shard_map.140), calls=%async_computation.1 | async-start | bytes 229376 | tf_op jit(solution)/shard_map/all_to_all | solution.py:880
  23.4 2.4 %shard_map.141.weights = f32[128,256]{1,0:T(8,128)S(1)} custom-call(f32[32,11,1,128]{3,2,1,0:T(1,128)S(1)} %all-to-all-done.received), custom_call_target="tpu_custom_call" | custom-call | tf_op jit(solution)/shard_map/pallas_call | solution.py:857
  25.8 5.8 %all-to-all-done.1.values = f32[32,7,1,128]{3,2,1,0:T(1,128)S(1)} async-done(((f32[32,7,1,128]{3,2,1,0:T(1,128)}), f32[32,7,1,128]{3,2,1,0:T(1,128)S(1)}, u32[]{:S(2)}, u32[]{:S(2)}) %all-to-all-start.1) | async-done | bytes 114720 | tf_op jit(solution)/shard_map/all_to_all | solution.py:880
  31.6 4.1 %shard_map.142 = (f32[136,256]{1,0:T(8,128)S(1)}, f32[2,128,128]{2,1,0:T(8,128)S(1)}) custom-call(f32[32,7,1,128]{3,2,1,0:T(1,128)S(1)} %all-to-all-done.1.values, f32[32,11,1,128]{3,2,1,0:T(1,128)S(1)} %all-to-all-done.received), custom_call_target="tpu_custom_call" | custom-call | tf_op jit(solution)/shard_map/pallas_call | solution.py:857
  35.6 0.1 collective-permute-start
  35.7 0.5 collective-permute-start.1
  36.2 1.0 %collective-permute-done.1.other_weights = f32[128,256]{1,0:T(8,128)S(1)} collective-permute-done((f32[128,256]{1,0:T(8,128)S(1)}, f32[128,256]{1,0:T(8,128)S(1)}, u32[]{:S(2)}, u32[]{:S(2)}) %collective-permute-start.1) | collective-permute-done | bytes 131104 | tf_op jit(solution)/shard_map/ppermute | solution.py:876
  37.3 0.0 collective-permute-done.other
  37.3 1.3 %shard_map.143 = (f32[32,6,1,128]{3,2,1,0:T(1,128)S(1)}, f32[5,128]{1,0:T(8,128)}, f32[4,256]{1,0:T(4,128)S(1)}, f32[128,256]{1,0:T(8,128)S(1)}, f32[128,256]{1,0:T(8,128)S(1)}) custom-call(f32[136,256]{1,0:T(8,128)S(1)} %get-tuple-element.46.bundle, f32[136,256]{1,0:T(8,128)S(1)} %collective-permute-done.other, f32[128,256]{1,0:T(8,128)S(1)} %shard_map.141.weights, ...), custom_call_target="tpu_custom_call" | custom-call | tf_op jit(solution)/shard_map/pallas_call | solution.py:857
  38.6 9.6 %all_to_all.15.values = f32[32,6,1,128]{3,2,1,0:T(1,128)S(1)} all-to-all(f32[32,6,1,128]{3,2,1,0:T(1,128)S(1)} %get-tuple-element.52), channel_id=1, replica_groups=mesh['src'=8,'tm'=4] {'src','tm'}, dimensions={0} | all-to-all | bytes 196608 | tf_op jit(solution)/shard_map/all_to_all | solution.py:880
  48.2 2.4 %shard_map.144.bundle = f32[136,256]{1,0:T(8,128)S(1)} custom-call(f32[32,6,1,128]{3,2,1,0:T(1,128)S(1)} %all_to_all.15.values, f32[32,11,1,128]{3,2,1,0:T(1,128)S(1)} %all-to-all-done.received, f32[136,256]{1,0:T(8,128)S(1)} %get-tuple-element.46.bundle, f32[2,128,128]{2,1,0:T(8,128)S(1)} %get-tuple-element.53.lines), custom_call_target="tpu_custom_call" | custom-call | tf_op jit(solution)/shard_map/pallas_call | solution.py:857
  50.6 0.1 collective-permute-start.2
  50.7 1.3 %collective-permute-done.2.other = f32[136,256]{1,0:T(8,128)S(1)} collective-permute-done((f32[136,256]{1,0:T(8,128)S(1)}, f32[136,256]{1,0:T(8,128)S(1)}, u32[]{:S(2)}, u32[]{:S(2)}) %collective-permute-start.2) | collective-permute-done | bytes 139296 | tf_op jit(solution)/shard_map/ppermute | solution.py:876
  52.0 1.6 %shard_map.145 = (f32[256,128]{1,0:T(8,128)}, f32[1,128]{1,0:T(1,128)}, f32[4,256]{1,0:T(4,128)}) custom-call(f32[136,256]{1,0:T(8,128)S(1)} %shard_map.144.bundle, f32[136,256]{1,0:T(8,128)S(1)} %collective-permute-done.2.other, f32[128,256]{1,0:T(8,128)S(1)} %get-tuple-element.54.table, f32[128,256]{1,0:T(8,128)S(1)} %get-tuple-element.55.scale, ...), custom_call_target="tpu_custom_call" | custom-call | tf_op jit(solution)/shard_map/pallas_call | solution.py:857
Async XLA Ops:
  3.0 16.4 %all-to-all-start = ((f32[32,11,1,128]{3,2,1,0:T(1,128)}), f32[32,11,1,128]{3,2,1,0:T(1,128)S(1)}, u32[]{:S(2)}, u32[]{:S(2)}) async-start(f32[32,11,1,128]{3,2,1,0:T(1,128)} %get-tuple-element.32), calls=%async_computation | async-start | bytes 360448 | tf_op jit(solution)/shard_map/all_to_all | solution.py:880
  20.8 10.8 %all-to-all-start.1 = ((f32[32,7,1,128]{3,2,1,0:T(1,128)}), f32[32,7,1,128]{3,2,1,0:T(1,128)S(1)}, u32[]{:S(2)}, u32[]{:S(2)}) async-start(f32[32,7,1,128]{3,2,1,0:T(1,128)} %shard_map.140), calls=%async_computation.1 | async-start | bytes 229376 | tf_op jit(solution)/shard_map/all_to_all | solution.py:880
  35.6 1.6 %collective-permute-start = (f32[136,256]{1,0:T(8,128)S(1)}, f32[136,256]{1,0:T(8,128)S(1)}, u32[]{:S(2)}, u32[]{:S(2)}) collective-permute-start(f32[136,256]{1,0:T(8,128)S(1)} %get-tuple-element.46.bundle), channel_id=1, source_target_pairs={{0,4},{4,0},{8,12},{12,8},{16,20},{20,16},{24,28},{28,24},{1,5},{5... | collective-permute-start | bytes 417800 | tf_op jit(solution)/shard_map/ppermute | solution.py:876
  35.7 1.5 %collective-permute-start.1 = (f32[128,256]{1,0:T(8,128)S(1)}, f32[128,256]{1,0:T(8,128)S(1)}, u32[]{:S(2)}, u32[]{:S(2)}) collective-permute-start(f32[128,256]{1,0:T(8,128)S(1)} %shard_map.141.weights), channel_id=1, source_target_pairs={{0,4},{4,0},{8,12},{12,8},{16,20},{20,16},{24,28},{28,24},{1,5},{5... | collective-permute-start | bytes 393224 | tf_op jit(solution)/shard_map/ppermute | solution.py:876
  50.6 1.4 %collective-permute-start.2 = (f32[136,256]{1,0:T(8,128)S(1)}, f32[136,256]{1,0:T(8,128)S(1)}, u32[]{:S(2)}, u32[]{:S(2)}) collective-permute-start(f32[136,256]{1,0:T(8,128)S(1)} %shard_map.144.bundle), channel_id=1, source_target_pairs={{0,4},{4,0},{8,12},{12,8},{16,20},{20,16},{24,28},{28,24},{1,5},{5... | collective-permute-start | bytes 417800 | tf_op jit(solution)/shard_map/ppermute | solution.py:876

commit v8 on v7

--- a/solution.py
+++ b/solution.py
@@ -160,14 +160,8 @@
 PLAN = plan_of(ORDER)
 
 
-def reciprocal(value):
-    found = pl.reciprocal(value, approx=True)
-    found = found * (2.0 - value * found)
-    return found * (2.0 - value * found)
-
-
 def block_rows(entry, lines):
-    scale = reciprocal(entry[0, 0] * entry[1, 1] - entry[0, 1] * entry[0, 1])
+    scale = 1.0 / (entry[0, 0] * entry[1, 1] - entry[0, 1] * entry[0, 1])
     low, mid, high = entry[0, 0] * scale, entry[0, 1] * scale, entry[1, 1] * scale
     turned = {}
     for column in (2, 3):
@@ -181,7 +175,7 @@
     lower = [
         lines[row] - (entry[0, row] * upper[0] + entry[1, row] * upper[1]) for row in (2, 3)
     ]
-    scale = reciprocal(rest[2, 2] * rest[3, 3] - rest[2, 3] * rest[2, 3])
+    scale = 1.0 / (rest[2, 2] * rest[3, 3] - rest[2, 3] * rest[2, 3])
     third = (rest[3, 3] * scale) * lower[0] - (rest[2, 3] * scale) * lower[1]
     fourth = (rest[2, 2] * scale) * lower[1] - (rest[2, 3] * scale) * lower[0]
     return [
@@ -500,13 +494,17 @@
 PIECE = 2
 
 
-def fetch(pairs, sems):
+def begin(pairs, sems):
     copies = [
         pltpu.make_async_copy(origin, held, sems.at[place])
         for place, (origin, held) in enumerate(pairs)
     ]
     for copy in copies:
         copy.start()
+    return copies
+
+
+def finish(copies):
     for copy in copies:
         copy.wait()
 
@@ -551,16 +549,27 @@
     send_out, design_out, weighted_out, cal_id,
     weight_obs, present, attitude_partials, phase, knot_base, start, stacked, sems,
 ):
-    fetch(
+    copies = begin(
         [
+            (weight_in, weight_obs), (present_in, present), (cal_in, cal_id), (start_in, start),
             (phase_in, phase), (knot_in, knot_base), (attitude_in, attitude_partials),
-            (weight_in, weight_obs), (present_in, present), (cal_in, cal_id), (start_in, start),
         ],
         sems,
     )
+    finish(copies[:4])
     rows = weight_obs.shape[0]
     weighted = present[...].astype(F32) * weight_obs[...]
     weighted_out[...] = weighted
+    first, second = tile_of(cal_id[...].astype(F32)), tile_of(weighted)
+    devices = send_out.shape[0]
+    for device in range(devices):
+        core = core_of(device, rows)
+        for index in range(rows):
+            at = rows * core + index
+            send_out[device, PIECE + index] = first[at : at + 1]
+            send_out[device, PIECE + rows + index] = second[at : at + 1]
+        send_out[device, PIECE + 2 * rows] = start[...]
+    finish(copies[4:])
     u = phase[...]
     other = 1.0 - u
     square = u * u
@@ -571,15 +580,6 @@
         (-3.0 * cube + 3.0 * square + 3.0 * u + 1.0) / 6.0,
         cube / 6.0,
     ]
-    first, second = tile_of(cal_id[...].astype(F32)), tile_of(weighted)
-    devices = send_out.shape[0]
-    for device in range(devices):
-        core = core_of(device, rows)
-        for index in range(rows):
-            at = rows * core + index
-            send_out[device, PIECE + index] = first[at : at + 1]
-            send_out[device, PIECE + rows + index] = second[at : at + 1]
-        send_out[device, PIECE + 2 * rows] = start[...]
     for row in range(rows):
         at = slice(row, row + 1)
         for channel in range(4):
@@ -599,13 +599,14 @@
     partials_out, factor_out, target_out, table_out, hits_out, units_out, parts_out, observed,
     source_partials, source_id, table, sems,
 ):
-    fetch(
+    copies = begin(
         [
             (observed_in, observed), (source_in, source_partials), (id_in, source_id),
             (calibration_in, table),
         ],
         sems,
     )
+    finish(copies)
     rows, slots = observed.shape
     matrix = jnp.zeros((40, SRC_DEV), F32)
     for row in range(rows):
@@ -828,13 +829,11 @@
 
 def final_kernel(
     axis, line, bundle, other, table, scale, ids, units, observed, parts, explained,
-    cal_out, attitude_out, resid_out, new_cal, sem,
+    cal_out, attitude_out, resid_out,
 ):
     rows = parts.shape[0]
     table_t = table[...] + (bundle[:LANES] + other[:LANES]) * scale[...]
-    new_cal[...] = table_t.T
-    copy = pltpu.make_async_copy(new_cal, cal_out, sem)
-    copy.start()
+    cal_out[...] = table_t.T
     picked = pick_from(table_t, flat(ids[...]), units[...], rows)
     me = lax.axis_index(line)
     lines = both_halves(axis, bundle, other, rows // PIECE)
@@ -844,21 +843,20 @@
         at = slice(row, row + 1)
         resid_out[at] = observed[at] - model_of(lines[row], parts[row]) - picked[row] - explained[at]
     attitude_out[...] = own
-    copy.wait()
 
 
 VMEM = pl.BlockSpec(memory_space=pltpu.VMEM)
 ANY = pl.BlockSpec(memory_space=pltpu.HBM)
 
 
-def call(kernel, outs, *args, away=0, scratch=(), specs=None):
+def call(kernel, outs, *args, away=0, scratch=()):
     near = args[: len(args) - away]
     far = [pltpu.with_memory_space_constraint(arg, pltpu.HBM) for arg in args[len(args) - away :]]
     return pl.pallas_call(
         kernel,
         out_shape=outs,
         in_specs=[VMEM] * len(near) + [ANY] * away,
-        out_specs=specs or [VMEM] * len(outs),
+        out_specs=[VMEM] * len(outs),
         scratch_shapes=scratch,
         compiler_params=pltpu.CompilerParams(vmem_limit_bytes=VMEM_BYTES),
     )(*near, *far)
@@ -925,8 +923,7 @@
     values, received = lax.optimization_barrier((values, received))
     values = exchange(values)
     (weights,) = call(weights_kernel, [leave(LANES, HIGH)], received)
-    weights, received = lax.optimization_barrier((weights, received))
-    other_weights = swap(weights)
+    other_weights, received = lax.optimization_barrier((swap(weights), received))
     bundle, lines = call(
         functools.partial(solve_kernel, "src"),
         [leave(LANES + SUB, HIGH), stay(half, WIDTH, WIDTH)],
@@ -950,8 +947,6 @@
         functools.partial(final_kernel, "src", "tm"),
         [leave(HIGH, LANES), leave(1, WIDTH), leave(rows, slots)],
         bundle, swap(bundle), table, scale, cal_id, units, seen, parts, explained,
-        scratch=[pltpu.VMEM((HIGH, LANES), F32), pltpu.SemaphoreType.DMA],
-        specs=[ANY, VMEM, VMEM],
     )
     return (params, now.reshape(WIDTH), cal.reshape(CAL), final)
 

time: 54 us -> 53.1 us (0.983)
  Pallas kernels: 17 us -> 16.2 us
    ppermute x3, waiting for transfers between devices: 2.39 us -> 3.94 us  [swap(): lax.ppermute(value, 'src', [(at, at ^ 1) for at in range(lax.axis_size('s...]
    all_to_all x2, waiting for transfers between devices: 13.3 us -> 11.9 us  [exchange(): return lax.all_to_all(value, ('src', 'tm'), 0, 0, tiled=True)]
    pallas_call x8, Pallas kernels: 17 us -> 16.2 us  [call(): pl.pallas_call(kernel, out_shape=outs, in_specs=[VMEM] * len(near) + [ANY...]
  transfers between devices with their start and end apart: 5 -> 5, of which waited for: 4 -> 5; matrix products, arithmetic and copies ran while one was open for 0% -> 0% of each run, Pallas kernels for 7% -> 7%
where the time goes in v8:
time: 53.1 us; the launch traced here: 52.6 us
  Pallas kernels  16.2 us (31%)
  waiting for transfers between devices  15.9 us (30%)
  starting transfers between devices  10.2 us (19%)
  blocking collectives  9.62 us (18%)
  between operations  0.7 us (1%)
    pallas_call x8, Pallas kernels, call(): pl.pallas_call(kernel, out_shape=outs, in_specs=[VMEM] * len(near) + [ANY...  16.2 us
    all_to_all x2, waiting for transfers between devices, exchange(): return lax.all_to_all(value, ('src', 'tm'), 0, 0, tiled=True)  11.9 us
    all_to_all x2, starting transfers between devices, exchange(): return lax.all_to_all(value, ('src', 'tm'), 0, 0, tiled=True)  9.87 us
    all_to_all x1, blocking collectives, exchange(): return lax.all_to_all(value, ('src', 'tm'), 0, 0, tiled=True)  9.62 us
    ppermute x3, waiting for transfers between devices, swap(): lax.ppermute(value, 'src', [(at, at ^ 1) for at in range(lax.axis_size('s...  3.94 us
  transfers between devices with their start and end apart: 5, of which 5 were waited for; matrix products, arithmetic and copies ran while one was open for 0% of the time, Pallas kernels for 7%

profile of v8, /device:TPU:0, one launch (start us, length us, event | category | flops | bytes accessed | tf_op | source)
XLA Modules:
  0.0 52.6 jit_solution(13604349055846365082)
XLA Ops:
  0.6 2.4 %shard_map.138 = (f32[32,11,1,128]{3,2,1,0:T(1,128)}, f32[4,128,256]{2,1,0:T(8,128)S(1)}, f32[4,256]{1,0:T(4,128)S(1)}, s32[4,256]{1,0:T(4,128)S(1)}) custom-call(f32[4,256]{1,0:T(4,128)} %weight_in.1, s32[4,256]{1,0:T(4,128)} %present_in.1, f32[4,4,256]{2,1,0:T(4,128)} %attitude_in.1, f32[4,256]{1,0:T(4,128)} %phase_in.1, s32[4,256]{1,0:T(4,128)} %knot_in.1, ...), custom_call_target="tpu_custom_call" | custom-call | tf_op jit(solution)/shard_map/pallas_call | solution.py:855
  3.1 7.3 %all-to-all-start = ((f32[32,11,1,128]{3,2,1,0:T(1,128)}), f32[32,11,1,128]{3,2,1,0:T(1,128)S(1)}, u32[]{:S(2)}, u32[]{:S(2)}) async-start(f32[32,11,1,128]{3,2,1,0:T(1,128)} %get-tuple-element.32), calls=%async_computation | async-start | bytes 360448 | tf_op jit(solution)/shard_map/all_to_all | solution.py:878
  10.4 1.5 %shard_map.139 = (f32[4,8,256]{2,1,0:T(8,128)S(1)}, f32[16,128]{1,0:T(8,128)S(1)}, f32[4,256]{1,0:T(4,128)S(1)}, f32[128,256]{1,0:T(8,128)S(1)}, bf16[4,128,256]...) custom-call(s32[4,256]{1,0:T(4,128)S(1)} %get-tuple-element.33.cal_i, ...), custom_call_target="tpu_custom_call" | custom-call | tf_op jit(solution)/shard_map/pallas_call | solution.py:855
  11.9 7.5 %all-to-all-done.received = f32[32,11,1,128]{3,2,1,0:T(1,128)S(1)} async-done(((f32[32,11,1,128]{3,2,1,0:T(1,128)}), f32[32,11,1,128]{3,2,1,0:T(1,128)S(1)}, u32[]{:S(2)}, u32[]{:S(2)}) %all-to-all-start) | async-done | bytes 180256 | tf_op jit(solution)/shard_map/all_to_all | solution.py:878
  19.5 1.4 %shard_map.140 = f32[32,7,1,128]{3,2,1,0:T(1,128)} custom-call(f32[32,11,1,128]{3,2,1,0:T(1,128)S(1)} %all-to-all-done.received, f32[4,256]{1,0:T(4,128)S(1)} %get-tuple-element.38.target, bf16[4,256,256]{2,1,0:T(8,128)(2,1)S(1)} %get-tuple-element.39.parts, f32[4,8,256]{2,1,0:T(8,128)S(1)} %get-tuple-element.40.partials, ...), custom_call_target="tpu_custom_call" | custom-call | tf_op jit(solution)/shard_map/pallas_call | solution.py:855
  20.8 2.6 %all-to-all-start.1 = ((f32[32,7,1,128]{3,2,1,0:T(1,128)}), f32[32,7,1,128]{3,2,1,0:T(1,128)S(1)}, u32[]{:S(2)}, u32[]{:S(2)}) async-start(f32[32,7,1,128]{3,2,1,0:T(1,128)} %shard_map.140), calls=%async_computation.1 | async-start | bytes 229376 | tf_op jit(solution)/shard_map/all_to_all | solution.py:878
  23.4 2.4 %shard_map.141.weights = f32[128,256]{1,0:T(8,128)S(1)} custom-call(f32[32,11,1,128]{3,2,1,0:T(1,128)S(1)} %all-to-all-done.received), custom_call_target="tpu_custom_call" | custom-call | tf_op jit(solution)/shard_map/pallas_call | solution.py:855
  25.8 0.2 collective-permute-start
  26.0 1.2 %collective-permute-done.other_weights = f32[128,256]{1,0:T(8,128)S(1)} collective-permute-done((f32[128,256]{1,0:T(8,128)S(1)}, f32[128,256]{1,0:T(8,128)S(1)}, u32[]{:S(2)}, u32[]{:S(2)}) %collective-permute-start) | collective-permute-done | bytes 131104 | tf_op jit(solution)/shard_map/ppermute | solution.py:874
  27.2 4.4 %all-to-all-done.1.values = f32[32,7,1,128]{3,2,1,0:T(1,128)S(1)} async-done(((f32[32,7,1,128]{3,2,1,0:T(1,128)}), f32[32,7,1,128]{3,2,1,0:T(1,128)S(1)}, u32[]{:S(2)}, u32[]{:S(2)}) %all-to-all-start.1) | async-done | bytes 114720 | tf_op jit(solution)/shard_map/all_to_all | solution.py:878
  31.6 3.8 %shard_map.142 = (f32[136,256]{1,0:T(8,128)S(1)}, f32[2,128,128]{2,1,0:T(8,128)S(1)}) custom-call(f32[32,7,1,128]{3,2,1,0:T(1,128)S(1)} %all-to-all-done.1.values, f32[32,11,1,128]{3,2,1,0:T(1,128)S(1)} %all-to-all-done.received), custom_call_target="tpu_custom_call" | custom-call | tf_op jit(solution)/shard_map/pallas_call | solution.py:855
  35.4 0.1 collective-permute-start.1
  35.5 1.3 %collective-permute-done.1.other = f32[136,256]{1,0:T(8,128)S(1)} collective-permute-done((f32[136,256]{1,0:T(8,128)S(1)}, f32[136,256]{1,0:T(8,128)S(1)}, u32[]{:S(2)}, u32[]{:S(2)}) %collective-permute-start.1) | collective-permute-done | bytes 139296 | tf_op jit(solution)/shard_map/ppermute | solution.py:874
  36.9 1.3 %shard_map.143 = (f32[32,6,1,128]{3,2,1,0:T(1,128)S(1)}, f32[5,128]{1,0:T(8,128)}, f32[4,256]{1,0:T(4,128)S(1)}, f32[128,256]{1,0:T(8,128)S(1)}, f32[128,256]{1,0:T(8,128)S(1)}) custom-call(f32[136,256]{1,0:T(8,128)S(1)} %get-tuple-element.46.bundle, f32[136,256]{1,0:T(8,128)S(1)} %collective-permute-done.1.other, f32[128,256]{1,0:T(8,128)S(1)} %shard_map.141.weights, ...), custom_call_target="tpu_custom_call" | custom-call | tf_op jit(solution)/shard_map/pallas_call | solution.py:855
  38.2 9.6 %all_to_all.15.values = f32[32,6,1,128]{3,2,1,0:T(1,128)S(1)} all-to-all(f32[32,6,1,128]{3,2,1,0:T(1,128)S(1)} %get-tuple-element.52), channel_id=1, replica_groups=mesh['src'=8,'tm'=4] {'src','tm'}, dimensions={0} | all-to-all | bytes 196608 | tf_op jit(solution)/shard_map/all_to_all | solution.py:878
  47.8 2.4 %shard_map.144.bundle = f32[136,256]{1,0:T(8,128)S(1)} custom-call(f32[32,6,1,128]{3,2,1,0:T(1,128)S(1)} %all_to_all.15.values, f32[32,11,1,128]{3,2,1,0:T(1,128)S(1)} %all-to-all-done.received, f32[136,256]{1,0:T(8,128)S(1)} %get-tuple-element.46.bundle, f32[2,128,128]{2,1,0:T(8,128)S(1)} %get-tuple-element.53.lines), custom_call_target="tpu_custom_call" | custom-call | tf_op jit(solution)/shard_map/pallas_call | solution.py:855
  50.2 0.1 collective-permute-start.2
  50.3 1.3 %collective-permute-done.2.other = f32[136,256]{1,0:T(8,128)S(1)} collective-permute-done((f32[136,256]{1,0:T(8,128)S(1)}, f32[136,256]{1,0:T(8,128)S(1)}, u32[]{:S(2)}, u32[]{:S(2)}) %collective-permute-start.2) | collective-permute-done | bytes 139296 | tf_op jit(solution)/shard_map/ppermute | solution.py:874
  51.6 1.0 %shard_map.145 = (f32[256,128]{1,0:T(8,128)}, f32[1,128]{1,0:T(1,128)}, f32[4,256]{1,0:T(4,128)}) custom-call(f32[136,256]{1,0:T(8,128)S(1)} %shard_map.144.bundle, f32[136,256]{1,0:T(8,128)S(1)} %collective-permute-done.2.other, f32[128,256]{1,0:T(8,128)S(1)} %get-tuple-element.54.table, f32[128,256]{1,0:T(8,128)S(1)} %get-tuple-element.55.scale, ...), custom_call_target="tpu_custom_call" | custom-call | tf_op jit(solution)/shard_map/pallas_call | solution.py:855
Async XLA Ops:
  3.1 16.4 %all-to-all-start = ((f32[32,11,1,128]{3,2,1,0:T(1,128)}), f32[32,11,1,128]{3,2,1,0:T(1,128)S(1)}, u32[]{:S(2)}, u32[]{:S(2)}) async-start(f32[32,11,1,128]{3,2,1,0:T(1,128)} %get-tuple-element.32), calls=%async_computation | async-start | bytes 360448 | tf_op jit(solution)/shard_map/all_to_all | solution.py:878
  20.8 10.8 %all-to-all-start.1 = ((f32[32,7,1,128]{3,2,1,0:T(1,128)}), f32[32,7,1,128]{3,2,1,0:T(1,128)S(1)}, u32[]{:S(2)}, u32[]{:S(2)}) async-start(f32[32,7,1,128]{3,2,1,0:T(1,128)} %shard_map.140), calls=%async_computation.1 | async-start | bytes 229376 | tf_op jit(solution)/shard_map/all_to_all | solution.py:878
  25.8 1.4 %collective-permute-start = (f32[128,256]{1,0:T(8,128)S(1)}, f32[128,256]{1,0:T(8,128)S(1)}, u32[]{:S(2)}, u32[]{:S(2)}) collective-permute-start(f32[128,256]{1,0:T(8,128)S(1)} %shard_map.141.weights), channel_id=1, source_target_pairs={{0,4},{4,0},{8,12},{12,8},{16,20},{20,16},{24,28},{28,24},{1,5},{5... | collective-permute-start | bytes 393224 | tf_op jit(solution)/shard_map/ppermute | solution.py:874
  35.4 1.4 %collective-permute-start.1 = (f32[136,256]{1,0:T(8,128)S(1)}, f32[136,256]{1,0:T(8,128)S(1)}, u32[]{:S(2)}, u32[]{:S(2)}) collective-permute-start(f32[136,256]{1,0:T(8,128)S(1)} %get-tuple-element.46.bundle), channel_id=1, source_target_pairs={{0,4},{4,0},{8,12},{12,8},{16,20},{20,16},{24,28},{28,24},{1,5},{5... | collective-permute-start | bytes 417800 | tf_op jit(solution)/shard_map/ppermute | solution.py:874
  50.2 1.4 %collective-permute-start.2 = (f32[136,256]{1,0:T(8,128)S(1)}, f32[136,256]{1,0:T(8,128)S(1)}, u32[]{:S(2)}, u32[]{:S(2)}) collective-permute-start(f32[136,256]{1,0:T(8,128)S(1)} %shard_map.144.bundle), channel_id=1, source_target_pairs={{0,4},{4,0},{8,12},{12,8},{16,20},{20,16},{24,28},{28,24},{1,5},{5... | collective-permute-start | bytes 417800 | tf_op jit(solution)/shard_map/ppermute | solution.py:874

commit v9 on v8

--- a/solution.py
+++ b/solution.py
@@ -186,25 +186,25 @@
     ]
 
 
-def eliminate(matrix, right, lines_out):
+def eliminate(state, entries, right, lines_out):
     shape = (8, WIDTH)
-    tiles = [matrix[8 * tile : 8 * tile + 8] for tile in range(WIDTH // 8)]
     lane = iota(shape, 1)
     for step in PLAN:
-        held = list(tiles)
-        border = right
-        for knot, reach in step:
+        works = []
+        for slot, (knot, reach) in enumerate(step):
             at, sub, first = knot // 2, 4 * (knot % 2), 4 * knot
             inside = lane // 4 == knot
-            columns = {
-                tile: [
-                    jnp.broadcast_to(held[tile][:, first + index : first + index + 1], shape)
+            columns = {}
+            for tile in sorted({at, *reach}):
+                held = state[8 * tile : 8 * tile + 8]
+                columns[tile] = [
+                    jnp.broadcast_to(held[:, first + index : first + index + 1], shape)
                     for index in range(4)
                 ]
-                for tile in sorted({at, *reach})
-            }
+            for index in range(4):
+                entries[slot, index] = columns[at][index]
             entry = {
-                (one, two): jnp.broadcast_to(columns[at][two][sub + one : sub + one + 1], shape)
+                (one, two): jnp.broadcast_to(entries[slot, two, sub + one : sub + one + 1], shape)
                 for one in range(4)
                 for two in range(one, 4)
             }
@@ -212,18 +212,21 @@
                 jnp.where(
                     inside,
                     jnp.where(lane == first + index, -1.0, 0.0),
-                    jnp.broadcast_to(held[at][sub + index : sub + index + 1], shape),
+                    jnp.broadcast_to(state[first + index : first + index + 1], shape),
                 )
                 for index in range(4)
             ]
-            lines = block_rows(entry, lines)
+            works.append((knot, reach, inside, columns, block_rows(entry, lines)))
+        border = right
+        for knot, reach, inside, columns, lines in works:
             for index in range(4):
-                lines_out[first + index : first + index + 1] = lines[index][0:1]
+                lines_out[4 * knot + index : 4 * knot + index + 1] = lines[index][0:1]
             for tile in reach:
                 factors = columns[tile]
                 taken = factors[0] * lines[0] + factors[1] * lines[1]
                 taken = taken + (factors[2] * lines[2] + factors[3] * lines[3])
-                tiles[tile] = jnp.where(inside, 0.0, tiles[tile]) - taken
+                rows = slice(8 * tile, 8 * tile + 8)
+                state[rows] = jnp.where(inside, 0.0, state[rows]) - taken
             right = swept(right, border, knot, [line[0:1] for line in lines])
         yield
     return right
@@ -761,7 +764,7 @@
     bundle[LANES + place : LANES + place + 1] = jnp.concatenate([line, line], axis=1)
 
 
-def solve_kernel(axis, values, received, bundle_out, lines_out, bands):
+def solve_kernel(axis, values, received, bundle_out, lines_out, bands, states, entries):
     half = lines_out.shape[0]
     rows = values.shape[1] - half - 1
     for device in range(values.shape[0]):
@@ -769,8 +772,13 @@
     bundle_out[LANES:] = jnp.zeros((SUB, HIGH), F32)
 
     def attitude(place):
-        matrix = matrix_of(bands[BAND * place : BAND * (place + 1)])
-        change = yield from eliminate(matrix, right_side(values, rows + place), lines_out.at[place])
+        states[place] = matrix_of(bands[BAND * place : BAND * (place + 1)])
+        change = yield from eliminate(
+            states.at[place],
+            entries.at[place],
+            right_side(values, rows + place),
+            lines_out.at[place],
+        )
         start = received[half * core(axis) + place, received.shape[1] - 1]
         put(bundle_out, place, start + change)
         yield
@@ -928,7 +936,10 @@
         functools.partial(solve_kernel, "src"),
         [leave(LANES + SUB, HIGH), stay(half, WIDTH, WIDTH)],
         values, received,
-        scratch=[pltpu.VMEM((half * BAND, WIDTH), F32)],
+        scratch=[
+            pltpu.VMEM((half * BAND, WIDTH), F32), pltpu.VMEM((half, WIDTH, WIDTH), F32),
+            pltpu.VMEM((half, len(PLAN[0]), 4, 8, WIDTH), F32),
+        ],
     )
     values, params, explained, table, scale = call(
         functools.partial(second_kernel, "src"),

time: 53.1 us -> 52.3 us (0.985)
  Pallas kernels: 16.2 us -> 15.5 us
    pallas_call x8, Pallas kernels: 16.2 us -> 15.5 us  [call(): pl.pallas_call(kernel, out_shape=outs, in_specs=[VMEM] * len(near) + [ANY...]
  transfers between devices with their start and end apart: 5 -> 5, of which waited for: 5 -> 5; matrix products, arithmetic and copies ran while one was open for 0% -> 0% of each run, Pallas kernels for 7% -> 8%
where the time goes in v9:
time: 52.3 us; the launch traced here: 51.8 us
  waiting for transfers between devices  15.9 us (30%)
  Pallas kernels  15.5 us (30%)
  starting transfers between devices  10.2 us (20%)
  blocking collectives  9.62 us (18%)
  between operations  0.7 us (1%)
    pallas_call x8, Pallas kernels, call(): pl.pallas_call(kernel, out_shape=outs, in_specs=[VMEM] * len(near) + [ANY...  15.5 us
    all_to_all x2, waiting for transfers between devices, exchange(): return lax.all_to_all(value, ('src', 'tm'), 0, 0, tiled=True)  11.9 us
    all_to_all x2, starting transfers between devices, exchange(): return lax.all_to_all(value, ('src', 'tm'), 0, 0, tiled=True)  9.87 us
    all_to_all x1, blocking collectives, exchange(): return lax.all_to_all(value, ('src', 'tm'), 0, 0, tiled=True)  9.62 us
    ppermute x3, waiting for transfers between devices, swap(): lax.ppermute(value, 'src', [(at, at ^ 1) for at in range(lax.axis_size('s...  3.94 us
  transfers between devices with their start and end apart: 5, of which 5 were waited for; matrix products, arithmetic and copies ran while one was open for 0% of the time, Pallas kernels for 8%

profile of v9, /device:TPU:0, one launch (start us, length us, event | category | flops | bytes accessed | tf_op | source)
XLA Modules:
  0.0 51.8 jit_solution(3093807889949161656)
XLA Ops:
  0.6 2.4 %shard_map.138 = (f32[32,11,1,128]{3,2,1,0:T(1,128)}, f32[4,128,256]{2,1,0:T(8,128)S(1)}, f32[4,256]{1,0:T(4,128)S(1)}, s32[4,256]{1,0:T(4,128)S(1)}) custom-call(f32[4,256]{1,0:T(4,128)} %weight_in.1, s32[4,256]{1,0:T(4,128)} %present_in.1, f32[4,4,256]{2,1,0:T(4,128)} %attitude_in.1, f32[4,256]{1,0:T(4,128)} %phase_in.1, s32[4,256]{1,0:T(4,128)} %knot_in.1, ...), custom_call_target="tpu_custom_call" | custom-call | tf_op jit(solution)/shard_map/pallas_call | solution.py:863
  3.1 7.3 %all-to-all-start = ((f32[32,11,1,128]{3,2,1,0:T(1,128)}), f32[32,11,1,128]{3,2,1,0:T(1,128)S(1)}, u32[]{:S(2)}, u32[]{:S(2)}) async-start(f32[32,11,1,128]{3,2,1,0:T(1,128)} %get-tuple-element.32), calls=%async_computation | async-start | bytes 360448 | tf_op jit(solution)/shard_map/all_to_all | solution.py:886
  10.4 1.5 %shard_map.139 = (f32[4,8,256]{2,1,0:T(8,128)S(1)}, f32[16,128]{1,0:T(8,128)S(1)}, f32[4,256]{1,0:T(4,128)S(1)}, f32[128,256]{1,0:T(8,128)S(1)}, bf16[4,128,256]...) custom-call(s32[4,256]{1,0:T(4,128)S(1)} %get-tuple-element.33.cal_i, ...), custom_call_target="tpu_custom_call" | custom-call | tf_op jit(solution)/shard_map/pallas_call | solution.py:863
  11.9 7.5 %all-to-all-done.received = f32[32,11,1,128]{3,2,1,0:T(1,128)S(1)} async-done(((f32[32,11,1,128]{3,2,1,0:T(1,128)}), f32[32,11,1,128]{3,2,1,0:T(1,128)S(1)}, u32[]{:S(2)}, u32[]{:S(2)}) %all-to-all-start) | async-done | bytes 180256 | tf_op jit(solution)/shard_map/all_to_all | solution.py:886
  19.5 1.4 %shard_map.140 = f32[32,7,1,128]{3,2,1,0:T(1,128)} custom-call(f32[32,11,1,128]{3,2,1,0:T(1,128)S(1)} %all-to-all-done.received, f32[4,256]{1,0:T(4,128)S(1)} %get-tuple-element.38.target, bf16[4,256,256]{2,1,0:T(8,128)(2,1)S(1)} %get-tuple-element.39.parts, f32[4,8,256]{2,1,0:T(8,128)S(1)} %get-tuple-element.40.partials, ...), custom_call_target="tpu_custom_call" | custom-call | tf_op jit(solution)/shard_map/pallas_call | solution.py:863
  20.8 2.6 %all-to-all-start.1 = ((f32[32,7,1,128]{3,2,1,0:T(1,128)}), f32[32,7,1,128]{3,2,1,0:T(1,128)S(1)}, u32[]{:S(2)}, u32[]{:S(2)}) async-start(f32[32,7,1,128]{3,2,1,0:T(1,128)} %shard_map.140), calls=%async_computation.1 | async-start | bytes 229376 | tf_op jit(solution)/shard_map/all_to_all | solution.py:886
  23.4 2.4 %shard_map.141.weights = f32[128,256]{1,0:T(8,128)S(1)} custom-call(f32[32,11,1,128]{3,2,1,0:T(1,128)S(1)} %all-to-all-done.received), custom_call_target="tpu_custom_call" | custom-call | tf_op jit(solution)/shard_map/pallas_call | solution.py:863
  25.8 0.2 collective-permute-start
  26.0 1.2 %collective-permute-done.other_weights = f32[128,256]{1,0:T(8,128)S(1)} collective-permute-done((f32[128,256]{1,0:T(8,128)S(1)}, f32[128,256]{1,0:T(8,128)S(1)}, u32[]{:S(2)}, u32[]{:S(2)}) %collective-permute-start) | collective-permute-done | bytes 131104 | tf_op jit(solution)/shard_map/ppermute | solution.py:882
  27.2 4.4 %all-to-all-done.1.values = f32[32,7,1,128]{3,2,1,0:T(1,128)S(1)} async-done(((f32[32,7,1,128]{3,2,1,0:T(1,128)}), f32[32,7,1,128]{3,2,1,0:T(1,128)S(1)}, u32[]{:S(2)}, u32[]{:S(2)}) %all-to-all-start.1) | async-done | bytes 114720 | tf_op jit(solution)/shard_map/all_to_all | solution.py:886
  31.6 3.1 %shard_map.142 = (f32[136,256]{1,0:T(8,128)S(1)}, f32[2,128,128]{2,1,0:T(8,128)S(1)}) custom-call(f32[32,7,1,128]{3,2,1,0:T(1,128)S(1)} %all-to-all-done.1.values, f32[32,11,1,128]{3,2,1,0:T(1,128)S(1)} %all-to-all-done.received), custom_call_target="tpu_custom_call" | custom-call | tf_op jit(solution)/shard_map/pallas_call | solution.py:863
  34.7 0.1 collective-permute-start.1
  34.8 1.3 %collective-permute-done.1.other = f32[136,256]{1,0:T(8,128)S(1)} collective-permute-done((f32[136,256]{1,0:T(8,128)S(1)}, f32[136,256]{1,0:T(8,128)S(1)}, u32[]{:S(2)}, u32[]{:S(2)}) %collective-permute-start.1) | collective-permute-done | bytes 139296 | tf_op jit(solution)/shard_map/ppermute | solution.py:882
  36.1 1.3 %shard_map.143 = (f32[32,6,1,128]{3,2,1,0:T(1,128)S(1)}, f32[5,128]{1,0:T(8,128)}, f32[4,256]{1,0:T(4,128)S(1)}, f32[128,256]{1,0:T(8,128)S(1)}, f32[128,256]{1,0:T(8,128)S(1)}) custom-call(f32[136,256]{1,0:T(8,128)S(1)} %get-tuple-element.46.bundle, f32[136,256]{1,0:T(8,128)S(1)} %collective-permute-done.1.other, f32[128,256]{1,0:T(8,128)S(1)} %shard_map.141.weights, ...), custom_call_target="tpu_custom_call" | custom-call | tf_op jit(solution)/shard_map/pallas_call | solution.py:863
  37.4 9.6 %all_to_all.15.values = f32[32,6,1,128]{3,2,1,0:T(1,128)S(1)} all-to-all(f32[32,6,1,128]{3,2,1,0:T(1,128)S(1)} %get-tuple-element.52), channel_id=1, replica_groups=mesh['src'=8,'tm'=4] {'src','tm'}, dimensions={0} | all-to-all | bytes 196608 | tf_op jit(solution)/shard_map/all_to_all | solution.py:886
  47.1 2.4 %shard_map.144.bundle = f32[136,256]{1,0:T(8,128)S(1)} custom-call(f32[32,6,1,128]{3,2,1,0:T(1,128)S(1)} %all_to_all.15.values, f32[32,11,1,128]{3,2,1,0:T(1,128)S(1)} %all-to-all-done.received, f32[136,256]{1,0:T(8,128)S(1)} %get-tuple-element.46.bundle, f32[2,128,128]{2,1,0:T(8,128)S(1)} %get-tuple-element.53.lines), custom_call_target="tpu_custom_call" | custom-call | tf_op jit(solution)/shard_map/pallas_call | solution.py:863
  49.4 0.1 collective-permute-start.2
  49.5 1.3 %collective-permute-done.2.other = f32[136,256]{1,0:T(8,128)S(1)} collective-permute-done((f32[136,256]{1,0:T(8,128)S(1)}, f32[136,256]{1,0:T(8,128)S(1)}, u32[]{:S(2)}, u32[]{:S(2)}) %collective-permute-start.2) | collective-permute-done | bytes 139296 | tf_op jit(solution)/shard_map/ppermute | solution.py:882
  50.9 1.0 %shard_map.145 = (f32[256,128]{1,0:T(8,128)}, f32[1,128]{1,0:T(1,128)}, f32[4,256]{1,0:T(4,128)}) custom-call(f32[136,256]{1,0:T(8,128)S(1)} %shard_map.144.bundle, f32[136,256]{1,0:T(8,128)S(1)} %collective-permute-done.2.other, f32[128,256]{1,0:T(8,128)S(1)} %get-tuple-element.54.table, f32[128,256]{1,0:T(8,128)S(1)} %get-tuple-element.55.scale, ...), custom_call_target="tpu_custom_call" | custom-call | tf_op jit(solution)/shard_map/pallas_call | solution.py:863
Async XLA Ops:
  3.1 16.4 %all-to-all-start = ((f32[32,11,1,128]{3,2,1,0:T(1,128)}), f32[32,11,1,128]{3,2,1,0:T(1,128)S(1)}, u32[]{:S(2)}, u32[]{:S(2)}) async-start(f32[32,11,1,128]{3,2,1,0:T(1,128)} %get-tuple-element.32), calls=%async_computation | async-start | bytes 360448 | tf_op jit(solution)/shard_map/all_to_all | solution.py:886
  20.8 10.8 %all-to-all-start.1 = ((f32[32,7,1,128]{3,2,1,0:T(1,128)}), f32[32,7,1,128]{3,2,1,0:T(1,128)S(1)}, u32[]{:S(2)}, u32[]{:S(2)}) async-start(f32[32,7,1,128]{3,2,1,0:T(1,128)} %shard_map.140), calls=%async_computation.1 | async-start | bytes 229376 | tf_op jit(solution)/shard_map/all_to_all | solution.py:886
  25.8 1.4 %collective-permute-start = (f32[128,256]{1,0:T(8,128)S(1)}, f32[128,256]{1,0:T(8,128)S(1)}, u32[]{:S(2)}, u32[]{:S(2)}) collective-permute-start(f32[128,256]{1,0:T(8,128)S(1)} %shard_map.141.weights), channel_id=1, source_target_pairs={{0,4},{4,0},{8,12},{12,8},{16,20},{20,16},{24,28},{28,24},{1,5},{5... | collective-permute-start | bytes 393224 | tf_op jit(solution)/shard_map/ppermute | solution.py:882
  34.7 1.4 %collective-permute-start.1 = (f32[136,256]{1,0:T(8,128)S(1)}, f32[136,256]{1,0:T(8,128)S(1)}, u32[]{:S(2)}, u32[]{:S(2)}) collective-permute-start(f32[136,256]{1,0:T(8,128)S(1)} %get-tuple-element.46.bundle), channel_id=1, source_target_pairs={{0,4},{4,0},{8,12},{12,8},{16,20},{20,16},{24,28},{28,24},{1,5},{5... | collective-permute-start | bytes 417800 | tf_op jit(solution)/shard_map/ppermute | solution.py:882
  49.4 1.4 %collective-permute-start.2 = (f32[136,256]{1,0:T(8,128)S(1)}, f32[136,256]{1,0:T(8,128)S(1)}, u32[]{:S(2)}, u32[]{:S(2)}) collective-permute-start(f32[136,256]{1,0:T(8,128)S(1)} %shard_map.144.bundle), channel_id=1, source_target_pairs={{0,4},{4,0},{8,12},{12,8},{16,20},{20,16},{24,28},{28,24},{1,5},{5... | collective-permute-start | bytes 417800 | tf_op jit(solution)/shard_map/ppermute | solution.py:882

commit v10 on v9

--- a/solution.py
+++ b/solution.py
@@ -683,8 +683,12 @@
         send_out[device, send_out.shape[1] - 1] = totals[core_of(device, rows)]
 
 
-def wide(row, count):
-    tile = jnp.broadcast_to(row, (16, LANES)).astype(BF16)
+def spread(line):
+    return jnp.broadcast_to(line, (SUB, LANES))
+
+
+def wide(tile, count):
+    tile = jnp.concatenate([tile, tile], axis=0).astype(BF16)
     return jnp.concatenate([tile] * (count // 16), axis=0)
 
 
@@ -697,10 +701,10 @@
         lefts, rights = [], []
         for device in (begin, begin + 1):
             for index in range(rows):
-                unit = received[device, PIECE + index]
+                unit = spread(received[device, PIECE + index])
                 high = jnp.floor(unit * (1.0 / LANES))
                 hit = low_row == wide(unit - LANES * high, LANES)
-                value = value_of(device, index)
+                value = spread(value_of(device, index))
                 first = value.astype(BF16).astype(F32)
                 lefts.append(
                     jnp.concatenate(

time: 52.3 us -> 52.2 us (level)
  no operation moved by 1% of the time
where the time goes in v10:
time: 52.2 us; the launch traced here: 51.8 us
  waiting for transfers between devices  15.9 us (30%)
  Pallas kernels  15.4 us (30%)
  starting transfers between devices  10.2 us (20%)
  blocking collectives  9.62 us (18%)
  between operations  0.7 us (1%)
    pallas_call x8, Pallas kernels, call(): pl.pallas_call(kernel, out_shape=outs, in_specs=[VMEM] * len(near) + [ANY...  15.4 us
    all_to_all x2, waiting for transfers between devices, exchange(): return lax.all_to_all(value, ('src', 'tm'), 0, 0, tiled=True)  11.9 us
    all_to_all x2, starting transfers between devices, exchange(): return lax.all_to_all(value, ('src', 'tm'), 0, 0, tiled=True)  9.87 us
    all_to_all x1, blocking collectives, exchange(): return lax.all_to_all(value, ('src', 'tm'), 0, 0, tiled=True)  9.62 us
    ppermute x3, waiting for transfers between devices, swap(): lax.ppermute(value, 'src', [(at, at ^ 1) for at in range(lax.axis_size('s...  3.94 us
  transfers between devices with their start and end apart: 5, of which 5 were waited for; matrix products, arithmetic and copies ran while one was open for 0% of the time, Pallas kernels for 8%

profile of v10, /device:TPU:0, one launch (start us, length us, event | category | flops | bytes accessed | tf_op | source)
XLA Modules:
  0.0 51.8 jit_solution(8745821201017488464)
XLA Ops:
  0.6 2.4 %shard_map.138 = (f32[32,11,1,128]{3,2,1,0:T(1,128)}, f32[4,128,256]{2,1,0:T(8,128)S(1)}, f32[4,256]{1,0:T(4,128)S(1)}, s32[4,256]{1,0:T(4,128)S(1)}) custom-call(f32[4,256]{1,0:T(4,128)} %weight_in.1, s32[4,256]{1,0:T(4,128)} %present_in.1, f32[4,4,256]{2,1,0:T(4,128)} %attitude_in.1, f32[4,256]{1,0:T(4,128)} %phase_in.1, s32[4,256]{1,0:T(4,128)} %knot_in.1, ...), custom_call_target="tpu_custom_call" | custom-call | tf_op jit(solution)/shard_map/pallas_call | solution.py:867
  3.1 7.3 %all-to-all-start = ((f32[32,11,1,128]{3,2,1,0:T(1,128)}), f32[32,11,1,128]{3,2,1,0:T(1,128)S(1)}, u32[]{:S(2)}, u32[]{:S(2)}) async-start(f32[32,11,1,128]{3,2,1,0:T(1,128)} %get-tuple-element.32), calls=%async_computation | async-start | bytes 360448 | tf_op jit(solution)/shard_map/all_to_all | solution.py:890
  10.4 1.5 %shard_map.139 = (f32[4,8,256]{2,1,0:T(8,128)S(1)}, f32[16,128]{1,0:T(8,128)S(1)}, f32[4,256]{1,0:T(4,128)S(1)}, f32[128,256]{1,0:T(8,128)S(1)}, bf16[4,128,256]...) custom-call(s32[4,256]{1,0:T(4,128)S(1)} %get-tuple-element.33.cal_i, ...), custom_call_target="tpu_custom_call" | custom-call | tf_op jit(solution)/shard_map/pallas_call | solution.py:867
  11.9 7.5 %all-to-all-done.received = f32[32,11,1,128]{3,2,1,0:T(1,128)S(1)} async-done(((f32[32,11,1,128]{3,2,1,0:T(1,128)}), f32[32,11,1,128]{3,2,1,0:T(1,128)S(1)}, u32[]{:S(2)}, u32[]{:S(2)}) %all-to-all-start) | async-done | bytes 180256 | tf_op jit(solution)/shard_map/all_to_all | solution.py:890
  19.5 1.4 %shard_map.140 = f32[32,7,1,128]{3,2,1,0:T(1,128)} custom-call(f32[32,11,1,128]{3,2,1,0:T(1,128)S(1)} %all-to-all-done.received, f32[4,256]{1,0:T(4,128)S(1)} %get-tuple-element.38.target, bf16[4,256,256]{2,1,0:T(8,128)(2,1)S(1)} %get-tuple-element.39.parts, f32[4,8,256]{2,1,0:T(8,128)S(1)} %get-tuple-element.40.partials, ...), custom_call_target="tpu_custom_call" | custom-call | tf_op jit(solution)/shard_map/pallas_call | solution.py:867
  20.8 2.6 %all-to-all-start.1 = ((f32[32,7,1,128]{3,2,1,0:T(1,128)}), f32[32,7,1,128]{3,2,1,0:T(1,128)S(1)}, u32[]{:S(2)}, u32[]{:S(2)}) async-start(f32[32,7,1,128]{3,2,1,0:T(1,128)} %shard_map.140), calls=%async_computation.1 | async-start | bytes 229376 | tf_op jit(solution)/shard_map/all_to_all | solution.py:890
  23.4 2.4 %shard_map.141.weights = f32[128,256]{1,0:T(8,128)S(1)} custom-call(f32[32,11,1,128]{3,2,1,0:T(1,128)S(1)} %all-to-all-done.received), custom_call_target="tpu_custom_call" | custom-call | tf_op jit(solution)/shard_map/pallas_call | solution.py:867
  25.8 0.2 collective-permute-start
  26.0 1.2 %collective-permute-done.other_weights = f32[128,256]{1,0:T(8,128)S(1)} collective-permute-done((f32[128,256]{1,0:T(8,128)S(1)}, f32[128,256]{1,0:T(8,128)S(1)}, u32[]{:S(2)}, u32[]{:S(2)}) %collective-permute-start) | collective-permute-done | bytes 131104 | tf_op jit(solution)/shard_map/ppermute | solution.py:886
  27.2 4.4 %all-to-all-done.1.values = f32[32,7,1,128]{3,2,1,0:T(1,128)S(1)} async-done(((f32[32,7,1,128]{3,2,1,0:T(1,128)}), f32[32,7,1,128]{3,2,1,0:T(1,128)S(1)}, u32[]{:S(2)}, u32[]{:S(2)}) %all-to-all-start.1) | async-done | bytes 114720 | tf_op jit(solution)/shard_map/all_to_all | solution.py:890
  31.6 3.0 %shard_map.142 = (f32[136,256]{1,0:T(8,128)S(1)}, f32[2,128,128]{2,1,0:T(8,128)S(1)}) custom-call(f32[32,7,1,128]{3,2,1,0:T(1,128)S(1)} %all-to-all-done.1.values, f32[32,11,1,128]{3,2,1,0:T(1,128)S(1)} %all-to-all-done.received), custom_call_target="tpu_custom_call" | custom-call | tf_op jit(solution)/shard_map/pallas_call | solution.py:867
  34.6 0.1 collective-permute-start.1
  34.7 1.3 %collective-permute-done.1.other = f32[136,256]{1,0:T(8,128)S(1)} collective-permute-done((f32[136,256]{1,0:T(8,128)S(1)}, f32[136,256]{1,0:T(8,128)S(1)}, u32[]{:S(2)}, u32[]{:S(2)}) %collective-permute-start.1) | collective-permute-done | bytes 139296 | tf_op jit(solution)/shard_map/ppermute | solution.py:886
  36.1 1.3 %shard_map.143 = (f32[32,6,1,128]{3,2,1,0:T(1,128)S(1)}, f32[5,128]{1,0:T(8,128)}, f32[4,256]{1,0:T(4,128)S(1)}, f32[128,256]{1,0:T(8,128)S(1)}, f32[128,256]{1,0:T(8,128)S(1)}) custom-call(f32[136,256]{1,0:T(8,128)S(1)} %get-tuple-element.46.bundle, f32[136,256]{1,0:T(8,128)S(1)} %collective-permute-done.1.other, f32[128,256]{1,0:T(8,128)S(1)} %shard_map.141.weights, ...), custom_call_target="tpu_custom_call" | custom-call | tf_op jit(solution)/shard_map/pallas_call | solution.py:867
  37.4 9.6 %all_to_all.15.values = f32[32,6,1,128]{3,2,1,0:T(1,128)S(1)} all-to-all(f32[32,6,1,128]{3,2,1,0:T(1,128)S(1)} %get-tuple-element.52), channel_id=1, replica_groups=mesh['src'=8,'tm'=4] {'src','tm'}, dimensions={0} | all-to-all | bytes 196608 | tf_op jit(solution)/shard_map/all_to_all | solution.py:890
  47.0 2.4 %shard_map.144.bundle = f32[136,256]{1,0:T(8,128)S(1)} custom-call(f32[32,6,1,128]{3,2,1,0:T(1,128)S(1)} %all_to_all.15.values, f32[32,11,1,128]{3,2,1,0:T(1,128)S(1)} %all-to-all-done.received, f32[136,256]{1,0:T(8,128)S(1)} %get-tuple-element.46.bundle, f32[2,128,128]{2,1,0:T(8,128)S(1)} %get-tuple-element.53.lines), custom_call_target="tpu_custom_call" | custom-call | tf_op jit(solution)/shard_map/pallas_call | solution.py:867
  49.4 0.1 collective-permute-start.2
  49.5 1.3 %collective-permute-done.2.other = f32[136,256]{1,0:T(8,128)S(1)} collective-permute-done((f32[136,256]{1,0:T(8,128)S(1)}, f32[136,256]{1,0:T(8,128)S(1)}, u32[]{:S(2)}, u32[]{:S(2)}) %collective-permute-start.2) | collective-permute-done | bytes 139296 | tf_op jit(solution)/shard_map/ppermute | solution.py:886
  50.8 1.0 %shard_map.145 = (f32[256,128]{1,0:T(8,128)}, f32[1,128]{1,0:T(1,128)}, f32[4,256]{1,0:T(4,128)}) custom-call(f32[136,256]{1,0:T(8,128)S(1)} %shard_map.144.bundle, f32[136,256]{1,0:T(8,128)S(1)} %collective-permute-done.2.other, f32[128,256]{1,0:T(8,128)S(1)} %get-tuple-element.54.table, f32[128,256]{1,0:T(8,128)S(1)} %get-tuple-element.55.scale, ...), custom_call_target="tpu_custom_call" | custom-call | tf_op jit(solution)/shard_map/pallas_call | solution.py:867
Async XLA Ops:
  3.1 16.4 %all-to-all-start = ((f32[32,11,1,128]{3,2,1,0:T(1,128)}), f32[32,11,1,128]{3,2,1,0:T(1,128)S(1)}, u32[]{:S(2)}, u32[]{:S(2)}) async-start(f32[32,11,1,128]{3,2,1,0:T(1,128)} %get-tuple-element.32), calls=%async_computation | async-start | bytes 360448 | tf_op jit(solution)/shard_map/all_to_all | solution.py:890
  20.8 10.8 %all-to-all-start.1 = ((f32[32,7,1,128]{3,2,1,0:T(1,128)}), f32[32,7,1,128]{3,2,1,0:T(1,128)S(1)}, u32[]{:S(2)}, u32[]{:S(2)}) async-start(f32[32,7,1,128]{3,2,1,0:T(1,128)} %shard_map.140), calls=%async_computation.1 | async-start | bytes 229376 | tf_op jit(solution)/shard_map/all_to_all | solution.py:890
  25.8 1.4 %collective-permute-start = (f32[128,256]{1,0:T(8,128)S(1)}, f32[128,256]{1,0:T(8,128)S(1)}, u32[]{:S(2)}, u32[]{:S(2)}) collective-permute-start(f32[128,256]{1,0:T(8,128)S(1)} %shard_map.141.weights), channel_id=1, source_target_pairs={{0,4},{4,0},{8,12},{12,8},{16,20},{20,16},{24,28},{28,24},{1,5},{5... | collective-permute-start | bytes 393224 | tf_op jit(solution)/shard_map/ppermute | solution.py:886
  34.6 1.4 %collective-permute-start.1 = (f32[136,256]{1,0:T(8,128)S(1)}, f32[136,256]{1,0:T(8,128)S(1)}, u32[]{:S(2)}, u32[]{:S(2)}) collective-permute-start(f32[136,256]{1,0:T(8,128)S(1)} %get-tuple-element.46.bundle), channel_id=1, source_target_pairs={{0,4},{4,0},{8,12},{12,8},{16,20},{20,16},{24,28},{28,24},{1,5},{5... | collective-permute-start | bytes 417800 | tf_op jit(solution)/shard_map/ppermute | solution.py:886
  49.4 1.4 %collective-permute-start.2 = (f32[136,256]{1,0:T(8,128)S(1)}, f32[136,256]{1,0:T(8,128)S(1)}, u32[]{:S(2)}, u32[]{:S(2)}) collective-permute-start(f32[136,256]{1,0:T(8,128)S(1)} %shard_map.144.bundle), channel_id=1, source_target_pairs={{0,4},{4,0},{8,12},{12,8},{16,20},{20,16},{24,28},{28,24},{1,5},{5... | collective-permute-start | bytes 417800 | tf_op jit(solution)/shard_map/ppermute | solution.py:886

commit v11 on v10

--- a/solution.py
+++ b/solution.py
@@ -697,9 +697,9 @@
     low_row = iota((LANES, LANES), 0).astype(F32).astype(BF16)
     high_row = iota((HIGH, LANES), 0).astype(F32).astype(BF16)
     one, none = jnp.ones((), BF16), jnp.zeros((), BF16)
-    for begin in range(0, received.shape[0], 2):
+    for begin in range(0, received.shape[0], 4):
         lefts, rights = [], []
-        for device in (begin, begin + 1):
+        for device in range(begin, begin + 4):
             for index in range(rows):
                 unit = spread(received[device, PIECE + index])
                 high = jnp.floor(unit * (1.0 / LANES))
@@ -902,7 +902,7 @@
     received, design, weighted, units_seen = call(
         normals_kernel,
         [
-            leave(devices, PIECE + 2 * rows + 1, 1, LANES), stay(rows, WIDTH, slots),
+            stay(devices, PIECE + 2 * rows + 1, 1, LANES), stay(rows, WIDTH, slots),
             stay(rows, slots), stay(rows, slots, dtype=jnp.int32),
         ],
         weight_obs, present, attitude_partials, phase, knot_base, cal_id, first_q,
@@ -929,7 +929,7 @@
     )
     received, factor = lax.optimization_barrier((received, factor))
     (values,) = call(
-        first_kernel, [leave(devices, rows + half + 1, 1, LANES)],
+        first_kernel, [stay(devices, rows + half + 1, 1, LANES)],
         received, target, parts, partials, factor, weighted, hits,
     )
     values, received = lax.optimization_barrier((values, received))

time: 52.2 us -> 52.2 us (level)
  no operation moved by 1% of the time
where the time goes in v11:
time: 52.2 us; the launch traced here: 51.8 us
  waiting for transfers between devices  15.9 us (30%)
  Pallas kernels  15.4 us (30%)
  starting transfers between devices  10.2 us (20%)
  blocking collectives  9.62 us (18%)
  between operations  0.7 us (1%)
    pallas_call x8, Pallas kernels, call(): pl.pallas_call(kernel, out_shape=outs, in_specs=[VMEM] * len(near) + [ANY...  15.4 us
    all_to_all x2, waiting for transfers between devices, exchange(): return lax.all_to_all(value, ('src', 'tm'), 0, 0, tiled=True)  11.9 us
    all_to_all x2, starting transfers between devices, exchange(): return lax.all_to_all(value, ('src', 'tm'), 0, 0, tiled=True)  9.87 us
    all_to_all x1, blocking collectives, exchange(): return lax.all_to_all(value, ('src', 'tm'), 0, 0, tiled=True)  9.62 us
    ppermute x3, waiting for transfers between devices, swap(): lax.ppermute(value, 'src', [(at, at ^ 1) for at in range(lax.axis_size('s...  3.94 us
  transfers between devices with their start and end apart: 5, of which 5 were waited for; matrix products, arithmetic and copies ran while one was open for 0% of the time, Pallas kernels for 8%

profile of v11, /device:TPU:0, one launch (start us, length us, event | category | flops | bytes accessed | tf_op | source)
XLA Modules:
  0.0 51.8 jit_solution(11861223549153198147)
XLA Ops:
  0.6 2.4 %shard_map.138 = (f32[32,11,1,128]{3,2,1,0:T(1,128)}, f32[4,128,256]{2,1,0:T(8,128)S(1)}, f32[4,256]{1,0:T(4,128)S(1)}, s32[4,256]{1,0:T(4,128)S(1)}) custom-call(f32[4,256]{1,0:T(4,128)} %weight_in.1, s32[4,256]{1,0:T(4,128)} %present_in.1, f32[4,4,256]{2,1,0:T(4,128)} %attitude_in.1, f32[4,256]{1,0:T(4,128)} %phase_in.1, s32[4,256]{1,0:T(4,128)} %knot_in.1, ...), custom_call_target="tpu_custom_call" | custom-call | tf_op jit(solution)/shard_map/pallas_call | solution.py:867
  3.1 7.3 %all-to-all-start = ((f32[32,11,1,128]{3,2,1,0:T(1,128)}), f32[32,11,1,128]{3,2,1,0:T(1,128)S(1)}, u32[]{:S(2)}, u32[]{:S(2)}) async-start(f32[32,11,1,128]{3,2,1,0:T(1,128)} %get-tuple-element.32), calls=%async_computation | async-start | bytes 360448 | tf_op jit(solution)/shard_map/all_to_all | solution.py:890
  10.4 1.5 %shard_map.139 = (f32[4,8,256]{2,1,0:T(8,128)S(1)}, f32[16,128]{1,0:T(8,128)S(1)}, f32[4,256]{1,0:T(4,128)S(1)}, f32[128,256]{1,0:T(8,128)S(1)}, bf16[4,128,256]...) custom-call(s32[4,256]{1,0:T(4,128)S(1)} %get-tuple-element.33.cal_i, ...), custom_call_target="tpu_custom_call" | custom-call | tf_op jit(solution)/shard_map/pallas_call | solution.py:867
  11.9 7.5 %all-to-all-done.received = f32[32,11,1,128]{3,2,1,0:T(1,128)S(1)} async-done(((f32[32,11,1,128]{3,2,1,0:T(1,128)}), f32[32,11,1,128]{3,2,1,0:T(1,128)S(1)}, u32[]{:S(2)}, u32[]{:S(2)}) %all-to-all-start) | async-done | bytes 180256 | tf_op jit(solution)/shard_map/all_to_all | solution.py:890
  19.5 1.4 %shard_map.140 = f32[32,7,1,128]{3,2,1,0:T(1,128)} custom-call(f32[32,11,1,128]{3,2,1,0:T(1,128)S(1)} %all-to-all-done.received, f32[4,256]{1,0:T(4,128)S(1)} %get-tuple-element.38.target, bf16[4,256,256]{2,1,0:T(8,128)(2,1)S(1)} %get-tuple-element.39.parts, f32[4,8,256]{2,1,0:T(8,128)S(1)} %get-tuple-element.40.partials, ...), custom_call_target="tpu_custom_call" | custom-call | tf_op jit(solution)/shard_map/pallas_call | solution.py:867
  20.8 2.6 %all-to-all-start.1 = ((f32[32,7,1,128]{3,2,1,0:T(1,128)}), f32[32,7,1,128]{3,2,1,0:T(1,128)S(1)}, u32[]{:S(2)}, u32[]{:S(2)}) async-start(f32[32,7,1,128]{3,2,1,0:T(1,128)} %shard_map.140), calls=%async_computation.1 | async-start | bytes 229376 | tf_op jit(solution)/shard_map/all_to_all | solution.py:890
  23.4 2.4 %shard_map.141.weights = f32[128,256]{1,0:T(8,128)S(1)} custom-call(f32[32,11,1,128]{3,2,1,0:T(1,128)S(1)} %all-to-all-done.received), custom_call_target="tpu_custom_call" | custom-call | tf_op jit(solution)/shard_map/pallas_call | solution.py:867
  25.8 0.2 collective-permute-start
  26.0 1.2 %collective-permute-done.other_weights = f32[128,256]{1,0:T(8,128)S(1)} collective-permute-done((f32[128,256]{1,0:T(8,128)S(1)}, f32[128,256]{1,0:T(8,128)S(1)}, u32[]{:S(2)}, u32[]{:S(2)}) %collective-permute-start) | collective-permute-done | bytes 131104 | tf_op jit(solution)/shard_map/ppermute | solution.py:886
  27.2 4.4 %all-to-all-done.1.values = f32[32,7,1,128]{3,2,1,0:T(1,128)S(1)} async-done(((f32[32,7,1,128]{3,2,1,0:T(1,128)}), f32[32,7,1,128]{3,2,1,0:T(1,128)S(1)}, u32[]{:S(2)}, u32[]{:S(2)}) %all-to-all-start.1) | async-done | bytes 114720 | tf_op jit(solution)/shard_map/all_to_all | solution.py:890
  31.6 3.0 %shard_map.142 = (f32[136,256]{1,0:T(8,128)S(1)}, f32[2,128,128]{2,1,0:T(8,128)S(1)}) custom-call(f32[32,7,1,128]{3,2,1,0:T(1,128)S(1)} %all-to-all-done.1.values, f32[32,11,1,128]{3,2,1,0:T(1,128)S(1)} %all-to-all-done.received), custom_call_target="tpu_custom_call" | custom-call | tf_op jit(solution)/shard_map/pallas_call | solution.py:867
  34.6 0.1 collective-permute-start.1
  34.7 1.3 %collective-permute-done.1.other = f32[136,256]{1,0:T(8,128)S(1)} collective-permute-done((f32[136,256]{1,0:T(8,128)S(1)}, f32[136,256]{1,0:T(8,128)S(1)}, u32[]{:S(2)}, u32[]{:S(2)}) %collective-permute-start.1) | collective-permute-done | bytes 139296 | tf_op jit(solution)/shard_map/ppermute | solution.py:886
  36.1 1.3 %shard_map.143 = (f32[32,6,1,128]{3,2,1,0:T(1,128)S(1)}, f32[5,128]{1,0:T(8,128)}, f32[4,256]{1,0:T(4,128)S(1)}, f32[128,256]{1,0:T(8,128)S(1)}, f32[128,256]{1,0:T(8,128)S(1)}) custom-call(f32[136,256]{1,0:T(8,128)S(1)} %get-tuple-element.46.bundle, f32[136,256]{1,0:T(8,128)S(1)} %collective-permute-done.1.other, f32[128,256]{1,0:T(8,128)S(1)} %shard_map.141.weights, ...), custom_call_target="tpu_custom_call" | custom-call | tf_op jit(solution)/shard_map/pallas_call | solution.py:867
  37.4 9.6 %all_to_all.15.values = f32[32,6,1,128]{3,2,1,0:T(1,128)S(1)} all-to-all(f32[32,6,1,128]{3,2,1,0:T(1,128)S(1)} %get-tuple-element.52), channel_id=1, replica_groups=mesh['src'=8,'tm'=4] {'src','tm'}, dimensions={0} | all-to-all | bytes 196608 | tf_op jit(solution)/shard_map/all_to_all | solution.py:890
  47.0 2.4 %shard_map.144.bundle = f32[136,256]{1,0:T(8,128)S(1)} custom-call(f32[32,6,1,128]{3,2,1,0:T(1,128)S(1)} %all_to_all.15.values, f32[32,11,1,128]{3,2,1,0:T(1,128)S(1)} %all-to-all-done.received, f32[136,256]{1,0:T(8,128)S(1)} %get-tuple-element.46.bundle, f32[2,128,128]{2,1,0:T(8,128)S(1)} %get-tuple-element.53.lines), custom_call_target="tpu_custom_call" | custom-call | tf_op jit(solution)/shard_map/pallas_call | solution.py:867
  49.4 0.1 collective-permute-start.2
  49.4 1.3 %collective-permute-done.2.other = f32[136,256]{1,0:T(8,128)S(1)} collective-permute-done((f32[136,256]{1,0:T(8,128)S(1)}, f32[136,256]{1,0:T(8,128)S(1)}, u32[]{:S(2)}, u32[]{:S(2)}) %collective-permute-start.2) | collective-permute-done | bytes 139296 | tf_op jit(solution)/shard_map/ppermute | solution.py:886
  50.8 1.0 %shard_map.145 = (f32[256,128]{1,0:T(8,128)}, f32[1,128]{1,0:T(1,128)}, f32[4,256]{1,0:T(4,128)}) custom-call(f32[136,256]{1,0:T(8,128)S(1)} %shard_map.144.bundle, f32[136,256]{1,0:T(8,128)S(1)} %collective-permute-done.2.other, f32[128,256]{1,0:T(8,128)S(1)} %get-tuple-element.54.table, f32[128,256]{1,0:T(8,128)S(1)} %get-tuple-element.55.scale, ...), custom_call_target="tpu_custom_call" | custom-call | tf_op jit(solution)/shard_map/pallas_call | solution.py:867
Async XLA Ops:
  3.1 16.4 %all-to-all-start = ((f32[32,11,1,128]{3,2,1,0:T(1,128)}), f32[32,11,1,128]{3,2,1,0:T(1,128)S(1)}, u32[]{:S(2)}, u32[]{:S(2)}) async-start(f32[32,11,1,128]{3,2,1,0:T(1,128)} %get-tuple-element.32), calls=%async_computation | async-start | bytes 360448 | tf_op jit(solution)/shard_map/all_to_all | solution.py:890
  20.8 10.8 %all-to-all-start.1 = ((f32[32,7,1,128]{3,2,1,0:T(1,128)}), f32[32,7,1,128]{3,2,1,0:T(1,128)S(1)}, u32[]{:S(2)}, u32[]{:S(2)}) async-start(f32[32,7,1,128]{3,2,1,0:T(1,128)} %shard_map.140), calls=%async_computation.1 | async-start | bytes 229376 | tf_op jit(solution)/shard_map/all_to_all | solution.py:890
  25.8 1.4 %collective-permute-start = (f32[128,256]{1,0:T(8,128)S(1)}, f32[128,256]{1,0:T(8,128)S(1)}, u32[]{:S(2)}, u32[]{:S(2)}) collective-permute-start(f32[128,256]{1,0:T(8,128)S(1)} %shard_map.141.weights), channel_id=1, source_target_pairs={{0,4},{4,0},{8,12},{12,8},{16,20},{20,16},{24,28},{28,24},{1,5},{5... | collective-permute-start | bytes 393224 | tf_op jit(solution)/shard_map/ppermute | solution.py:886
  34.6 1.4 %collective-permute-start.1 = (f32[136,256]{1,0:T(8,128)S(1)}, f32[136,256]{1,0:T(8,128)S(1)}, u32[]{:S(2)}, u32[]{:S(2)}) collective-permute-start(f32[136,256]{1,0:T(8,128)S(1)} %get-tuple-element.46.bundle), channel_id=1, source_target_pairs={{0,4},{4,0},{8,12},{12,8},{16,20},{20,16},{24,28},{28,24},{1,5},{5... | collective-permute-start | bytes 417800 | tf_op jit(solution)/shard_map/ppermute | solution.py:886
  49.4 1.4 %collective-permute-start.2 = (f32[136,256]{1,0:T(8,128)S(1)}, f32[136,256]{1,0:T(8,128)S(1)}, u32[]{:S(2)}, u32[]{:S(2)}) collective-permute-start(f32[136,256]{1,0:T(8,128)S(1)} %shard_map.144.bundle), channel_id=1, source_target_pairs={{0,4},{4,0},{8,12},{12,8},{16,20},{20,16},{24,28},{28,24},{1,5},{5... | collective-permute-start | bytes 417800 | tf_op jit(solution)/shard_map/ppermute | solution.py:886

commit v12 on v10

--- a/solution.py
+++ b/solution.py
@@ -549,7 +549,7 @@
 
 def normals_kernel(
     weight_in, present_in, attitude_in, phase_in, knot_in, cal_in, start_in,
-    send_out, design_out, weighted_out, cal_id,
+    send_out, parts_out, weighted_out, cal_id,
     weight_obs, present, attitude_partials, phase, knot_base, start, stacked, sems,
 ):
     copies = begin(
@@ -590,16 +590,23 @@
             stacked[row, channel : channel + 1] = lines
             stacked[row, channel + 4 : channel + 5] = lines
         design = design_of(knot_base[at], [part[at] for part in basis], stacked[row])
-        design_out[row] = design
-        band = pack_band(exact_dot_t(design * weighted[at], design))
+        one, two, three = split3(design)
+        parts_out[row, :WIDTH] = one
+        parts_out[row, WIDTH:] = two
+        high, middle, low = split3(design * weighted[at])
+        most = dot_t(jnp.concatenate([high, middle], axis=0), jnp.concatenate([one, two], axis=0))
+        rest = dot_t(jnp.concatenate([high, low], axis=0), jnp.concatenate([three, one], axis=0))
+        small = most[WIDTH:, WIDTH:] + (rest[:WIDTH, :WIDTH] + rest[WIDTH:, WIDTH:])
+        small = small + (most[:WIDTH, WIDTH:] + most[WIDTH:, :WIDTH])
+        band = pack_band(most[:WIDTH, :WIDTH] + small)
         half, place = divmod(row, rows // PIECE)
         for index in range(BAND):
             send_out[place * BAND + index, half] = band[index : index + 1]
 
 
 def sources_kernel(
-    cal_id, weighted, design, observed_in, source_in, id_in, calibration_in,
-    partials_out, factor_out, target_out, table_out, hits_out, units_out, parts_out, observed,
+    cal_id, weighted, observed_in, source_in, id_in, calibration_in,
+    partials_out, factor_out, target_out, table_out, hits_out, units_out, observed,
     source_partials, source_id, table, sems,
 ):
     copies = begin(
@@ -624,9 +631,6 @@
         hits_out[row] = one_hot(source_id[at], SRC_DEV)
         found = dot_t(jnp.concatenate(split3(products), axis=0), hits_out[row])
         matrix = matrix + found[:40] + found[40:80] + found[80:]
-        first, second, unused = split3(design[row])
-        parts_out[row, :WIDTH] = first
-        parts_out[row, WIDTH:] = second
     ids = flat(cal_id[...])
     units_out[...] = one_hot(ids // LANES, HIGH)
     inverse = small_factor(matrix)
@@ -899,10 +903,11 @@
     half = rows // PIECE
     first_q = attitude.reshape(1, WIDTH)
     held = [weight_obs, present, attitude_partials, phase, knot_base, first_q]
-    received, design, weighted, units_seen = call(
+    received, parts, weighted, units_seen = call(
         normals_kernel,
         [
-            leave(devices, PIECE + 2 * rows + 1, 1, LANES), stay(rows, WIDTH, slots),
+            leave(devices, PIECE + 2 * rows + 1, 1, LANES),
+            stay(rows, 2 * WIDTH, slots, dtype=BF16),
             stay(rows, slots), stay(rows, slots, dtype=jnp.int32),
         ],
         weight_obs, present, attitude_partials, phase, knot_base, cal_id, first_q,
@@ -912,14 +917,14 @@
     )
     received = exchange(received)
     cal_id = units_seen
-    partials, factor, target, table, hits, units, parts, seen = call(
+    partials, factor, target, table, hits, units, seen = call(
         sources_kernel,
         [
             stay(rows, SUB, slots), stay(16, SRC_DEV), stay(rows, slots), stay(LANES, HIGH),
             stay(rows, SRC_DEV, slots, dtype=BF16), stay(HIGH, rows * slots, dtype=BF16),
-            stay(rows, 2 * WIDTH, slots, dtype=BF16), stay(rows, slots),
+            stay(rows, slots),
         ],
-        cal_id, weighted, design, observed, source_partials, source_id,
+        cal_id, weighted, observed, source_partials, source_id,
         calibration.reshape(HIGH, LANES),
         away=4,
         scratch=[

time: 52.2 us -> 52.1 us (level)
  transfers between devices with their start and end apart: 5 -> 5, of which waited for: 5 -> 5; matrix products, arithmetic and copies ran while one was open for 0% -> 0% of each run, Pallas kernels for 8% -> 7%
where the time goes in v12:
time: 52.1 us; the launch traced here: 51.6 us
  waiting for transfers between devices  15.9 us (31%)
  Pallas kernels  15.2 us (29%)
  starting transfers between devices  10.2 us (20%)
  blocking collectives  9.62 us (18%)
  between operations  0.7 us (1%)
    pallas_call x8, Pallas kernels, call(): pl.pallas_call(kernel, out_shape=outs, in_specs=[VMEM] * len(near) + [ANY...  15.2 us
    all_to_all x2, waiting for transfers between devices, exchange(): return lax.all_to_all(value, ('src', 'tm'), 0, 0, tiled=True)  12 us
    all_to_all x2, starting transfers between devices, exchange(): return lax.all_to_all(value, ('src', 'tm'), 0, 0, tiled=True)  9.88 us
    all_to_all x1, blocking collectives, exchange(): return lax.all_to_all(value, ('src', 'tm'), 0, 0, tiled=True)  9.62 us
    ppermute x3, waiting for transfers between devices, swap(): lax.ppermute(value, 'src', [(at, at ^ 1) for at in range(lax.axis_size('s...  3.92 us
  transfers between devices with their start and end apart: 5, of which 5 were waited for; matrix products, arithmetic and copies ran while one was open for 0% of the time, Pallas kernels for 7%

profile of v12, /device:TPU:0, one launch (start us, length us, event | category | flops | bytes accessed | tf_op | source)
XLA Modules:
  0.0 51.6 jit_solution(2591487560586557461)
XLA Ops:
  0.6 2.3 %shard_map.138 = (f32[32,11,1,128]{3,2,1,0:T(1,128)}, bf16[4,256,256]{2,1,0:T(8,128)(2,1)S(1)}, f32[4,256]{1,0:T(4,128)S(1)}, s32[4,256]{1,0:T(4,128)S(1)}) custom-call(f32[4,256]{1,0:T(4,128)} %weight_in.1, s32[4,256]{1,0:T(4,128)} %present_in.1, f32[4,4,256]{2,1,0:T(4,128)} %attitude_in.1, f32[4,256]{1,0:T(4,128)} %phase_in.1, s32[4,256]{1,0:T(4,128)} %knot_in.1, ...), custom_call_target="tpu_custom_call" | custom-call | tf_op jit(solution)/shard_map/pallas_call | solution.py:871
  2.9 7.3 %all-to-all-start = ((f32[32,11,1,128]{3,2,1,0:T(1,128)}), f32[32,11,1,128]{3,2,1,0:T(1,128)S(1)}, u32[]{:S(2)}, u32[]{:S(2)}) async-start(f32[32,11,1,128]{3,2,1,0:T(1,128)} %get-tuple-element.31), calls=%async_computation | async-start | bytes 360448 | tf_op jit(solution)/shard_map/all_to_all | solution.py:894
  10.2 1.5 %shard_map.139 = (f32[4,8,256]{2,1,0:T(8,128)S(1)}, f32[16,128]{1,0:T(8,128)S(1)}, f32[4,256]{1,0:T(4,128)S(1)}, f32[128,256]{1,0:T(8,128)S(1)}, bf16[4,128,256]...) custom-call(s32[4,256]{1,0:T(4,128)S(1)} %get-tuple-element.32.cal_id.ids, ...), custom_call_target="tpu_custom_call" | custom-call | tf_op jit(solution)/shard_map/pallas_call | solution.py:871
  11.7 7.6 %all-to-all-done.received = f32[32,11,1,128]{3,2,1,0:T(1,128)S(1)} async-done(((f32[32,11,1,128]{3,2,1,0:T(1,128)}), f32[32,11,1,128]{3,2,1,0:T(1,128)S(1)}, u32[]{:S(2)}, u32[]{:S(2)}) %all-to-all-start) | async-done | bytes 180256 | tf_op jit(solution)/shard_map/all_to_all | solution.py:894
  19.3 1.4 %shard_map.140 = f32[32,7,1,128]{3,2,1,0:T(1,128)} custom-call(f32[32,11,1,128]{3,2,1,0:T(1,128)S(1)} %all-to-all-done.received, f32[4,256]{1,0:T(4,128)S(1)} %get-tuple-element.36.target, bf16[4,256,256]{2,1,0:T(8,128)(2,1)S(1)} %get-tuple-element.37.parts, f32[4,8,256]{2,1,0:T(8,128)S(1)} %get-tuple-element.38.partials, ...), custom_call_target="tpu_custom_call" | custom-call | tf_op jit(solution)/shard_map/pallas_call | solution.py:871
  20.7 2.6 %all-to-all-start.1 = ((f32[32,7,1,128]{3,2,1,0:T(1,128)}), f32[32,7,1,128]{3,2,1,0:T(1,128)S(1)}, u32[]{:S(2)}, u32[]{:S(2)}) async-start(f32[32,7,1,128]{3,2,1,0:T(1,128)} %shard_map.140), calls=%async_computation.1 | async-start | bytes 229376 | tf_op jit(solution)/shard_map/all_to_all | solution.py:894
  23.3 2.4 %shard_map.141.weights = f32[128,256]{1,0:T(8,128)S(1)} custom-call(f32[32,11,1,128]{3,2,1,0:T(1,128)S(1)} %all-to-all-done.received), custom_call_target="tpu_custom_call" | custom-call | tf_op jit(solution)/shard_map/pallas_call | solution.py:871
  25.6 0.2 collective-permute-start
  25.8 1.2 %collective-permute-done.other_weights = f32[128,256]{1,0:T(8,128)S(1)} collective-permute-done((f32[128,256]{1,0:T(8,128)S(1)}, f32[128,256]{1,0:T(8,128)S(1)}, u32[]{:S(2)}, u32[]{:S(2)}) %collective-permute-start) | collective-permute-done | bytes 131104 | tf_op jit(solution)/shard_map/ppermute | solution.py:890
  27.0 4.4 %all-to-all-done.1.values = f32[32,7,1,128]{3,2,1,0:T(1,128)S(1)} async-done(((f32[32,7,1,128]{3,2,1,0:T(1,128)}), f32[32,7,1,128]{3,2,1,0:T(1,128)S(1)}, u32[]{:S(2)}, u32[]{:S(2)}) %all-to-all-start.1) | async-done | bytes 114720 | tf_op jit(solution)/shard_map/all_to_all | solution.py:894
  31.4 3.0 %shard_map.142 = (f32[136,256]{1,0:T(8,128)S(1)}, f32[2,128,128]{2,1,0:T(8,128)S(1)}) custom-call(f32[32,7,1,128]{3,2,1,0:T(1,128)S(1)} %all-to-all-done.1.values, f32[32,11,1,128]{3,2,1,0:T(1,128)S(1)} %all-to-all-done.received), custom_call_target="tpu_custom_call" | custom-call | tf_op jit(solution)/shard_map/pallas_call | solution.py:871
  34.5 0.1 collective-permute-start.1
  34.6 1.3 %collective-permute-done.1.other = f32[136,256]{1,0:T(8,128)S(1)} collective-permute-done((f32[136,256]{1,0:T(8,128)S(1)}, f32[136,256]{1,0:T(8,128)S(1)}, u32[]{:S(2)}, u32[]{:S(2)}) %collective-permute-start.1) | collective-permute-done | bytes 139296 | tf_op jit(solution)/shard_map/ppermute | solution.py:890
  35.9 1.3 %shard_map.143 = (f32[32,6,1,128]{3,2,1,0:T(1,128)S(1)}, f32[5,128]{1,0:T(8,128)}, f32[4,256]{1,0:T(4,128)S(1)}, f32[128,256]{1,0:T(8,128)S(1)}, f32[128,256]{1,0:T(8,128)S(1)}) custom-call(f32[136,256]{1,0:T(8,128)S(1)} %get-tuple-element.44.bundle, f32[136,256]{1,0:T(8,128)S(1)} %collective-permute-done.1.other, f32[128,256]{1,0:T(8,128)S(1)} %shard_map.141.weights, ...), custom_call_target="tpu_custom_call" | custom-call | tf_op jit(solution)/shard_map/pallas_call | solution.py:871
  37.2 9.6 %all_to_all.15.values = f32[32,6,1,128]{3,2,1,0:T(1,128)S(1)} all-to-all(f32[32,6,1,128]{3,2,1,0:T(1,128)S(1)} %get-tuple-element.50), channel_id=1, replica_groups=mesh['src'=8,'tm'=4] {'src','tm'}, dimensions={0} | all-to-all | bytes 196608 | tf_op jit(solution)/shard_map/all_to_all | solution.py:894
  46.8 2.4 %shard_map.144.bundle = f32[136,256]{1,0:T(8,128)S(1)} custom-call(f32[32,6,1,128]{3,2,1,0:T(1,128)S(1)} %all_to_all.15.values, f32[32,11,1,128]{3,2,1,0:T(1,128)S(1)} %all-to-all-done.received, f32[136,256]{1,0:T(8,128)S(1)} %get-tuple-element.44.bundle, f32[2,128,128]{2,1,0:T(8,128)S(1)} %get-tuple-element.51.lines), custom_call_target="tpu_custom_call" | custom-call | tf_op jit(solution)/shard_map/pallas_call | solution.py:871
  49.2 0.1 collective-permute-start.2
  49.3 1.3 %collective-permute-done.2.other = f32[136,256]{1,0:T(8,128)S(1)} collective-permute-done((f32[136,256]{1,0:T(8,128)S(1)}, f32[136,256]{1,0:T(8,128)S(1)}, u32[]{:S(2)}, u32[]{:S(2)}) %collective-permute-start.2) | collective-permute-done | bytes 139296 | tf_op jit(solution)/shard_map/ppermute | solution.py:890
  50.7 1.0 %shard_map.145 = (f32[256,128]{1,0:T(8,128)}, f32[1,128]{1,0:T(1,128)}, f32[4,256]{1,0:T(4,128)}) custom-call(f32[136,256]{1,0:T(8,128)S(1)} %shard_map.144.bundle, f32[136,256]{1,0:T(8,128)S(1)} %collective-permute-done.2.other, f32[128,256]{1,0:T(8,128)S(1)} %get-tuple-element.52.table, f32[128,256]{1,0:T(8,128)S(1)} %get-tuple-element.53.scale, ...), custom_call_target="tpu_custom_call" | custom-call | tf_op jit(solution)/shard_map/pallas_call | solution.py:871
Async XLA Ops:
  2.9 16.4 %all-to-all-start = ((f32[32,11,1,128]{3,2,1,0:T(1,128)}), f32[32,11,1,128]{3,2,1,0:T(1,128)S(1)}, u32[]{:S(2)}, u32[]{:S(2)}) async-start(f32[32,11,1,128]{3,2,1,0:T(1,128)} %get-tuple-element.31), calls=%async_computation | async-start | bytes 360448 | tf_op jit(solution)/shard_map/all_to_all | solution.py:894
  20.7 10.8 %all-to-all-start.1 = ((f32[32,7,1,128]{3,2,1,0:T(1,128)}), f32[32,7,1,128]{3,2,1,0:T(1,128)S(1)}, u32[]{:S(2)}, u32[]{:S(2)}) async-start(f32[32,7,1,128]{3,2,1,0:T(1,128)} %shard_map.140), calls=%async_computation.1 | async-start | bytes 229376 | tf_op jit(solution)/shard_map/all_to_all | solution.py:894
  25.6 1.4 %collective-permute-start = (f32[128,256]{1,0:T(8,128)S(1)}, f32[128,256]{1,0:T(8,128)S(1)}, u32[]{:S(2)}, u32[]{:S(2)}) collective-permute-start(f32[128,256]{1,0:T(8,128)S(1)} %shard_map.141.weights), channel_id=1, source_target_pairs={{0,4},{4,0},{8,12},{12,8},{16,20},{20,16},{24,28},{28,24},{1,5},{5... | collective-permute-start | bytes 393224 | tf_op jit(solution)/shard_map/ppermute | solution.py:890
  34.5 1.4 %collective-permute-start.1 = (f32[136,256]{1,0:T(8,128)S(1)}, f32[136,256]{1,0:T(8,128)S(1)}, u32[]{:S(2)}, u32[]{:S(2)}) collective-permute-start(f32[136,256]{1,0:T(8,128)S(1)} %get-tuple-element.44.bundle), channel_id=1, source_target_pairs={{0,4},{4,0},{8,12},{12,8},{16,20},{20,16},{24,28},{28,24},{1,5},{5... | collective-permute-start | bytes 417800 | tf_op jit(solution)/shard_map/ppermute | solution.py:890
  49.2 1.4 %collective-permute-start.2 = (f32[136,256]{1,0:T(8,128)S(1)}, f32[136,256]{1,0:T(8,128)S(1)}, u32[]{:S(2)}, u32[]{:S(2)}) collective-permute-start(f32[136,256]{1,0:T(8,128)S(1)} %shard_map.144.bundle), channel_id=1, source_target_pairs={{0,4},{4,0},{8,12},{12,8},{16,20},{20,16},{24,28},{28,24},{1,5},{5... | collective-permute-start | bytes 417800 | tf_op jit(solution)/shard_map/ppermute | solution.py:890

commit v13 on v12

--- a/solution.py
+++ b/solution.py
@@ -653,15 +653,15 @@
     sides = jnp.zeros((SUB, SRC_DEV), F32)
     for row in range(rows):
         products = partials[row] * (weighted[row : row + 1] * targets[row])
-        found = dot_t(jnp.concatenate(split3(products), axis=0), hits[row])
-        sides = sides + found[:SUB] + found[SUB : 2 * SUB] + found[2 * SUB :]
+        found = dot_t(jnp.concatenate(split3(products)[:2], axis=0), hits[row])
+        sides = sides + found[:SUB] + found[SUB:]
     params = small_apply(inverse, [sides[index : index + 1] for index in range(5)])
     table = jnp.concatenate(params + [jnp.zeros((3, SRC_DEV), F32)], axis=0)
-    split = jnp.concatenate(split3(table), axis=0)
+    split = jnp.concatenate(split3(table)[:2], axis=0)
     explained, scaled, rights = [], [], []
     for row in range(rows):
         found = dot(split, hits[row])
-        found = found[:SUB] + found[SUB : 2 * SUB] + found[2 * SUB :]
+        found = found[:SUB] + found[SUB:]
         explained.append(jnp.sum(found * partials[row], axis=0, keepdims=True))
     for row in range(rows):
         scaled.append(weighted[row : row + 1] * (targets[row] - explained[row]))

time: 52.1 us -> 51.9 us (level)
  no operation moved by 1% of the time
where the time goes in v13:
time: 51.9 us; the launch traced here: 51.4 us
  waiting for transfers between devices  15.9 us (31%)
  Pallas kernels  14.9 us (29%)
  starting transfers between devices  10.2 us (20%)
  blocking collectives  9.62 us (19%)
  between operations  0.7 us (1%)
    pallas_call x8, Pallas kernels, call(): pl.pallas_call(kernel, out_shape=outs, in_specs=[VMEM] * len(near) + [ANY...  14.9 us
    all_to_all x2, waiting for transfers between devices, exchange(): return lax.all_to_all(value, ('src', 'tm'), 0, 0, tiled=True)  12 us
    all_to_all x2, starting transfers between devices, exchange(): return lax.all_to_all(value, ('src', 'tm'), 0, 0, tiled=True)  9.88 us
    all_to_all x1, blocking collectives, exchange(): return lax.all_to_all(value, ('src', 'tm'), 0, 0, tiled=True)  9.62 us
    ppermute x3, waiting for transfers between devices, swap(): lax.ppermute(value, 'src', [(at, at ^ 1) for at in range(lax.axis_size('s...  3.94 us
  transfers between devices with their start and end apart: 5, of which 5 were waited for; matrix products, arithmetic and copies ran while one was open for 0% of the time, Pallas kernels for 7%

profile of v13, /device:TPU:0, one launch (start us, length us, event | category | flops | bytes accessed | tf_op | source)
XLA Modules:
  0.0 51.4 jit_solution(10378150356665663956)
XLA Ops:
  0.6 2.3 %shard_map.138 = (f32[32,11,1,128]{3,2,1,0:T(1,128)}, bf16[4,256,256]{2,1,0:T(8,128)(2,1)S(1)}, f32[4,256]{1,0:T(4,128)S(1)}, s32[4,256]{1,0:T(4,128)S(1)}) custom-call(f32[4,256]{1,0:T(4,128)} %weight_in.1, s32[4,256]{1,0:T(4,128)} %present_in.1, f32[4,4,256]{2,1,0:T(4,128)} %attitude_in.1, f32[4,256]{1,0:T(4,128)} %phase_in.1, s32[4,256]{1,0:T(4,128)} %knot_in.1, ...), custom_call_target="tpu_custom_call" | custom-call | tf_op jit(solution)/shard_map/pallas_call | solution.py:871
  2.9 7.3 %all-to-all-start = ((f32[32,11,1,128]{3,2,1,0:T(1,128)}), f32[32,11,1,128]{3,2,1,0:T(1,128)S(1)}, u32[]{:S(2)}, u32[]{:S(2)}) async-start(f32[32,11,1,128]{3,2,1,0:T(1,128)} %get-tuple-element.31), calls=%async_computation | async-start | bytes 360448 | tf_op jit(solution)/shard_map/all_to_all | solution.py:894
  10.2 1.5 %shard_map.139 = (f32[4,8,256]{2,1,0:T(8,128)S(1)}, f32[16,128]{1,0:T(8,128)S(1)}, f32[4,256]{1,0:T(4,128)S(1)}, f32[128,256]{1,0:T(8,128)S(1)}, bf16[4,128,256]...) custom-call(s32[4,256]{1,0:T(4,128)S(1)} %get-tuple-element.32.cal_id.ids, ...), custom_call_target="tpu_custom_call" | custom-call | tf_op jit(solution)/shard_map/pallas_call | solution.py:871
  11.7 7.6 %all-to-all-done.received = f32[32,11,1,128]{3,2,1,0:T(1,128)S(1)} async-done(((f32[32,11,1,128]{3,2,1,0:T(1,128)}), f32[32,11,1,128]{3,2,1,0:T(1,128)S(1)}, u32[]{:S(2)}, u32[]{:S(2)}) %all-to-all-start) | async-done | bytes 180256 | tf_op jit(solution)/shard_map/all_to_all | solution.py:894
  19.3 1.3 %shard_map.140 = f32[32,7,1,128]{3,2,1,0:T(1,128)} custom-call(f32[32,11,1,128]{3,2,1,0:T(1,128)S(1)} %all-to-all-done.received, f32[4,256]{1,0:T(4,128)S(1)} %get-tuple-element.36.target, bf16[4,256,256]{2,1,0:T(8,128)(2,1)S(1)} %get-tuple-element.37.parts, f32[4,8,256]{2,1,0:T(8,128)S(1)} %get-tuple-element.38.partials, ...), custom_call_target="tpu_custom_call" | custom-call | tf_op jit(solution)/shard_map/pallas_call | solution.py:871
  20.7 2.6 %all-to-all-start.1 = ((f32[32,7,1,128]{3,2,1,0:T(1,128)}), f32[32,7,1,128]{3,2,1,0:T(1,128)S(1)}, u32[]{:S(2)}, u32[]{:S(2)}) async-start(f32[32,7,1,128]{3,2,1,0:T(1,128)} %shard_map.140), calls=%async_computation.1 | async-start | bytes 229376 | tf_op jit(solution)/shard_map/all_to_all | solution.py:894
  23.2 2.4 %shard_map.141.weights = f32[128,256]{1,0:T(8,128)S(1)} custom-call(f32[32,11,1,128]{3,2,1,0:T(1,128)S(1)} %all-to-all-done.received), custom_call_target="tpu_custom_call" | custom-call | tf_op jit(solution)/shard_map/pallas_call | solution.py:871
  25.6 0.2 collective-permute-start
  25.8 1.2 %collective-permute-done.other_weights = f32[128,256]{1,0:T(8,128)S(1)} collective-permute-done((f32[128,256]{1,0:T(8,128)S(1)}, f32[128,256]{1,0:T(8,128)S(1)}, u32[]{:S(2)}, u32[]{:S(2)}) %collective-permute-start) | collective-permute-done | bytes 131104 | tf_op jit(solution)/shard_map/ppermute | solution.py:890
  27.0 4.4 %all-to-all-done.1.values = f32[32,7,1,128]{3,2,1,0:T(1,128)S(1)} async-done(((f32[32,7,1,128]{3,2,1,0:T(1,128)}), f32[32,7,1,128]{3,2,1,0:T(1,128)S(1)}, u32[]{:S(2)}, u32[]{:S(2)}) %all-to-all-start.1) | async-done | bytes 114720 | tf_op jit(solution)/shard_map/all_to_all | solution.py:894
  31.4 3.0 %shard_map.142 = (f32[136,256]{1,0:T(8,128)S(1)}, f32[2,128,128]{2,1,0:T(8,128)S(1)}) custom-call(f32[32,7,1,128]{3,2,1,0:T(1,128)S(1)} %all-to-all-done.1.values, f32[32,11,1,128]{3,2,1,0:T(1,128)S(1)} %all-to-all-done.received), custom_call_target="tpu_custom_call" | custom-call | tf_op jit(solution)/shard_map/pallas_call | solution.py:871
  34.5 0.1 collective-permute-start.1
  34.5 1.3 %collective-permute-done.1.other = f32[136,256]{1,0:T(8,128)S(1)} collective-permute-done((f32[136,256]{1,0:T(8,128)S(1)}, f32[136,256]{1,0:T(8,128)S(1)}, u32[]{:S(2)}, u32[]{:S(2)}) %collective-permute-start.1) | collective-permute-done | bytes 139296 | tf_op jit(solution)/shard_map/ppermute | solution.py:890
  35.9 1.1 %shard_map.143 = (f32[32,6,1,128]{3,2,1,0:T(1,128)S(1)}, f32[5,128]{1,0:T(8,128)}, f32[4,256]{1,0:T(4,128)S(1)}, f32[128,256]{1,0:T(8,128)S(1)}, f32[128,256]{1,0:T(8,128)S(1)}) custom-call(f32[136,256]{1,0:T(8,128)S(1)} %get-tuple-element.44.bundle, f32[136,256]{1,0:T(8,128)S(1)} %collective-permute-done.1.other, f32[128,256]{1,0:T(8,128)S(1)} %shard_map.141.weights, ...), custom_call_target="tpu_custom_call" | custom-call | tf_op jit(solution)/shard_map/pallas_call | solution.py:871
  37.0 9.6 %all_to_all.15.values = f32[32,6,1,128]{3,2,1,0:T(1,128)S(1)} all-to-all(f32[32,6,1,128]{3,2,1,0:T(1,128)S(1)} %get-tuple-element.50), channel_id=1, replica_groups=mesh['src'=8,'tm'=4] {'src','tm'}, dimensions={0} | all-to-all | bytes 196608 | tf_op jit(solution)/shard_map/all_to_all | solution.py:894
  46.6 2.4 %shard_map.144.bundle = f32[136,256]{1,0:T(8,128)S(1)} custom-call(f32[32,6,1,128]{3,2,1,0:T(1,128)S(1)} %all_to_all.15.values, f32[32,11,1,128]{3,2,1,0:T(1,128)S(1)} %all-to-all-done.received, f32[136,256]{1,0:T(8,128)S(1)} %get-tuple-element.44.bundle, f32[2,128,128]{2,1,0:T(8,128)S(1)} %get-tuple-element.51.lines), custom_call_target="tpu_custom_call" | custom-call | tf_op jit(solution)/shard_map/pallas_call | solution.py:871
  49.0 0.1 collective-permute-start.2
  49.1 1.3 %collective-permute-done.2.other = f32[136,256]{1,0:T(8,128)S(1)} collective-permute-done((f32[136,256]{1,0:T(8,128)S(1)}, f32[136,256]{1,0:T(8,128)S(1)}, u32[]{:S(2)}, u32[]{:S(2)}) %collective-permute-start.2) | collective-permute-done | bytes 139296 | tf_op jit(solution)/shard_map/ppermute | solution.py:890
  50.4 1.0 %shard_map.145 = (f32[256,128]{1,0:T(8,128)}, f32[1,128]{1,0:T(1,128)}, f32[4,256]{1,0:T(4,128)}) custom-call(f32[136,256]{1,0:T(8,128)S(1)} %shard_map.144.bundle, f32[136,256]{1,0:T(8,128)S(1)} %collective-permute-done.2.other, f32[128,256]{1,0:T(8,128)S(1)} %get-tuple-element.52.table, f32[128,256]{1,0:T(8,128)S(1)} %get-tuple-element.53.scale, ...), custom_call_target="tpu_custom_call" | custom-call | tf_op jit(solution)/shard_map/pallas_call | solution.py:871
Async XLA Ops:
  2.9 16.4 %all-to-all-start = ((f32[32,11,1,128]{3,2,1,0:T(1,128)}), f32[32,11,1,128]{3,2,1,0:T(1,128)S(1)}, u32[]{:S(2)}, u32[]{:S(2)}) async-start(f32[32,11,1,128]{3,2,1,0:T(1,128)} %get-tuple-element.31), calls=%async_computation | async-start | bytes 360448 | tf_op jit(solution)/shard_map/all_to_all | solution.py:894
  20.7 10.8 %all-to-all-start.1 = ((f32[32,7,1,128]{3,2,1,0:T(1,128)}), f32[32,7,1,128]{3,2,1,0:T(1,128)S(1)}, u32[]{:S(2)}, u32[]{:S(2)}) async-start(f32[32,7,1,128]{3,2,1,0:T(1,128)} %shard_map.140), calls=%async_computation.1 | async-start | bytes 229376 | tf_op jit(solution)/shard_map/all_to_all | solution.py:894
  25.6 1.4 %collective-permute-start = (f32[128,256]{1,0:T(8,128)S(1)}, f32[128,256]{1,0:T(8,128)S(1)}, u32[]{:S(2)}, u32[]{:S(2)}) collective-permute-start(f32[128,256]{1,0:T(8,128)S(1)} %shard_map.141.weights), channel_id=1, source_target_pairs={{0,4},{4,0},{8,12},{12,8},{16,20},{20,16},{24,28},{28,24},{1,5},{5... | collective-permute-start | bytes 393224 | tf_op jit(solution)/shard_map/ppermute | solution.py:890
  34.5 1.4 %collective-permute-start.1 = (f32[136,256]{1,0:T(8,128)S(1)}, f32[136,256]{1,0:T(8,128)S(1)}, u32[]{:S(2)}, u32[]{:S(2)}) collective-permute-start(f32[136,256]{1,0:T(8,128)S(1)} %get-tuple-element.44.bundle), channel_id=1, source_target_pairs={{0,4},{4,0},{8,12},{12,8},{16,20},{20,16},{24,28},{28,24},{1,5},{5... | collective-permute-start | bytes 417800 | tf_op jit(solution)/shard_map/ppermute | solution.py:890
  49.0 1.4 %collective-permute-start.2 = (f32[136,256]{1,0:T(8,128)S(1)}, f32[136,256]{1,0:T(8,128)S(1)}, u32[]{:S(2)}, u32[]{:S(2)}) collective-permute-start(f32[136,256]{1,0:T(8,128)S(1)} %shard_map.144.bundle), channel_id=1, source_target_pairs={{0,4},{4,0},{8,12},{12,8},{16,20},{20,16},{24,28},{28,24},{1,5},{5... | collective-permute-start | bytes 417800 | tf_op jit(solution)/shard_map/ppermute | solution.py:890
